TPU v7x, 256 devices: a whole 4x4x8 slice. The times are simulated.
256 devices in a mesh: replica: 4 (over x_lo, core), fsdp: 64 (over x_hi, y, z).
Axes of the slice: x: 4 (x_hi: 2, x_lo: 2; x = x_hi * 2 + x_lo), y: 4, z: 8, core: 2. Of those that a mesh axis runs over, the one named last changes fastest.
Arguments:
- hidden_in: bfloat16 [4, 16384, 8192], P('replica', 'fsdp'), may hold values from -27 to 27
- norm_gain: float32 [4, 8192], P('replica'), may hold values from 0.1 to 1.9
- key_weight: bfloat16 [4, 8192, 512], P('replica', 'fsdp'), may hold values from -1 to 1.5
- key_cotangent: bfloat16 [4, 16384, 512], P('replica', 'fsdp'), may hold values from -40 to 40
- outer_params: float32 [8, 8192, 512], P(None, 'fsdp'), may hold values from -6 to 6
- outer_momentum: float32 [8, 8192, 512], P(None, 'fsdp'), may hold values from -3 to 3
- inner_params: float32 [4, 8, 8192, 512], P('replica', None, 'fsdp'), may hold values from -6 to 6
- fragment_index: int32 [1], replicated, may hold values from 0 to 7
Outputs:
- key_out: bfloat16 [4, 16384, 512], P('replica', 'fsdp')
- grad_weight: float32 [4, 8192, 512], P('replica', 'fsdp')
- grad_hidden: bfloat16 [4, 16384, 8192], P('replica', 'fsdp')
- grad_gain: float32 [4, 8192], P('replica')
- new_params: float32 [8192, 512], P('fsdp')
- new_momentum: float32 [8192, 512], P('fsdp')
All inputs are finite; a program needn't handle non-finite values.
Results may differ from a plain program's by a relative error of at most 0.0049.
Values may be sent and summed in bfloat16 or wider, within the bound.
No kernel may reach another device: no remote copies, remote signals or barrier semaphores. Data moves between devices by JAX's collectives and lax.ppermute only.
A program may use at most 128 MiB of HBM per device.

v0:
```python
import functools

import jax
import jax.numpy as jnp
from jax import lax
from jax.experimental import pallas as pl
from jax.experimental.pallas import tpu as pltpu
from jax.sharding import Mesh
from jax.sharding import PartitionSpec as P

GROUP = ("xh", "y", "z")
REPL = ("xl", "core")
SIZE = {"xh": 2, "y": 4, "z": 8}
BF16 = jnp.bfloat16
F32 = jnp.float32
LANES = 128


def shift(value, axis, step):
    n = SIZE[axis]
    return lax.ppermute(value, axis, [(i, (i + step) % n) for i in range(n)])


def gather(own, axis):
    n = SIZE[axis]
    blocks = {0: own}
    right = left = own
    for hop in range(1, n // 2 + 1):
        right = shift(right, axis, 1)
        blocks[hop] = right
        if hop < n - hop:
            left = shift(left, axis, -1)
            blocks[n - hop] = left
    return [blocks[i] for i in range(n)]


def scatter_sum(part, axis, dim):
    n = SIZE[axis]

    def term(step):
        at = (lax.axis_index(axis) + step) & (n - 1)
        return lax.dynamic_slice_in_dim(part, at, 1, dim)

    left = shift(term(-(n // 2)).astype(BF16), axis, -1)
    right = None
    for hop in range(n // 2 - 1, 0, -1):
        ahead, behind = term(hop), term(-hop) + left.astype(F32)
        if right is not None:
            ahead = ahead + right.astype(F32)
        right = shift(ahead.astype(BF16), axis, 1)
        left = shift(behind.astype(BF16), axis, -1)
    return term(0) + right.astype(F32) + left.astype(F32)


def swap_sum(part, dim):
    me = lax.axis_index("xh")
    other = shift(lax.dynamic_slice_in_dim(part, 1 - me, 1, dim).astype(BF16), "xh", 1)
    return lax.dynamic_slice_in_dim(part, me, 1, dim) + other.astype(F32)


def weight_grad_kernel(hidden, gain, cotangent, a_out, b_out, inv_out, inverse, turned):
    step = pl.program_id(0)
    tokens, width = hidden.shape
    blocks, cut, _ = a_out.shape
    span = blocks * LANES

    @pl.when(step == 0)
    def _():
        def add(i, total):
            piece = hidden[:, pl.ds(pl.multiple_of(i * 512, 512), 512)].astype(F32)
            square = piece * piece
            for j in range(4):
                total = total + square[:, j * LANES : (j + 1) * LANES]
            return total

        total = lax.fori_loop(0, width // 512, add, jnp.zeros((tokens, LANES), F32))
        mean = jnp.sum(total, axis=-1, keepdims=True) / width
        inverse[...] = jnp.broadcast_to(lax.rsqrt(mean + 1e-05), (tokens, LANES))
        inv_out[...] = inverse[...]
        turned[...] = cotangent[...].T

    for j in range(0, blocks, 2):
        at = pl.ds(pl.multiple_of(step * span + j * LANES, 2 * LANES), 2 * LANES)
        scaled = (hidden[:, at].astype(F32) * inverse[:, :1] * gain[:, at]).astype(BF16)
        both = jnp.dot(turned[...], scaled, preferred_element_type=F32)
        for i in range(2):
            lanes = slice(i * LANES, (i + 1) * LANES)
            a_out[j + i] = both[:cut, lanes]
            b_out[j + i] = both[cut:, lanes]


def weight_grad(hidden, gain, cotangent):
    tokens, width = hidden.shape
    keys = cotangent.shape[1]
    blocks, per_step, cut = width // LANES, 8, keys // 2
    whole = lambda i: (0, 0)
    part = jax.ShapeDtypeStruct((blocks, cut, LANES), F32)
    return pl.pallas_call(
        weight_grad_kernel,
        grid=(blocks // per_step,),
        out_shape=(part, part, jax.ShapeDtypeStruct((tokens, LANES), F32)),
        in_specs=[
            pl.BlockSpec((tokens, width), whole),
            pl.BlockSpec((1, width), whole),
            pl.BlockSpec((tokens, keys), whole),
        ],
        out_specs=(
            pl.BlockSpec((per_step, cut, LANES), lambda i: (i, 0, 0)),
            pl.BlockSpec((per_step, cut, LANES), lambda i: (i, 0, 0)),
            pl.BlockSpec((tokens, LANES), whole),
        ),
        scratch_shapes=[pltpu.VMEM((tokens, LANES), F32), pltpu.VMEM((keys, tokens), BF16)],
        compiler_params=pltpu.CompilerParams(vmem_limit_bytes=32 * 1024 * 1024),
        cost_estimate=pl.CostEstimate(
            flops=2 * tokens * width * keys, bytes_accessed=22 * 1024 * 1024, transcendentals=0
        ),
        name="weight_grad",
    )(hidden, gain, cotangent)


def tail_kernel(na, nb, place, hidden, gain, cotangent, inverse, *refs):
    a_hbm, b_hbm = refs[:na], refs[na : na + nb]
    key_out, grad_hidden, a_all, b_all, grad, key_a, key_b, dots, sems = refs[na + nb :]
    tokens, width = hidden.shape
    cut = key_a.shape[1]
    x, y, z = place[0], place[1], place[2]
    copies = [pltpu.make_async_copy(ref, a_all.at[i], sems.at[i]) for i, ref in enumerate(a_hbm)]
    copies += [
        pltpu.make_async_copy(ref, b_all.at[i], sems.at[na + i]) for i, ref in enumerate(b_hbm)
    ]
    for copy in copies:
        copy.start()
    key_a[...] = jnp.zeros_like(key_a)
    key_b[...] = jnp.zeros_like(key_b)
    dots[...] = jnp.zeros_like(dots)

    def lanes_of(xr, yr, zr):
        block = (x ^ xr) * 32 + ((y - yr) & 3) * 8 + ((z - zr) & 7)
        return pl.ds(pl.multiple_of(block * LANES, LANES), LANES)

    def normed_at(at):
        return hidden[:, at].astype(F32) * inverse[...]

    for copy in copies[:na]:
        copy.wait()

    def a_step(zr, carry):
        rows = a_all[zr]
        grads = lax.dot_general(
            cotangent[:, :cut], rows, (((1,), (1,)), ((), ())), preferred_element_type=F32
        )
        scaled = []
        for i in range(8):
            at = lanes_of(i % 2, i // 2, zr)
            grad[:, at] = grads[:, i * LANES : (i + 1) * LANES]
            scaled.append((normed_at(at) * gain[:, at]).astype(BF16))
        key_a[...] += jnp.dot(
            jnp.concatenate(scaled, axis=1), rows, preferred_element_type=F32
        )
        return carry

    lax.fori_loop(0, na, a_step, 0)
    for copy in copies[na:]:
        copy.wait()

    def b_step(i, carry):
        yr, half = i // 2, i % 2
        rows = b_all[yr, pl.ds(pl.multiple_of(half * 1024, 1024), 1024), :]
        grads = lax.dot_general(
            cotangent[:, cut:], rows, (((1,), (1,)), ((), ())), preferred_element_type=F32
        )
        scaled = []
        total = dots[...]
        for j in range(8):
            at = lanes_of(j % 2, yr, half * 4 + j // 2)
            full = grad[:, at] + grads[:, j * LANES : (j + 1) * LANES]
            weighted = full * gain[:, at]
            normed = normed_at(at)
            grad[:, at] = weighted
            total = total + weighted * normed
            scaled.append((normed * gain[:, at]).astype(BF16))
        dots[...] = total
        key_b[...] += jnp.dot(
            jnp.concatenate(scaled, axis=1), rows, preferred_element_type=F32
        )
        return carry

    lax.fori_loop(0, 2 * nb, b_step, 0)
    key_out[:, :cut] = key_a[...].astype(BF16)
    key_out[:, cut:] = key_b[...].astype(BF16)
    mean = jnp.sum(dots[...], axis=-1, keepdims=True) / width

    def finish(i, carry):
        at = pl.ds(pl.multiple_of(i * 512, 512), 512)
        inv = inverse[:, :1]
        normed = hidden[:, at].astype(F32) * inv
        grad_hidden[:, at] = (inv * (grad[:, at] - normed * mean)).astype(BF16)
        return carry

    lax.fori_loop(0, width // 512, finish, 0)


def tail(place, hidden, gain, cotangent, inverse, a_blocks, b_blocks):
    tokens, width = hidden.shape
    keys = cotangent.shape[1]
    cut = keys // 2
    na, nb = len(a_blocks), len(b_blocks)
    vmem = pl.BlockSpec(memory_space=pltpu.VMEM)
    return pl.pallas_call(
        functools.partial(tail_kernel, na, nb),
        out_shape=(
            jax.ShapeDtypeStruct((tokens, keys), BF16),
            jax.ShapeDtypeStruct((tokens, width), BF16),
        ),
        in_specs=[pl.BlockSpec(memory_space=pltpu.SMEM)]
        + [vmem] * 4
        + [pl.BlockSpec(memory_space=pl.ANY)] * (na + nb),
        out_specs=(vmem, vmem),
        scratch_shapes=[
            pltpu.VMEM((na, width // na, cut), BF16),
            pltpu.VMEM((nb, width // nb, cut), BF16),
            pltpu.VMEM((tokens, width), F32),
            pltpu.VMEM((tokens, cut), F32),
            pltpu.VMEM((tokens, cut), F32),
            pltpu.VMEM((tokens, LANES), F32),
            pltpu.SemaphoreType.DMA((na + nb,)),
        ],
        compiler_params=pltpu.CompilerParams(vmem_limit_bytes=40 * 1024 * 1024),
        cost_estimate=pl.CostEstimate(
            flops=4 * tokens * width * keys, bytes_accessed=18 * 1024 * 1024, transcendentals=0
        ),
        name="tail",
    )(place, hidden, gain, cotangent, inverse, *a_blocks, *b_blocks)


def outer_step(current, moment, average):
    moment_new = 0.9 * moment + average
    return (current - 0.7 * (average + 0.9 * moment_new), moment_new)


def per_device(
    hidden_in,
    norm_gain,
    key_weight,
    key_cotangent,
    outer_params,
    outer_momentum,
    inner_params,
    fragment_index,
):
    hidden = hidden_in[0]
    cotangent = key_cotangent[0]
    own = key_weight[0]
    rows, width = own.shape
    cut = width // 2
    groups = SIZE["xh"], SIZE["y"], SIZE["z"]
    devices = groups[0] * groups[1] * groups[2]
    factor = float(hidden.shape[0] * devices) ** (-0.5)

    chosen = fragment_index[0]
    current = lax.dynamic_index_in_dim(outer_params, chosen, 0, keepdims=False)
    inner_now = lax.dynamic_index_in_dim(inner_params[0], chosen, 0, keepdims=False)
    summed = lax.psum(current - inner_now, REPL)

    other = shift(own, "xh", 1)
    part_a, part_b, inverse = weight_grad(hidden, norm_gain, cotangent)
    other, inverse = lax.optimization_barrier((other, inverse))

    def summed_columns(part, first, second):
        part = part.reshape(*groups, cut, rows)
        for axis in (first, second):
            part = scatter_sum(part, axis, 1 if axis == "y" else 2)
        return swap_sum(part, 0).reshape(cut, rows)

    grad_a = summed_columns(part_a, "z", "y")
    grad_b = summed_columns(part_b, "y", "z")
    grad_weight = jnp.concatenate([grad_a.T, grad_b.T], axis=-1) * factor

    pair = jnp.concatenate([own, other])
    a_blocks = gather(jnp.concatenate(gather(pair[:, :cut], "y")), "z")
    b_blocks = gather(jnp.concatenate(gather(pair[:, cut:], "z")), "y")

    me = lax.axis_index(GROUP)
    own_gain = lax.dynamic_slice_in_dim(norm_gain[0], me * rows, rows)
    own_sum = jnp.sum(own.astype(F32) * grad_weight, axis=-1) / own_gain
    grad_gain = lax.all_to_all(
        jnp.broadcast_to(own_sum[None], (devices, rows)), GROUP, 0, 0, tiled=True
    ).reshape(-1)

    place = jnp.stack([lax.axis_index(axis) for axis in GROUP])
    key_out, grad_hidden = tail(
        place, hidden, norm_gain, cotangent, inverse, a_blocks, b_blocks
    )

    summed, grad_gain = lax.optimization_barrier((summed, grad_gain))
    moment = lax.dynamic_index_in_dim(outer_momentum, chosen, 0, keepdims=False)
    new_params, new_momentum = outer_step(current, moment, summed / 4.0)
    return (
        key_out[None],
        grad_weight[None],
        grad_hidden[None],
        grad_gain[None],
        new_params,
        new_momentum,
    )


def solution(mesh):
    fine = Mesh(mesh.devices.reshape(2, 2, 2, 4, 8), (*REPL, *GROUP))
    placed = (
        P(REPL, GROUP, None),
        P(REPL, None),
        P(REPL, GROUP, None),
        P(REPL, GROUP, None),
        P(None, GROUP, None),
        P(None, GROUP, None),
        P(REPL, None, GROUP, None),
        P(),
    )
    return jax.shard_map(
        per_device,
        mesh=fine,
        in_specs=placed,
        out_specs=(
            P(REPL, GROUP, None),
            P(REPL, GROUP, None),
            P(REPL, GROUP, None),
            P(REPL, None),
            P(GROUP, None),
            P(GROUP, None),
        ),
        check_vma=False,
    )
```

profile of v0, /device:TPU:2, one launch (start us, length us, event | category | flops | bytes accessed | tf_op | source)
XLA Modules:
  0.0 257.7 jit_solution(5239538861272099182)
XLA Ops:
  11.1 5.9 %weight_grad.1 = (f32[64,256,128]{2,1,0:T(8,128)S(1)}, f32[64,256,128]{2,1,0:T(8,128)S(1)}, f32[256,128]{1,0:T(8,128)S(1)}) custom-call(bf16[256,8192]{1,0:T(8,128)(2,1)S(1)} %bitcast.45, f32[1,8192]{1,0:T(1,128)S(1)} %copy-done.2, bf16[256,512]{1,0:T(8,128)(2,1)S(1)} %bitcast.47), custom_call_target="tpu_custom_call" | custom-call | flops 2147483648 | bytes 23068672 | tf_op jit(solution)/shard_map/weight_grad/pallas_call | solution.py:98
  17.0 3.3 %copy-done = f32[64,256,128]{2,1,0:T(8,128)} copy-done((f32[64,256,128]{2,1,0:T(8,128)}, f32[64,256,128]{2,1,0:T(8,128)S(1)}, u32[]{:S(2)}) %copy-start) | copy-done | bytes 8388632
  20.3 3.3 %copy-done.1 = f32[64,256,128]{2,1,0:T(8,128)} copy-done((f32[64,256,128]{2,1,0:T(8,128)}, f32[64,256,128]{2,1,0:T(8,128)S(1)}, u32[]{:S(2)}) %copy-start.1) | copy-done | bytes 8388632
  23.7 9.0 %copy.15 = f32[64,256,128]{1,2,0:T(8,128)} copy(f32[64,256,128]{2,1,0:T(8,128)} %copy-done.1) | data formatting | bytes 16777216 | tf_op jit(solution)/shard_map/weight_grad/pallas_call | solution.py:98
  32.6 3.5 %dynamic-slice_convert_fusion.1 = (bf16[2,1,8,256,128]{3,4,2,1,0:T(8,128)(2,1)S(1)}, bf16[2,1,8,256,128]{3,4,2,1,0:T(8,128)(2,1)}) fusion(f32[2,4,8,256,128]{3,4,2,1,0:T(8,128)} %bitcast.55, s32[]{:T(128)S(6)} %select_n.74, s32[]{:T(128)S(6)} %select_n.76), kind=kLoop, calls=%fused_computation.3 | loop fusion | bytes 4194312 | tf_op jit(solution)/shard_map/convert_element_type | solution.py:50
  39.1 9.1 %copy.14 = f32[64,256,128]{1,2,0:T(8,128)} copy(f32[64,256,128]{2,1,0:T(8,128)} %copy-done) | data formatting | bytes 16777216 | tf_op jit(solution)/shard_map/weight_grad/pallas_call | solution.py:98
  54.8 4.3 %collective-permute-done = bf16[128,512]{1,0:T(8,128)(2,1)S(1)} collective-permute-done((bf16[128,512]{1,0:T(8,128)(2,1)S(1)}, bf16[128,512]{1,0:T(8,128)(2,1)S(1)}, u32[]{:S(2)}, u32[]{:S(2)}) %collective-permute-start) | collective-permute-done | bytes 131104 | tf_op jit(solution)/shard_map/ppermute | solution.py:21
  63.7 7.4 %collective-permute-done.11 = bf16[256,256]{1,0:T(8,128)(2,1)} collective-permute-done((bf16[256,256]{1,0:T(8,128)(2,1)}, bf16[256,256]{1,0:T(8,128)(2,1)}, u32[]{:S(2)}, u32[]{:S(2)}) %collective-permute-start.11) | collective-permute-done | bytes 131104 | tf_op jit(solution)/shard_map/ppermute | solution.py:21
  78.5 3.2 %collective-permute-start.16 = (bf16[256,256]{1,0:T(8,128)(2,1)}, bf16[256,256]{1,0:T(8,128)(2,1)S(1)}, u32[]{:S(2)}, u32[]{:S(2)}) collective-permute-start(bf16[256,256]{1,0:T(8,128)(2,1)} %copy-done.10), channel_id=1, source_target_pairs={{0,7},{1,0},{2,1},{3,2},{4,3},{5,4},{6,5},{7,6},{8,15},{9,8},{10,9... | collective-permute-start | bytes 393224 | tf_op jit(solution)/shard_map/ppermute | solution.py:21
  83.7 6.7 %collective-permute-done.16 = bf16[256,256]{1,0:T(8,128)(2,1)S(1)} collective-permute-done((bf16[256,256]{1,0:T(8,128)(2,1)}, bf16[256,256]{1,0:T(8,128)(2,1)S(1)}, u32[]{:S(2)}, u32[]{:S(2)}) %collective-permute-start.16) | collective-permute-done | bytes 131104 | tf_op jit(solution)/shard_map/ppermute | solution.py:21
  91.0 3.2 %collective-permute-done.13 = bf16[256,256]{1,0:T(8,128)(2,1)S(1)} collective-permute-done((bf16[256,256]{1,0:T(8,128)(2,1)}, bf16[256,256]{1,0:T(8,128)(2,1)S(1)}, u32[]{:S(2)}, u32[]{:S(2)}) %collective-permute-start.13) | collective-permute-done | bytes 131104 | tf_op jit(solution)/shard_map/ppermute | solution.py:21
  107.1 3.3 %collective-permute-start.8 = (bf16[1024,256]{1,0:T(8,128)(2,1)S(1)}, bf16[1024,256]{1,0:T(8,128)(2,1)}, u32[]{:S(2)}, u32[]{:S(2)}) collective-permute-start(bf16[1024,256]{1,0:T(8,128)(2,1)S(1)} %pad_maximum_fusion.refs_0_), channel_id=1, source_target_pairs={{0,7},{1,0},{2,1},{3,2},{4,3},{5,4},{6,5},{7,6},{8,15},{9,8},{10,9... | collective-permute-start | bytes 1572872 | tf_op jit(solution)/shard_map/ppermute | solution.py:21
  110.4 8.0 %collective-permute-done.25 = bf16[2,4,1,256,128]{3,4,2,1,0:T(8,128)(2,1)S(1)} collective-permute-done((bf16[2,4,1,256,128]{3,4,2,1,0:T(8,128)(2,1)S(1)}, bf16[2,4,1,256,128]{3,4,2,1,0:T(8,128)(2,1)S(1)}, u32[]{:S(2)}, u32[]{:S(2)}) %collective-permute-start.25) | collective-permute-done | bytes 524320 | tf_op jit(solution)/shard_map/ppermute | solution.py:21
  120.6 3.7 %collective-permute-start.26 = (bf16[2,4,1,256,128]{3,4,2,1,0:T(8,128)(2,1)}, bf16[2,4,1,256,128]{3,4,2,1,0:T(8,128)(2,1)}, u32[]{:S(2)}, u32[]{:S(2)}) collective-permute-start(bf16[2,4,1,256,128]{3,4,2,1,0:T(8,128)(2,1)} %add_convert_fusion.2), channel_id=1, source_target_pairs={{0,7},{1,0},{2,1},{3,2},{4,3},{5,4},{6,5},{7,6},{8,15},{9,8},{10,9... | collective-permute-start | bytes 1572872 | tf_op jit(solution)/shard_map/ppermute | solution.py:21
  129.6 3.8 %collective-permute-start.9 = (bf16[1024,256]{1,0:T(8,128)(2,1)}, bf16[1024,256]{1,0:T(8,128)(2,1)}, u32[]{:S(2)}, u32[]{:S(2)}) collective-permute-start(bf16[1024,256]{1,0:T(8,128)(2,1)} %collective-permute-done.8.refs_7_), channel_id=1, source_target_pairs={{0,7},{1,0},{2,1},{3,2},{4,3},{5,4},{6,5},{7,6},{8,15},{9,8},{10,9... | collective-permute-start | bytes 1572872 | tf_op jit(solution)/shard_map/ppermute | solution.py:21
  134.6 6.4 %collective-permute-done.26 = bf16[2,4,1,256,128]{3,4,2,1,0:T(8,128)(2,1)} collective-permute-done((bf16[2,4,1,256,128]{3,4,2,1,0:T(8,128)(2,1)}, bf16[2,4,1,256,128]{3,4,2,1,0:T(8,128)(2,1)}, u32[]{:S(2)}, u32[]{:S(2)}) %collective-permute-start.26) | collective-permute-done | bytes 524320 | tf_op jit(solution)/shard_map/ppermute | solution.py:21
  143.3 12.6 %collective-permute-start.23 = (bf16[2,4,1,256,128]{3,4,2,1,0:T(8,128)(2,1)}, bf16[2,4,1,256,128]{3,4,2,1,0:T(8,128)(2,1)}, u32[]{:S(2)}, u32[]{:S(2)}) collective-permute-start(bf16[2,4,1,256,128]{3,4,2,1,0:T(8,128)(2,1)} %get-tuple-element.28), channel_id=1, source_target_pairs={{0,1},{1,2},{2,3},{3,4},{4,5},{5,6},{6,7},{7,0},{8,9},{9,10},{10,1... | collective-permute-start | bytes 1572872 | tf_op jit(solution)/shard_map/ppermute | solution.py:21
  155.9 3.2 %collective-permute-start.6 = (bf16[1024,256]{1,0:T(8,128)(2,1)}, bf16[1024,256]{1,0:T(8,128)(2,1)}, u32[]{:S(2)}, u32[]{:S(2)}) collective-permute-start(bf16[1024,256]{1,0:T(8,128)(2,1)} %collective-permute-done.5.refs_2_), channel_id=1, source_target_pairs={{0,1},{1,2},{2,3},{3,4},{4,5},{5,6},{6,7},{7,0},{8,9},{9,10},{10,1... | collective-permute-start | bytes 1572872 | tf_op jit(solution)/shard_map/ppermute | solution.py:21
  163.6 12.2 %collective-permute-done.39 = bf16[2,1,1,256,128]{3,4,2,1,0:T(8,128)(2,1)} collective-permute-done((bf16[2,1,1,256,128]{3,4,2,1,0:T(8,128)(2,1)}, bf16[2,1,1,256,128]{3,4,2,1,0:T(8,128)(2,1)}, u32[]{:S(2)}, u32[]{:S(2)}) %collective-permute-start.39) | collective-permute-done | bytes 131104 | tf_op jit(solution)/shard_map/ppermute | solution.py:21
  182.6 6.8 %collective-permute-done.40 = bf16[2,1,1,256,128]{3,4,2,1,0:T(8,128)(2,1)S(1)} collective-permute-done((bf16[2,1,1,256,128]{3,4,2,1,0:T(8,128)(2,1)S(1)}, bf16[2,1,1,256,128]{3,4,2,1,0:T(8,128)(2,1)S(1)}, u32[]{:S(2)}, u32[]{:S(2)}) %collective-permute-start.40) | collective-permute-done | bytes 131104 | tf_op jit(solution)/shard_map/ppermute | solution.py:21
  198.7 3.3 %collective-permute-start.30 = (bf16[2,1,1,256,128]{3,4,2,1,0:T(8,128)(2,1)S(1)}, bf16[2,1,1,256,128]{3,4,2,1,0:T(8,128)(2,1)S(1)}, u32[]{:S(2)}, u32[]{:S(2)}) collective-permute-start(bf16[2,1,1,256,128]{3,4,2,1,0:T(8,128)(2,1)S(1)} %add_convert_fusion.11), channel_id=1, source_target_pairs={{0,24},{8,0},{16,8},{24,16},{1,25},{9,1},{17,9},{25,17},{2,26},{10... | collective-permute-start | bytes 393224 | tf_op jit(solution)/shard_map/ppermute | solution.py:21
  202.0 16.6 %tail.1 = (bf16[256,512]{1,0:T(8,128)(2,1)}, bf16[256,8192]{1,0:T(8,128)(2,1)}) custom-call(s32[3]{0:T(128)S(1)} %pad_add_fusion.place, bf16[256,8192]{1,0:T(8,128)(2,1)S(1)} %bitcast.46, f32[1,8192]{1,0:T(1,128)S(1)} %copy-done.3, bf16[256,512]{1,0:T(8,128)(2,1)S(1)} %bitcast.48, f32[256,128]{1,0:T(8,128)S(1)} %get-tuple-element.16.inverse, ...), custom_call_target="tpu_custom_call" | custom-call | flops 4294967296 | bytes 18874368 | tf_op jit(solution)/shard_map/tail/pallas_call | solution.py:209
  228.6 7.5 %all-to-all-start = ((f32[64,1,128]{2,1,0:T(1,128)}), f32[64,1,128]{2,1,0:T(1,128)S(1)}, u32[]{:S(2)}, u32[]{:S(2)}) async-start(f32[64,1,128]{2,1,0:T(1,128)} %broadcast_in_dim.18), calls=%async_computation | async-start | bytes 65536 | tf_op jit(solution)/shard_map/all_to_all | solution.py:286
  236.9 11.2 %all-to-all-done = f32[64,1,128]{2,1,0:T(1,128)S(1)} async-done(((f32[64,1,128]{2,1,0:T(1,128)}), f32[64,1,128]{2,1,0:T(1,128)S(1)}, u32[]{:S(2)}, u32[]{:S(2)}) %all-to-all-start) | async-done | bytes 32800 | tf_op jit(solution)/shard_map/all_to_all | solution.py:286
  (136 shorter events, 84.9 us)
Async XLA Ops:
  7.2 229.7 %all-reduce.2.cloned.1.call-start = ((), (), s32[]{:S(2)}) async-start(), calls=%async_computation.1 | async-start | bytes 524288 | tf_op jit(solution)/shard_map/psum | solution.py:263
  36.1 58.5 %collective-permute-start.33 = (bf16[2,1,8,256,128]{3,4,2,1,0:T(8,128)(2,1)}, bf16[2,1,8,256,128]{3,4,2,1,0:T(8,128)(2,1)}, u32[]{:S(2)}, u32[]{:S(2)}) collective-permute-start(bf16[2,1,8,256,128]{3,4,2,1,0:T(8,128)(2,1)} %get-tuple-element.33), channel_id=1, source_target_pairs={{0,24},{8,0},{16,8},{24,16},{1,25},{9,1},{17,9},{25,17},{2,26},{10... | collective-permute-start | bytes 3145736 | tf_op jit(solution)/shard_map/ppermute | solution.py:21
  50.7 21.2 %collective-permute-start.21 = (bf16[2,4,1,256,128]{3,4,2,1,0:T(8,128)(2,1)S(1)}, bf16[2,4,1,256,128]{3,4,2,1,0:T(8,128)(2,1)S(1)}, u32[]{:S(2)}, u32[]{:S(2)}) collective-permute-start(bf16[2,4,1,256,128]{3,4,2,1,0:T(8,128)(2,1)S(1)} %get-tuple-element.30), channel_id=1, source_target_pairs={{0,1},{1,2},{2,3},{3,4},{4,5},{5,6},{6,7},{7,0},{8,9},{9,10},{10,1... | collective-permute-start | bytes 1572872 | tf_op jit(solution)/shard_map/ppermute | solution.py:21
  74.6 23.8 %collective-permute-start.24 = (bf16[2,4,1,256,128]{3,4,2,1,0:T(8,128)(2,1)}, bf16[2,4,1,256,128]{3,4,2,1,0:T(8,128)(2,1)}, u32[]{:S(2)}, u32[]{:S(2)}) collective-permute-start(bf16[2,4,1,256,128]{3,4,2,1,0:T(8,128)(2,1)} %get-tuple-element.31), channel_id=1, source_target_pairs={{0,7},{1,0},{2,1},{3,2},{4,3},{5,4},{6,5},{7,6},{8,15},{9,8},{10,9... | collective-permute-start | bytes 1572872 | tf_op jit(solution)/shard_map/ppermute | solution.py:21
  78.5 22.0 %collective-permute-start.22 = (bf16[2,4,1,256,128]{3,4,2,1,0:T(8,128)(2,1)S(1)}, bf16[2,4,1,256,128]{3,4,2,1,0:T(8,128)(2,1)}, u32[]{:S(2)}, u32[]{:S(2)}) collective-permute-start(bf16[2,4,1,256,128]{3,4,2,1,0:T(8,128)(2,1)S(1)} %add_convert_fusion.5), channel_id=1, source_target_pairs={{0,1},{1,2},{2,3},{3,4},{4,5},{5,6},{6,7},{7,0},{8,9},{9,10},{10,1... | collective-permute-start | bytes 1572872 | tf_op jit(solution)/shard_map/ppermute | solution.py:21
  90.4 33.8 %collective-permute-start.32 = (bf16[2,1,8,256,128]{3,4,2,1,0:T(8,128)(2,1)S(1)}, bf16[2,1,8,256,128]{3,4,2,1,0:T(8,128)(2,1)S(1)}, u32[]{:S(2)}, u32[]{:S(2)}) collective-permute-start(bf16[2,1,8,256,128]{3,4,2,1,0:T(8,128)(2,1)S(1)} %get-tuple-element.32), channel_id=1, source_target_pairs={{0,8},{8,16},{16,24},{24,0},{1,9},{9,17},{17,25},{25,1},{2,10},{10... | collective-permute-start | bytes 3145736 | tf_op jit(solution)/shard_map/ppermute | solution.py:21
  98.4 25.8 %collective-permute-start.34 = (bf16[2,1,8,256,128]{3,4,2,1,0:T(8,128)(2,1)S(1)}, bf16[2,1,8,256,128]{3,4,2,1,0:T(8,128)(2,1)S(1)}, u32[]{:S(2)}, u32[]{:S(2)}) collective-permute-start(bf16[2,1,8,256,128]{3,4,2,1,0:T(8,128)(2,1)S(1)} %add_convert_fusion), channel_id=1, source_target_pairs={{0,24},{8,0},{16,8},{24,16},{1,25},{9,1},{17,9},{25,17},{2,26},{10... | collective-permute-start | bytes 3145736 | tf_op jit(solution)/shard_map/ppermute | solution.py:21
  106.9 20.4 %collective-permute-start.4 = (bf16[1024,256]{1,0:T(8,128)(2,1)S(1)}, bf16[1024,256]{1,0:T(8,128)(2,1)S(1)}, u32[]{:S(2)}, u32[]{:S(2)}) collective-permute-start(bf16[1024,256]{1,0:T(8,128)(2,1)S(1)} %pad_maximum_fusion.refs_0_), channel_id=1, source_target_pairs={{0,1},{1,2},{2,3},{3,4},{4,5},{5,6},{6,7},{7,0},{8,9},{9,10},{10,1... | collective-permute-start | bytes 1572872 | tf_op jit(solution)/shard_map/ppermute | solution.py:21
  107.1 22.5 %collective-permute-start.8 = (bf16[1024,256]{1,0:T(8,128)(2,1)S(1)}, bf16[1024,256]{1,0:T(8,128)(2,1)}, u32[]{:S(2)}, u32[]{:S(2)}) collective-permute-start(bf16[1024,256]{1,0:T(8,128)(2,1)S(1)} %pad_maximum_fusion.refs_0_), channel_id=1, source_target_pairs={{0,7},{1,0},{2,1},{3,2},{4,3},{5,4},{6,5},{7,6},{8,15},{9,8},{10,9... | collective-permute-start | bytes 1572872 | tf_op jit(solution)/shard_map/ppermute | solution.py:21
  120.6 20.4 %collective-permute-start.26 = (bf16[2,4,1,256,128]{3,4,2,1,0:T(8,128)(2,1)}, bf16[2,4,1,256,128]{3,4,2,1,0:T(8,128)(2,1)}, u32[]{:S(2)}, u32[]{:S(2)}) collective-permute-start(bf16[2,4,1,256,128]{3,4,2,1,0:T(8,128)(2,1)} %add_convert_fusion.2), channel_id=1, source_target_pairs={{0,7},{1,0},{2,1},{3,2},{4,3},{5,4},{6,5},{7,6},{8,15},{9,8},{10,9... | collective-permute-start | bytes 1572872 | tf_op jit(solution)/shard_map/ppermute | solution.py:21
  127.2 35.6 %collective-permute-start.18 = (bf16[2048,256]{1,0:T(8,128)(2,1)S(1)}, bf16[2048,256]{1,0:T(8,128)(2,1)S(1)}, u32[]{:S(2)}, u32[]{:S(2)}) collective-permute-start(bf16[2048,256]{1,0:T(8,128)(2,1)S(1)} %constant_dynamic-update-slice_fusion.refs_8_), channel_id=1, source_target_pairs={{0,8},{8,16},{16,24},{24,0},{1,9},{9,17},{17,25},{25,1},{2,10},{10... | collective-permute-start | bytes 3145736 | tf_op jit(solution)/shard_map/ppermute | solution.py:21
  129.6 31.3 %collective-permute-start.9 = (bf16[1024,256]{1,0:T(8,128)(2,1)}, bf16[1024,256]{1,0:T(8,128)(2,1)}, u32[]{:S(2)}, u32[]{:S(2)}) collective-permute-start(bf16[1024,256]{1,0:T(8,128)(2,1)} %collective-permute-done.8.refs_7_), channel_id=1, source_target_pairs={{0,7},{1,0},{2,1},{3,2},{4,3},{5,4},{6,5},{7,6},{8,15},{9,8},{10,9... | collective-permute-start | bytes 1572872 | tf_op jit(solution)/shard_map/ppermute | solution.py:21
  133.6 22.3 %collective-permute-start.38 = (bf16[2,1,1,256,128]{3,4,2,1,0:T(8,128)(2,1)}, bf16[2,1,1,256,128]{3,4,2,1,0:T(8,128)(2,1)S(1)}, u32[]{:S(2)}, u32[]{:S(2)}) collective-permute-start(bf16[2,1,1,256,128]{3,4,2,1,0:T(8,128)(2,1)} %get-tuple-element.37), channel_id=1, source_target_pairs={{0,7},{1,0},{2,1},{3,2},{4,3},{5,4},{6,5},{7,6},{8,15},{9,8},{10,9... | collective-permute-start | bytes 393224 | tf_op jit(solution)/shard_map/ppermute | solution.py:21
  143.3 33.9 %collective-permute-start.23 = (bf16[2,4,1,256,128]{3,4,2,1,0:T(8,128)(2,1)}, bf16[2,4,1,256,128]{3,4,2,1,0:T(8,128)(2,1)}, u32[]{:S(2)}, u32[]{:S(2)}) collective-permute-start(bf16[2,4,1,256,128]{3,4,2,1,0:T(8,128)(2,1)} %get-tuple-element.28), channel_id=1, source_target_pairs={{0,1},{1,2},{2,3},{3,4},{4,5},{5,6},{6,7},{7,0},{8,9},{9,10},{10,1... | collective-permute-start | bytes 1572872 | tf_op jit(solution)/shard_map/ppermute | solution.py:21
  155.9 21.7 %collective-permute-start.6 = (bf16[1024,256]{1,0:T(8,128)(2,1)}, bf16[1024,256]{1,0:T(8,128)(2,1)}, u32[]{:S(2)}, u32[]{:S(2)}) collective-permute-start(bf16[1024,256]{1,0:T(8,128)(2,1)} %collective-permute-done.5.refs_2_), channel_id=1, source_target_pairs={{0,1},{1,2},{2,3},{3,4},{4,5},{5,6},{6,7},{7,0},{8,9},{9,10},{10,1... | collective-permute-start | bytes 1572872 | tf_op jit(solution)/shard_map/ppermute | solution.py:21
  159.1 20.2 %collective-permute-start.27 = (bf16[2,4,1,256,128]{3,4,2,1,0:T(8,128)(2,1)}, bf16[2,4,1,256,128]{3,4,2,1,0:T(8,128)(2,1)}, u32[]{:S(2)}, u32[]{:S(2)}) collective-permute-start(bf16[2,4,1,256,128]{3,4,2,1,0:T(8,128)(2,1)} %add_convert_fusion.1), channel_id=1, source_target_pairs={{0,7},{1,0},{2,1},{3,2},{4,3},{5,4},{6,5},{7,6},{8,15},{9,8},{10,9... | collective-permute-start | bytes 1572872 | tf_op jit(solution)/shard_map/ppermute | solution.py:21
  162.8 32.7 %collective-permute-start.20 = (bf16[2048,256]{1,0:T(8,128)(2,1)S(1)}, bf16[2048,256]{1,0:T(8,128)(2,1)S(1)}, u32[]{:S(2)}, u32[]{:S(2)}) collective-permute-start(bf16[2048,256]{1,0:T(8,128)(2,1)S(1)} %constant_dynamic-update-slice_fusion.refs_8_), channel_id=1, source_target_pairs={{0,24},{8,0},{16,8},{24,16},{1,25},{9,1},{17,9},{25,17},{2,26},{10... | collective-permute-start | bytes 3145736 | tf_op jit(solution)/shard_map/ppermute | solution.py:21
  175.7 26.3 %collective-permute-start.19 = (bf16[2048,256]{1,0:T(8,128)(2,1)S(1)}, bf16[2048,256]{1,0:T(8,128)(2,1)S(1)}, u32[]{:S(2)}, u32[]{:S(2)}) collective-permute-start(bf16[2048,256]{1,0:T(8,128)(2,1)S(1)} %collective-permute-done.18.refs_9_), channel_id=1, source_target_pairs={{0,8},{8,16},{16,24},{24,0},{1,9},{9,17},{17,25},{25,1},{2,10},{10... | collective-permute-start | bytes 3145736 | tf_op jit(solution)/shard_map/ppermute | solution.py:21
  177.6 21.0 %collective-permute-start.7 = (bf16[1024,256]{1,0:T(8,128)(2,1)}, bf16[1024,256]{1,0:T(8,128)(2,1)S(1)}, u32[]{:S(2)}, u32[]{:S(2)}) collective-permute-start(bf16[1024,256]{1,0:T(8,128)(2,1)} %collective-permute-done.6.refs_3_), channel_id=1, source_target_pairs={{0,1},{1,2},{2,3},{3,4},{4,5},{5,6},{6,7},{7,0},{8,9},{9,10},{10,1... | collective-permute-start | bytes 1572872 | tf_op jit(solution)/shard_map/ppermute | solution.py:21
  194.9 23.8 %collective-permute-start.37 = (bf16[2,1,1,256,128]{3,4,2,1,0:T(8,128)(2,1)S(1)}, bf16[2,1,1,256,128]{3,4,2,1,0:T(8,128)(2,1)S(1)}, u32[]{:S(2)}, u32[]{:S(2)}) collective-permute-start(bf16[2,1,1,256,128]{3,4,2,1,0:T(8,128)(2,1)S(1)} %get-tuple-element.34), channel_id=1, source_target_pairs={{0,1},{1,2},{2,3},{3,4},{4,5},{5,6},{6,7},{7,0},{8,9},{9,10},{10,1... | collective-permute-start | bytes 393224 | tf_op jit(solution)/shard_map/ppermute | solution.py:21
  195.5 26.4 %collective-permute-start.28 = (bf16[2,1,1,256,128]{3,4,2,1,0:T(8,128)(2,1)S(1)}, bf16[2,1,1,256,128]{3,4,2,1,0:T(8,128)(2,1)S(1)}, u32[]{:S(2)}, u32[]{:S(2)}) collective-permute-start(bf16[2,1,1,256,128]{3,4,2,1,0:T(8,128)(2,1)S(1)} %get-tuple-element.38), channel_id=1, source_target_pairs={{0,8},{8,16},{16,24},{24,0},{1,9},{9,17},{17,25},{25,1},{2,10},{10... | collective-permute-start | bytes 393224 | tf_op jit(solution)/shard_map/ppermute | solution.py:21
  195.6 23.0 %collective-permute-start.41 = (bf16[2,1,1,256,128]{3,4,2,1,0:T(8,128)(2,1)S(1)}, bf16[2,1,1,256,128]{3,4,2,1,0:T(8,128)(2,1)S(1)}, u32[]{:S(2)}, u32[]{:S(2)}) collective-permute-start(bf16[2,1,1,256,128]{3,4,2,1,0:T(8,128)(2,1)S(1)} %add_convert_fusion.6), channel_id=1, source_target_pairs={{0,7},{1,0},{2,1},{3,2},{4,3},{5,4},{6,5},{7,6},{8,15},{9,8},{10,9... | collective-permute-start | bytes 393224 | tf_op jit(solution)/shard_map/ppermute | solution.py:21
  198.7 23.2 %collective-permute-start.30 = (bf16[2,1,1,256,128]{3,4,2,1,0:T(8,128)(2,1)S(1)}, bf16[2,1,1,256,128]{3,4,2,1,0:T(8,128)(2,1)S(1)}, u32[]{:S(2)}, u32[]{:S(2)}) collective-permute-start(bf16[2,1,1,256,128]{3,4,2,1,0:T(8,128)(2,1)S(1)} %add_convert_fusion.11), channel_id=1, source_target_pairs={{0,24},{8,0},{16,8},{24,16},{1,25},{9,1},{17,9},{25,17},{2,26},{10... | collective-permute-start | bytes 393224 | tf_op jit(solution)/shard_map/ppermute | solution.py:21
  228.6 19.4 %all-to-all-start = ((f32[64,1,128]{2,1,0:T(1,128)}), f32[64,1,128]{2,1,0:T(1,128)S(1)}, u32[]{:S(2)}, u32[]{:S(2)}) async-start(f32[64,1,128]{2,1,0:T(1,128)} %broadcast_in_dim.18), calls=%async_computation | async-start | bytes 65536 | tf_op jit(solution)/shard_map/all_to_all | solution.py:286
  (34 other events, 330.7 us)
Sparse Core Ops, SparseCore 0:
  162.8 37.5 all-reduce.1
where the time goes:
time: 262 us; the launch traced here: 258 us
  starting transfers between devices  79.6 us (30%)
  waiting for transfers between devices  73.6 us (28%)
  local copies, waits for them, and re-layouts  39.7 us (15%)
  other arithmetic  27 us (10%)
  Pallas kernels  22.5 us (9%)
  between operations  15.3 us (6%)
    ppermute x43, starting transfers between devices, shift(): return lax.ppermute(value, axis, [(i, (i + step) % n) for i in range(n)])  72 us
    ppermute x43, waiting for transfers between devices, shift(): return lax.ppermute(value, axis, [(i, (i + step) % n) for i in range(n)])  62.4 us
    pallas_call x2, local copies, waits for them, and re-layouts, weight_grad(): pl.pallas_call(weight_grad_kernel, grid=(blocks // per_step,), out_shape=...  18 us
    pallas_call x1, Pallas kernels, tail(): pl.pallas_call(functools.partial(tail_kernel, na, nb), out_shape=(jax.Sha...  16.6 us
    unnamed x33, local copies, waits for them, and re-layouts  14.1 us
    all_to_all x1, waiting for transfers between devices, per_device(): lax.all_to_all(jnp.broadcast_to(own_sum[None], (devices, rows)), GROUP, 0...  11.2 us
    convert_element_type x6, other arithmetic, scatter_sum(): left = shift(behind.astype(BF16), axis, -1)  8.77 us
    all_to_all x1, starting transfers between devices, per_device(): lax.all_to_all(jnp.broadcast_to(own_sum[None], (devices, rows)), GROUP, 0...  7.52 us
  transfers between devices with their start and end apart: 45, of which 14 were waited for; matrix products, arithmetic and copies ran while one was open for 16% of the time, Pallas kernels for 6%

commit v1 on v0

--- a/solution.py
+++ b/solution.py
@@ -14,6 +14,8 @@
 BF16 = jnp.bfloat16
 F32 = jnp.float32
 LANES = 128
+FIRST = (0, 1, 7, 2)
+SECOND = (6, 3, 5, 4)
 
 
 def shift(value, axis, step):
@@ -21,16 +23,14 @@
     return lax.ppermute(value, axis, [(i, (i + step) % n) for i in range(n)])
 
 
-def gather(own, axis):
+def gather(own, axis, last):
     n = SIZE[axis]
     blocks = {0: own}
     right = left = own
-    for hop in range(1, n // 2 + 1):
-        right = shift(right, axis, 1)
-        blocks[hop] = right
-        if hop < n - hop:
-            left = shift(left, axis, -1)
-            blocks[n - hop] = left
+    for hop in range(1, n // 2):
+        right, left = shift(right, axis, 1), shift(left, axis, -1)
+        blocks[hop], blocks[n - hop] = right, left
+    blocks[n // 2] = shift(right if last > 0 else left, axis, last)
     return [blocks[i] for i in range(n)]
 
 
@@ -52,10 +52,9 @@
     return term(0) + right.astype(F32) + left.astype(F32)
 
 
-def swap_sum(part, dim):
-    me = lax.axis_index("xh")
-    other = shift(lax.dynamic_slice_in_dim(part, 1 - me, 1, dim).astype(BF16), "xh", 1)
-    return lax.dynamic_slice_in_dim(part, me, 1, dim) + other.astype(F32)
+def exchange_sum(part, axes):
+    blocks = lax.all_to_all(part.astype(BF16), axes, 0, 0, tiled=True)
+    return jnp.sum(blocks.astype(F32), axis=0)
 
 
 def weight_grad_kernel(hidden, gain, cotangent, a_out, b_out, inv_out, inverse, turned):
@@ -118,76 +117,41 @@
     )(hidden, gain, cotangent)
 
 
-def tail_kernel(na, nb, place, hidden, gain, cotangent, inverse, *refs):
-    a_hbm, b_hbm = refs[:na], refs[na : na + nb]
-    key_out, grad_hidden, a_all, b_all, grad, key_a, key_b, dots, sems = refs[na + nb :]
-    tokens, width = hidden.shape
-    cut = key_a.shape[1]
+def tail_kernel(count, place, hidden, gain, cotangent, inverse, *refs):
+    weights = refs[:count]
+    key_out, grad_hidden, held, grad, keys, dots, sems = refs[count:]
+    tokens, width = hidden.shape
     x, y, z = place[0], place[1], place[2]
-    copies = [pltpu.make_async_copy(ref, a_all.at[i], sems.at[i]) for i, ref in enumerate(a_hbm)]
-    copies += [
-        pltpu.make_async_copy(ref, b_all.at[i], sems.at[na + i]) for i, ref in enumerate(b_hbm)
-    ]
-    for copy in copies:
-        copy.start()
-    key_a[...] = jnp.zeros_like(key_a)
-    key_b[...] = jnp.zeros_like(key_b)
+    for i, ref in enumerate(weights):
+        pltpu.make_async_copy(ref, held.at[i], sems.at[i]).start()
+    keys[...] = jnp.zeros_like(keys)
     dots[...] = jnp.zeros_like(dots)
 
-    def lanes_of(xr, yr, zr):
-        block = (x ^ xr) * 32 + ((y - yr) & 3) * 8 + ((z - zr) & 7)
-        return pl.ds(pl.multiple_of(block * LANES, LANES), LANES)
-
-    def normed_at(at):
-        return hidden[:, at].astype(F32) * inverse[...]
-
-    for copy in copies[:na]:
-        copy.wait()
-
-    def a_step(zr, carry):
-        rows = a_all[zr]
+    def block(i, carry):
+        pltpu.make_async_copy(held.at[i], held.at[i], sems.at[i]).wait()
+        rows = held[i]
         grads = lax.dot_general(
-            cotangent[:, :cut], rows, (((1,), (1,)), ((), ())), preferred_element_type=F32
-        )
-        scaled = []
-        for i in range(8):
-            at = lanes_of(i % 2, i // 2, zr)
-            grad[:, at] = grads[:, i * LANES : (i + 1) * LANES]
-            scaled.append((normed_at(at) * gain[:, at]).astype(BF16))
-        key_a[...] += jnp.dot(
-            jnp.concatenate(scaled, axis=1), rows, preferred_element_type=F32
-        )
-        return carry
-
-    lax.fori_loop(0, na, a_step, 0)
-    for copy in copies[na:]:
-        copy.wait()
-
-    def b_step(i, carry):
-        yr, half = i // 2, i % 2
-        rows = b_all[yr, pl.ds(pl.multiple_of(half * 1024, 1024), 1024), :]
-        grads = lax.dot_general(
-            cotangent[:, cut:], rows, (((1,), (1,)), ((), ())), preferred_element_type=F32
+            cotangent[...], rows, (((1,), (1,)), ((), ())), preferred_element_type=F32
         )
         scaled = []
         total = dots[...]
         for j in range(8):
-            at = lanes_of(j % 2, yr, half * 4 + j // 2)
-            full = grad[:, at] + grads[:, j * LANES : (j + 1) * LANES]
-            weighted = full * gain[:, at]
-            normed = normed_at(at)
+            zr = jnp.where(i % 2 == 0, FIRST[j // 2], SECOND[j // 2])
+            feature = (x ^ (j % 2)) * 32 + ((y - i // 2) & 3) * 8 + ((z - zr) & 7)
+            at = pl.ds(pl.multiple_of(feature * LANES, LANES), LANES)
+            normed = hidden[:, at].astype(F32) * inverse[...]
+            weighted = grads[:, j * LANES : (j + 1) * LANES] * gain[:, at]
             grad[:, at] = weighted
             total = total + weighted * normed
             scaled.append((normed * gain[:, at]).astype(BF16))
         dots[...] = total
-        key_b[...] += jnp.dot(
+        keys[...] += jnp.dot(
             jnp.concatenate(scaled, axis=1), rows, preferred_element_type=F32
         )
         return carry
 
-    lax.fori_loop(0, 2 * nb, b_step, 0)
-    key_out[:, :cut] = key_a[...].astype(BF16)
-    key_out[:, cut:] = key_b[...].astype(BF16)
+    lax.fori_loop(0, count, block, 0)
+    key_out[...] = keys[...].astype(BF16)
     mean = jnp.sum(dots[...], axis=-1, keepdims=True) / width
 
     def finish(i, carry):
@@ -200,37 +164,34 @@
     lax.fori_loop(0, width // 512, finish, 0)
 
 
-def tail(place, hidden, gain, cotangent, inverse, a_blocks, b_blocks):
+def tail(place, hidden, gain, cotangent, inverse, weights):
     tokens, width = hidden.shape
     keys = cotangent.shape[1]
-    cut = keys // 2
-    na, nb = len(a_blocks), len(b_blocks)
+    count = len(weights)
     vmem = pl.BlockSpec(memory_space=pltpu.VMEM)
     return pl.pallas_call(
-        functools.partial(tail_kernel, na, nb),
+        functools.partial(tail_kernel, count),
         out_shape=(
             jax.ShapeDtypeStruct((tokens, keys), BF16),
             jax.ShapeDtypeStruct((tokens, width), BF16),
         ),
         in_specs=[pl.BlockSpec(memory_space=pltpu.SMEM)]
         + [vmem] * 4
-        + [pl.BlockSpec(memory_space=pl.ANY)] * (na + nb),
+        + [pl.BlockSpec(memory_space=pl.ANY)] * count,
         out_specs=(vmem, vmem),
         scratch_shapes=[
-            pltpu.VMEM((na, width // na, cut), BF16),
-            pltpu.VMEM((nb, width // nb, cut), BF16),
+            pltpu.VMEM((count, width // count, keys), BF16),
             pltpu.VMEM((tokens, width), F32),
-            pltpu.VMEM((tokens, cut), F32),
-            pltpu.VMEM((tokens, cut), F32),
+            pltpu.VMEM((tokens, keys), F32),
             pltpu.VMEM((tokens, LANES), F32),
-            pltpu.SemaphoreType.DMA((na + nb,)),
+            pltpu.SemaphoreType.DMA((count,)),
         ],
         compiler_params=pltpu.CompilerParams(vmem_limit_bytes=40 * 1024 * 1024),
         cost_estimate=pl.CostEstimate(
             flops=4 * tokens * width * keys, bytes_accessed=18 * 1024 * 1024, transcendentals=0
         ),
         name="tail",
-    )(place, hidden, gain, cotangent, inverse, *a_blocks, *b_blocks)
+    )(place, hidden, gain, cotangent, inverse, *weights)
 
 
 def outer_step(current, moment, average):
@@ -260,25 +221,23 @@
     chosen = fragment_index[0]
     current = lax.dynamic_index_in_dim(outer_params, chosen, 0, keepdims=False)
     inner_now = lax.dynamic_index_in_dim(inner_params[0], chosen, 0, keepdims=False)
-    summed = lax.psum(current - inner_now, REPL)
-
-    other = shift(own, "xh", 1)
+    summed = current - inner_now
+    for axis in REPL:
+        summed = summed + lax.ppermute(summed, axis, [(0, 1), (1, 0)])
+
+    pair = jnp.concatenate([own, shift(own, "xh", 1)])
+    along_z = gather(pair, "z", 1)
+    first = gather(jnp.concatenate([along_z[i] for i in FIRST]), "y", 1)
+    second = gather(jnp.concatenate([along_z[i] for i in SECOND]), "y", -1)
+    weights = [block for both in zip(first, second) for block in both]
+
     part_a, part_b, inverse = weight_grad(hidden, norm_gain, cotangent)
-    other, inverse = lax.optimization_barrier((other, inverse))
-
-    def summed_columns(part, first, second):
-        part = part.reshape(*groups, cut, rows)
-        for axis in (first, second):
-            part = scatter_sum(part, axis, 1 if axis == "y" else 2)
-        return swap_sum(part, 0).reshape(cut, rows)
-
-    grad_a = summed_columns(part_a, "z", "y")
-    grad_b = summed_columns(part_b, "y", "z")
-    grad_weight = jnp.concatenate([grad_a.T, grad_b.T], axis=-1) * factor
-
-    pair = jnp.concatenate([own, other])
-    a_blocks = gather(jnp.concatenate(gather(pair[:, :cut], "y")), "z")
-    b_blocks = gather(jnp.concatenate(gather(pair[:, cut:], "z")), "y")
+    part_a = part_a.reshape(*groups, cut, rows)
+    part_b = part_b.reshape(*groups, cut, rows)
+    sum_a = exchange_sum(scatter_sum(part_a, "z", 2).reshape(-1, cut, rows), ("xh", "y"))
+    sum_b = exchange_sum(scatter_sum(part_b, "y", 1).reshape(-1, cut, rows), ("xh", "z"))
+    sum_a, sum_b = lax.optimization_barrier((sum_a, sum_b))
+    grad_weight = jnp.concatenate([sum_a.T, sum_b.T], axis=-1) * factor
 
     me = lax.axis_index(GROUP)
     own_gain = lax.dynamic_slice_in_dim(norm_gain[0], me * rows, rows)
@@ -288,11 +247,8 @@
     ).reshape(-1)
 
     place = jnp.stack([lax.axis_index(axis) for axis in GROUP])
-    key_out, grad_hidden = tail(
-        place, hidden, norm_gain, cotangent, inverse, a_blocks, b_blocks
-    )
-
-    summed, grad_gain = lax.optimization_barrier((summed, grad_gain))
+    key_out, grad_hidden = tail(place, hidden, norm_gain, cotangent, inverse, weights)
+
     moment = lax.dynamic_index_in_dim(outer_momentum, chosen, 0, keepdims=False)
     new_params, new_momentum = outer_step(current, moment, summed / 4.0)
     return (

time: 262 us -> 235 us (0.90); the launches traced: 258 us -> 234 us
  waiting for transfers between devices: 73.6 us -> 106 us
  starting transfers between devices: 79.6 us -> 60.4 us
  local copies, waits for them, and re-layouts: 39.7 us -> 20.7 us
  between operations: 15.3 us -> 1.6 us
  Pallas kernels: 22.5 us -> 19.7 us
    ppermute x43 -> x24, starting transfers between devices: 72 us -> 37.8 us  [shift(): return lax.ppermute(value, axis, [(i, (i + step) % n) for i in range(n)])]
    pallas_call x2 -> x0, local copies, waits for them, and re-layouts: 18 us -> none  [weight_grad(): pl.pallas_call(weight_grad_kernel, grid=(blocks // per_step,), out_shape=...]
    all_to_all x0 -> x2, waiting for transfers between devices: none -> 15.1 us  [exchange_sum(): blocks = lax.all_to_all(part.astype(BF16), axes, 0, 0, tiled=True)]
    all_to_all x0 -> x2, starting transfers between devices: none -> 10.8 us  [exchange_sum(): blocks = lax.all_to_all(part.astype(BF16), axes, 0, 0, tiled=True)]
    ppermute x0 -> x2, waiting for transfers between devices: none -> 8.84 us  [per_device(): summed = summed + lax.ppermute(summed, axis, [(0, 1), (1, 0)])]
    ppermute x43 -> x24, waiting for transfers between devices: 62.4 us -> 71.2 us  [shift(): return lax.ppermute(value, axis, [(i, (i + step) % n) for i in range(n)])]
    convert_element_type x0 -> x2, other arithmetic: none -> 5.84 us  [exchange_sum(): blocks = lax.all_to_all(part.astype(BF16), axes, 0, 0, tiled=True)]
    add x4 -> x1, other arithmetic: 4.84 us -> 0.74 us  [per_device(): summed = summed + lax.ppermute(summed, axis, [(0, 1), (1, 0)])]
  transfers between devices with their start and end apart: 45 -> 29, of which waited for: 14 -> 15; matrix products, arithmetic and copies ran while one was open for 16% -> 12% of each run, Pallas kernels for 6% -> 6%
where the time goes in v1:
time: 235 us; the launch traced here: 234 us
  waiting for transfers between devices  106 us (45%)
  starting transfers between devices  60.4 us (26%)
  other arithmetic  25.3 us (11%)
  local copies, waits for them, and re-layouts  20.7 us (9%)
  Pallas kernels  19.7 us (8%)
    ppermute x24, waiting for transfers between devices, shift(): return lax.ppermute(value, axis, [(i, (i + step) % n) for i in range(n)])  71.2 us
    ppermute x24, starting transfers between devices, shift(): return lax.ppermute(value, axis, [(i, (i + step) % n) for i in range(n)])  37.8 us
    unnamed x30, local copies, waits for them, and re-layouts  15.2 us
    all_to_all x2, waiting for transfers between devices, exchange_sum(): blocks = lax.all_to_all(part.astype(BF16), axes, 0, 0, tiled=True)  15.1 us
    pallas_call x1, Pallas kernels, tail(): pl.pallas_call(functools.partial(tail_kernel, count), out_shape=(jax.Shap...  13.8 us
    all_to_all x1, waiting for transfers between devices, per_device(): lax.all_to_all(jnp.broadcast_to(own_sum[None], (devices, rows)), GROUP, 0...  11.2 us
    all_to_all x2, starting transfers between devices, exchange_sum(): blocks = lax.all_to_all(part.astype(BF16), axes, 0, 0, tiled=True)  10.8 us
    all_to_all x1, starting transfers between devices, per_device(): lax.all_to_all(jnp.broadcast_to(own_sum[None], (devices, rows)), GROUP, 0...  10.2 us
  transfers between devices with their start and end apart: 29, of which 15 were waited for; matrix products, arithmetic and copies ran while one was open for 12% of the time, Pallas kernels for 6%

profile of v1, /device:TPU:2, one launch (start us, length us, event | category | flops | bytes accessed | tf_op | source)
XLA Modules:
  0.0 234.0 jit_solution(17177032995622249659)
XLA Ops:
  4.5 5.9 %weight_grad.1 = (f32[64,256,128]{2,1,0:T(8,128)S(1)}, f32[64,256,128]{2,1,0:T(8,128)S(1)}, f32[256,128]{1,0:T(8,128)S(1)}) custom-call(bf16[256,8192]{1,0:T(8,128)(2,1)S(1)} %bitcast.48, f32[1,8192]{1,0:T(1,128)S(1)} %copy-done.2, bf16[256,512]{1,0:T(8,128)(2,1)S(1)} %bitcast.50), custom_call_target="tpu_custom_call" | custom-call | flops 2147483648 | bytes 23068672 | tf_op jit(solution)/shard_map/weight_grad/pallas_call | solution.py:97
  10.5 3.3 %copy-done.1 = f32[64,256,128]{2,1,0:T(8,128)} copy-done((f32[64,256,128]{2,1,0:T(8,128)}, f32[64,256,128]{2,1,0:T(8,128)S(1)}, u32[]{:S(2)}) %copy-start.1) | copy-done | bytes 8388632
  13.7 3.2 %copy-done = f32[64,256,128]{2,1,0:T(8,128)} copy-done((f32[64,256,128]{2,1,0:T(8,128)}, f32[64,256,128]{2,1,0:T(8,128)S(1)}, u32[]{:S(2)}) %copy-start) | copy-done | bytes 8388632
  19.2 4.0 %collective-permute-start.17 = (bf16[2,4,1,256,128]{4,3,2,1,0:T(8,128)(2,1)S(1)}, bf16[2,4,1,256,128]{4,3,2,1,0:T(8,128)(2,1)S(1)}, u32[]{:S(2)}, u32[]{:S(2)}) collective-permute-start(bf16[2,4,1,256,128]{4,3,2,1,0:T(8,128)(2,1)S(1)} %get-tuple-element.27), channel_id=1, source_target_pairs={{0,7},{1,0},{2,1},{3,2},{4,3},{5,4},{6,5},{7,6},{8,15},{9,8},{10,9... | collective-permute-start | bytes 1572872 | tf_op jit(solution)/shard_map/ppermute | solution.py:23
  23.2 11.8 %collective-permute-done.14 = bf16[2,4,1,256,128]{4,3,2,1,0:T(8,128)(2,1)S(1)} collective-permute-done((bf16[2,4,1,256,128]{4,3,2,1,0:T(8,128)(2,1)S(1)}, bf16[2,4,1,256,128]{4,3,2,1,0:T(8,128)(2,1)S(1)}, u32[]{:S(2)}, u32[]{:S(2)}) %collective-permute-start.14) | collective-permute-done | bytes 524320 | tf_op jit(solution)/shard_map/ppermute | solution.py:23
  38.7 12.1 %collective-permute-done.15 = bf16[2,4,1,256,128]{4,3,2,1,0:T(8,128)(2,1)S(1)} collective-permute-done((bf16[2,4,1,256,128]{4,3,2,1,0:T(8,128)(2,1)S(1)}, bf16[2,4,1,256,128]{4,3,2,1,0:T(8,128)(2,1)S(1)}, u32[]{:S(2)}, u32[]{:S(2)}) %collective-permute-start.15) | collective-permute-done | bytes 524320 | tf_op jit(solution)/shard_map/ppermute | solution.py:23
  53.8 3.5 %dynamic-slice_convert_fusion.1 = (bf16[2,1,8,256,128]{4,3,2,1,0:T(8,128)(2,1)}, bf16[2,1,8,256,128]{4,3,2,1,0:T(8,128)(2,1)S(1)}) fusion(f32[2,4,8,256,128]{4,3,2,1,0:T(8,128)} %bitcast.45, s32[]{:T(128)S(6)} %select_n.54, s32[]{:T(128)S(6)} %select_n.56), kind=kLoop, calls=%fused_computation.4 | loop fusion | bytes 4194312 | tf_op jit(solution)/shard_map/convert_element_type | solution.py:50
  64.3 4.6 %collective-permute-done.1 = bf16[256,512]{1,0:T(8,128)(2,1)} collective-permute-done((bf16[256,512]{1,0:T(8,128)(2,1)}, bf16[256,512]{1,0:T(8,128)(2,1)}, u32[]{:S(2)}, u32[]{:S(2)}) %collective-permute-start.1) | collective-permute-done | bytes 262176 | tf_op jit(solution)/shard_map/ppermute | solution.py:23
  86.7 5.5 %collective-permute-done.19 = bf16[2,4,1,256,128]{4,3,2,1,0:T(8,128)(2,1)S(1)} collective-permute-done((bf16[2,4,1,256,128]{4,3,2,1,0:T(8,128)(2,1)S(1)}, bf16[2,4,1,256,128]{4,3,2,1,0:T(8,128)(2,1)S(1)}, u32[]{:S(2)}, u32[]{:S(2)}) %collective-permute-start.19) | collective-permute-done | bytes 524320 | tf_op jit(solution)/shard_map/ppermute | solution.py:23
  99.5 7.5 %collective-permute-done.7 = bf16[256,512]{1,0:T(8,128)(2,1)S(1)} collective-permute-done((bf16[256,512]{1,0:T(8,128)(2,1)S(1)}, bf16[256,512]{1,0:T(8,128)(2,1)S(1)}, u32[]{:S(2)}, u32[]{:S(2)}) %collective-permute-start.7) | collective-permute-done | bytes 262176 | tf_op jit(solution)/shard_map/ppermute | solution.py:23
  107.0 3.3 %collective-permute-start.11 = (bf16[1024,512]{1,0:T(8,128)(2,1)S(1)}, bf16[1024,512]{1,0:T(8,128)(2,1)}, u32[]{:S(2)}, u32[]{:S(2)}) collective-permute-start(bf16[1024,512]{1,0:T(8,128)(2,1)S(1)} %constant_dynamic-update-slice_fusion.5.refs_1_), channel_id=1, source_target_pairs={{0,24},{8,0},{16,8},{24,16},{1,25},{9,1},{17,9},{25,17},{2,26},{10... | collective-permute-start | bytes 3145736 | tf_op jit(solution)/shard_map/ppermute | solution.py:23
  112.5 4.1 %all-to-all-start = ((bf16[8,256,128]{2,1,0:T(8,128)(2,1)}), bf16[8,256,128]{2,1,0:T(8,128)(2,1)}, u32[]{:S(2)}, u32[]{:S(2)}) async-start(bf16[8,256,128]{2,1,0:T(8,128)(2,1)} %bitcast.53), calls=%async_computation | async-start | bytes 1048576 | tf_op jit(solution)/shard_map/all_to_all | solution.py:56
  116.7 4.0 %collective-permute-done.23 = bf16[2,1,8,256,128]{4,3,2,1,0:T(8,128)(2,1)} collective-permute-done((bf16[2,1,8,256,128]{4,3,2,1,0:T(8,128)(2,1)}, bf16[2,1,8,256,128]{4,3,2,1,0:T(8,128)(2,1)}, u32[]{:S(2)}, u32[]{:S(2)}) %collective-permute-start.23) | collective-permute-done | bytes 1048608 | tf_op jit(solution)/shard_map/ppermute | solution.py:23
  120.7 3.6 %add_convert_fusion = bf16[2,1,8,256,128]{4,3,2,1,0:T(8,128)(2,1)} fusion(bf16[2,1,8,256,128]{4,3,2,1,0:T(8,128)(2,1)} %collective-permute-done.23, bf16[2,1,8,256,128]{4,3,2,1,0:T(8,128)(2,1)} %collective-permute-done.21, f32[2,4,8,256,128]{4,3,2,1,0:T(8,128)} %bitcast.47, s32[]{:T(128)S(6)} %select_n.53), kind=kLoop, calls=%fused_computation.1 | loop fusion | flops 2621440 | bytes 5242884 | tf_op jit(solution)/shard_map/convert_element_type | solution.py:56
  124.3 15.1 %all-to-all-done = bf16[8,256,128]{2,1,0:T(8,128)(2,1)} async-done(((bf16[8,256,128]{2,1,0:T(8,128)(2,1)}), bf16[8,256,128]{2,1,0:T(8,128)(2,1)}, u32[]{:S(2)}, u32[]{:S(2)}) %all-to-all-start) | async-done | bytes 524320 | tf_op jit(solution)/shard_map/all_to_all | solution.py:56
  139.4 6.7 %all-to-all-start.1 = ((bf16[16,256,128]{2,1,0:T(8,128)(2,1)}), bf16[16,256,128]{2,1,0:T(8,128)(2,1)}, u32[]{:S(2)}, u32[]{:S(2)}) async-start(bf16[16,256,128]{2,1,0:T(8,128)(2,1)} %bitcast.52), calls=%async_computation.1 | async-start | bytes 2097152 | tf_op jit(solution)/shard_map/all_to_all | solution.py:56
  146.1 3.6 %collective-permute-start.13 = (bf16[1024,512]{1,0:T(8,128)(2,1)S(1)}, bf16[1024,512]{1,0:T(8,128)(2,1)}, u32[]{:S(2)}, u32[]{:S(2)}) collective-permute-start(bf16[1024,512]{1,0:T(8,128)(2,1)S(1)} %constant_dynamic-update-slice_fusion.refs_0_), channel_id=1, source_target_pairs={{0,24},{8,0},{16,8},{24,16},{1,25},{9,1},{17,9},{25,17},{2,26},{10... | collective-permute-start | bytes 3145736 | tf_op jit(solution)/shard_map/ppermute | solution.py:23
  156.3 7.0 %collective-permute-done.24 = f32[128,512]{1,0:T(8,128)S(1)} collective-permute-done((f32[128,512]{1,0:T(8,128)S(1)}, f32[128,512]{1,0:T(8,128)S(1)}, u32[]{:S(2)}, u32[]{:S(2)}) %collective-permute-start.24) | collective-permute-done | bytes 262176 | tf_op jit(solution)/shard_map/ppermute | solution.py:226
  169.8 3.5 %collective-permute-done.13.refs_6_ = bf16[1024,512]{1,0:T(8,128)(2,1)} collective-permute-done((bf16[1024,512]{1,0:T(8,128)(2,1)S(1)}, bf16[1024,512]{1,0:T(8,128)(2,1)}, u32[]{:S(2)}, u32[]{:S(2)}) %collective-permute-start.13) | collective-permute-done | bytes 1048608 | tf_op jit(solution)/shard_map/ppermute | solution.py:23
  173.3 3.8 %collective-permute-done.9.refs_3_ = bf16[1024,512]{1,0:T(8,128)(2,1)} collective-permute-done((bf16[1024,512]{1,0:T(8,128)(2,1)S(1)}, bf16[1024,512]{1,0:T(8,128)(2,1)}, u32[]{:S(2)}, u32[]{:S(2)}) %collective-permute-start.9) | collective-permute-done | bytes 1048608 | tf_op jit(solution)/shard_map/ppermute | solution.py:23
  177.1 13.9 %collective-permute-done.10.refs_4_ = bf16[1024,512]{1,0:T(8,128)(2,1)} collective-permute-done((bf16[1024,512]{1,0:T(8,128)(2,1)S(1)}, bf16[1024,512]{1,0:T(8,128)(2,1)}, u32[]{:S(2)}, u32[]{:S(2)}) %collective-permute-start.10) | collective-permute-done | bytes 1048608 | tf_op jit(solution)/shard_map/ppermute | solution.py:23
  193.3 13.8 %tail.1 = (bf16[256,512]{1,0:T(8,128)(2,1)}, bf16[256,8192]{1,0:T(8,128)(2,1)}) custom-call(s32[3]{0:T(128)S(1)} %pad_add_fusion.place, bf16[256,8192]{1,0:T(8,128)(2,1)S(1)} %bitcast.49, f32[1,8192]{1,0:T(1,128)S(1)} %copy-done.3, bf16[256,512]{1,0:T(8,128)(2,1)S(1)} %bitcast.51, f32[256,128]{1,0:T(8,128)S(1)} %copy-done.9, ...), custom_call_target="tpu_custom_call" | custom-call | flops 4294967296 | bytes 18874368 | tf_op jit(solution)/shard_map/tail/pallas_call | solution.py:172
  211.2 10.2 %all-to-all-start.2 = ((f32[64,1,128]{2,1,0:T(1,128)}), f32[64,1,128]{2,1,0:T(1,128)S(1)}, u32[]{:S(2)}, u32[]{:S(2)}) async-start(f32[64,1,128]{2,1,0:T(1,128)} %broadcast_in_dim.15), calls=%async_computation.2 | async-start | bytes 65536 | tf_op jit(solution)/shard_map/all_to_all | solution.py:245
  222.2 11.2 %all-to-all-done.2 = f32[64,1,128]{2,1,0:T(1,128)S(1)} async-done(((f32[64,1,128]{2,1,0:T(1,128)}), f32[64,1,128]{2,1,0:T(1,128)S(1)}, u32[]{:S(2)}, u32[]{:S(2)}) %all-to-all-start.2) | async-done | bytes 32800 | tf_op jit(solution)/shard_map/all_to_all | solution.py:245
  (90 shorter events, 66.9 us)
Async XLA Ops:
  17.2 17.9 %collective-permute-start.14 = (bf16[2,4,1,256,128]{4,3,2,1,0:T(8,128)(2,1)S(1)}, bf16[2,4,1,256,128]{4,3,2,1,0:T(8,128)(2,1)S(1)}, u32[]{:S(2)}, u32[]{:S(2)}) collective-permute-start(bf16[2,4,1,256,128]{4,3,2,1,0:T(8,128)(2,1)S(1)} %get-tuple-element.26), channel_id=1, source_target_pairs={{0,1},{1,2},{2,3},{3,4},{4,5},{5,6},{6,7},{7,0},{8,9},{9,10},{10,1... | collective-permute-start | bytes 1572872 | tf_op jit(solution)/shard_map/ppermute | solution.py:23
  19.2 19.5 %collective-permute-start.17 = (bf16[2,4,1,256,128]{4,3,2,1,0:T(8,128)(2,1)S(1)}, bf16[2,4,1,256,128]{4,3,2,1,0:T(8,128)(2,1)S(1)}, u32[]{:S(2)}, u32[]{:S(2)}) collective-permute-start(bf16[2,4,1,256,128]{4,3,2,1,0:T(8,128)(2,1)S(1)} %get-tuple-element.27), channel_id=1, source_target_pairs={{0,7},{1,0},{2,1},{3,2},{4,3},{5,4},{6,5},{7,6},{8,15},{9,8},{10,9... | collective-permute-start | bytes 1572872 | tf_op jit(solution)/shard_map/ppermute | solution.py:23
  36.4 14.4 %collective-permute-start.15 = (bf16[2,4,1,256,128]{4,3,2,1,0:T(8,128)(2,1)S(1)}, bf16[2,4,1,256,128]{4,3,2,1,0:T(8,128)(2,1)S(1)}, u32[]{:S(2)}, u32[]{:S(2)}) collective-permute-start(bf16[2,4,1,256,128]{4,3,2,1,0:T(8,128)(2,1)S(1)} %add_convert_fusion.7), channel_id=1, source_target_pairs={{0,1},{1,2},{2,3},{3,4},{4,5},{5,6},{6,7},{7,0},{8,9},{9,10},{10,1... | collective-permute-start | bytes 1572872 | tf_op jit(solution)/shard_map/ppermute | solution.py:23
  36.5 23.8 %collective-permute-start = (bf16[128,512]{1,0:T(8,128)(2,1)S(1)}, bf16[128,512]{1,0:T(8,128)(2,1)S(1)}, u32[]{:S(2)}, u32[]{:S(2)}) collective-permute-start(bf16[128,512]{1,0:T(8,128)(2,1)S(1)} %bitcast.54), channel_id=1, source_target_pairs={{0,32},{32,0},{1,33},{33,1},{2,34},{34,2},{3,35},{35,3},{4,36},{36... | collective-permute-start | bytes 393224 | tf_op jit(solution)/shard_map/ppermute | solution.py:23
  53.6 19.6 %collective-permute-start.18 = (bf16[2,4,1,256,128]{4,3,2,1,0:T(8,128)(2,1)}, bf16[2,4,1,256,128]{4,3,2,1,0:T(8,128)(2,1)}, u32[]{:S(2)}, u32[]{:S(2)}) collective-permute-start(bf16[2,4,1,256,128]{4,3,2,1,0:T(8,128)(2,1)} %get-tuple-element.25), channel_id=1, source_target_pairs={{0,7},{1,0},{2,1},{3,2},{4,3},{5,4},{6,5},{7,6},{8,15},{9,8},{10,9... | collective-permute-start | bytes 1572872 | tf_op jit(solution)/shard_map/ppermute | solution.py:23
  57.3 26.5 %collective-permute-start.22 = (bf16[2,1,8,256,128]{4,3,2,1,0:T(8,128)(2,1)S(1)}, bf16[2,1,8,256,128]{4,3,2,1,0:T(8,128)(2,1)S(1)}, u32[]{:S(2)}, u32[]{:S(2)}) collective-permute-start(bf16[2,1,8,256,128]{4,3,2,1,0:T(8,128)(2,1)S(1)} %get-tuple-element.23), channel_id=1, source_target_pairs={{0,24},{8,0},{16,8},{24,16},{1,25},{9,1},{17,9},{25,17},{2,26},{10... | collective-permute-start | bytes 3145736 | tf_op jit(solution)/shard_map/ppermute | solution.py:23
  62.8 8.8 %collective-permute-start.2 = (bf16[256,512]{1,0:T(8,128)(2,1)}, bf16[256,512]{1,0:T(8,128)(2,1)}, u32[]{:S(2)}, u32[]{:S(2)}) collective-permute-start(bf16[256,512]{1,0:T(8,128)(2,1)} %pad_maximum_fusion), channel_id=1, source_target_pairs={{0,7},{1,0},{2,1},{3,2},{4,3},{5,4},{6,5},{7,6},{8,15},{9,8},{10,9... | collective-permute-start | bytes 786440 | tf_op jit(solution)/shard_map/ppermute | solution.py:23
  64.3 52.4 %collective-permute-start.21 = (bf16[2,1,8,256,128]{4,3,2,1,0:T(8,128)(2,1)}, bf16[2,1,8,256,128]{4,3,2,1,0:T(8,128)(2,1)}, u32[]{:S(2)}, u32[]{:S(2)}) collective-permute-start(bf16[2,1,8,256,128]{4,3,2,1,0:T(8,128)(2,1)} %get-tuple-element.22), channel_id=1, source_target_pairs={{0,8},{8,16},{16,24},{24,0},{1,9},{9,17},{17,25},{25,1},{2,10},{10... | collective-permute-start | bytes 3145736 | tf_op jit(solution)/shard_map/ppermute | solution.py:23
  71.7 9.4 %collective-permute-start.4 = (bf16[256,512]{1,0:T(8,128)(2,1)}, bf16[256,512]{1,0:T(8,128)(2,1)S(1)}, u32[]{:S(2)}, u32[]{:S(2)}) collective-permute-start(bf16[256,512]{1,0:T(8,128)(2,1)} %collective-permute-done.2), channel_id=1, source_target_pairs={{0,7},{1,0},{2,1},{3,2},{4,3},{5,4},{6,5},{7,6},{8,15},{9,8},{10,9... | collective-permute-start | bytes 786440 | tf_op jit(solution)/shard_map/ppermute | solution.py:23
  74.7 17.6 %collective-permute-start.19 = (bf16[2,4,1,256,128]{4,3,2,1,0:T(8,128)(2,1)S(1)}, bf16[2,4,1,256,128]{4,3,2,1,0:T(8,128)(2,1)S(1)}, u32[]{:S(2)}, u32[]{:S(2)}) collective-permute-start(bf16[2,4,1,256,128]{4,3,2,1,0:T(8,128)(2,1)S(1)} %add_convert_fusion.4), channel_id=1, source_target_pairs={{0,7},{1,0},{2,1},{3,2},{4,3},{5,4},{6,5},{7,6},{8,15},{9,8},{10,9... | collective-permute-start | bytes 1572872 | tf_op jit(solution)/shard_map/ppermute | solution.py:23
  76.7 20.0 %collective-permute-start.5 = (bf16[256,512]{1,0:T(8,128)(2,1)S(1)}, bf16[256,512]{1,0:T(8,128)(2,1)S(1)}, u32[]{:S(2)}, u32[]{:S(2)}) collective-permute-start(bf16[256,512]{1,0:T(8,128)(2,1)S(1)} %collective-permute-done.3), channel_id=1, source_target_pairs={{0,1},{1,2},{2,3},{3,4},{4,5},{5,6},{6,7},{7,0},{8,9},{9,10},{10,1... | collective-permute-start | bytes 786440 | tf_op jit(solution)/shard_map/ppermute | solution.py:23
  81.1 18.2 %collective-permute-start.6 = (bf16[256,512]{1,0:T(8,128)(2,1)S(1)}, bf16[256,512]{1,0:T(8,128)(2,1)S(1)}, u32[]{:S(2)}, u32[]{:S(2)}) collective-permute-start(bf16[256,512]{1,0:T(8,128)(2,1)S(1)} %collective-permute-done.4), channel_id=1, source_target_pairs={{0,7},{1,0},{2,1},{3,2},{4,3},{5,4},{6,5},{7,6},{8,15},{9,8},{10,9... | collective-permute-start | bytes 786440 | tf_op jit(solution)/shard_map/ppermute | solution.py:23
  83.8 23.2 %collective-permute-start.16 = (bf16[2,4,1,256,128]{4,3,2,1,0:T(8,128)(2,1)}, bf16[2,4,1,256,128]{4,3,2,1,0:T(8,128)(2,1)S(1)}, u32[]{:S(2)}, u32[]{:S(2)}) collective-permute-start(bf16[2,4,1,256,128]{4,3,2,1,0:T(8,128)(2,1)} %get-tuple-element.24), channel_id=1, source_target_pairs={{0,1},{1,2},{2,3},{3,4},{4,5},{5,6},{6,7},{7,0},{8,9},{9,10},{10,1... | collective-permute-start | bytes 1572872 | tf_op jit(solution)/shard_map/ppermute | solution.py:23
  92.2 28.5 %collective-permute-start.23 = (bf16[2,1,8,256,128]{4,3,2,1,0:T(8,128)(2,1)}, bf16[2,1,8,256,128]{4,3,2,1,0:T(8,128)(2,1)}, u32[]{:S(2)}, u32[]{:S(2)}) collective-permute-start(bf16[2,1,8,256,128]{4,3,2,1,0:T(8,128)(2,1)} %add_convert_fusion.1), channel_id=1, source_target_pairs={{0,24},{8,0},{16,8},{24,16},{1,25},{9,1},{17,9},{25,17},{2,26},{10... | collective-permute-start | bytes 3145736 | tf_op jit(solution)/shard_map/ppermute | solution.py:23
  96.7 13.5 %collective-permute-start.20 = (bf16[2,4,1,256,128]{4,3,2,1,0:T(8,128)(2,1)S(1)}, bf16[2,4,1,256,128]{4,3,2,1,0:T(8,128)(2,1)S(1)}, u32[]{:S(2)}, u32[]{:S(2)}) collective-permute-start(bf16[2,4,1,256,128]{4,3,2,1,0:T(8,128)(2,1)S(1)} %add_convert_fusion.3), channel_id=1, source_target_pairs={{0,7},{1,0},{2,1},{3,2},{4,3},{5,4},{6,5},{7,6},{8,15},{9,8},{10,9... | collective-permute-start | bytes 1572872 | tf_op jit(solution)/shard_map/ppermute | solution.py:23
  106.9 42.8 %collective-permute-start.8 = (bf16[1024,512]{1,0:T(8,128)(2,1)S(1)}, bf16[1024,512]{1,0:T(8,128)(2,1)S(1)}, u32[]{:S(2)}, u32[]{:S(2)}) collective-permute-start(bf16[1024,512]{1,0:T(8,128)(2,1)S(1)} %constant_dynamic-update-slice_fusion.refs_0_), channel_id=1, source_target_pairs={{0,8},{8,16},{16,24},{24,0},{1,9},{9,17},{17,25},{25,1},{2,10},{10... | collective-permute-start | bytes 3145736 | tf_op jit(solution)/shard_map/ppermute | solution.py:23
  107.0 43.1 %collective-permute-start.11 = (bf16[1024,512]{1,0:T(8,128)(2,1)S(1)}, bf16[1024,512]{1,0:T(8,128)(2,1)}, u32[]{:S(2)}, u32[]{:S(2)}) collective-permute-start(bf16[1024,512]{1,0:T(8,128)(2,1)S(1)} %constant_dynamic-update-slice_fusion.5.refs_1_), channel_id=1, source_target_pairs={{0,24},{8,0},{16,8},{24,16},{1,25},{9,1},{17,9},{25,17},{2,26},{10... | collective-permute-start | bytes 3145736 | tf_op jit(solution)/shard_map/ppermute | solution.py:23
  112.5 26.9 %all-to-all-start = ((bf16[8,256,128]{2,1,0:T(8,128)(2,1)}), bf16[8,256,128]{2,1,0:T(8,128)(2,1)}, u32[]{:S(2)}, u32[]{:S(2)}) async-start(bf16[8,256,128]{2,1,0:T(8,128)(2,1)} %bitcast.53), calls=%async_computation | async-start | bytes 1048576 | tf_op jit(solution)/shard_map/all_to_all | solution.py:56
  139.4 67.7 %all-to-all-start.1 = ((bf16[16,256,128]{2,1,0:T(8,128)(2,1)}), bf16[16,256,128]{2,1,0:T(8,128)(2,1)}, u32[]{:S(2)}, u32[]{:S(2)}) async-start(bf16[16,256,128]{2,1,0:T(8,128)(2,1)} %bitcast.52), calls=%async_computation.1 | async-start | bytes 2097152 | tf_op jit(solution)/shard_map/all_to_all | solution.py:56
  146.1 27.2 %collective-permute-start.13 = (bf16[1024,512]{1,0:T(8,128)(2,1)S(1)}, bf16[1024,512]{1,0:T(8,128)(2,1)}, u32[]{:S(2)}, u32[]{:S(2)}) collective-permute-start(bf16[1024,512]{1,0:T(8,128)(2,1)S(1)} %constant_dynamic-update-slice_fusion.refs_0_), channel_id=1, source_target_pairs={{0,24},{8,0},{16,8},{24,16},{1,25},{9,1},{17,9},{25,17},{2,26},{10... | collective-permute-start | bytes 3145736 | tf_op jit(solution)/shard_map/ppermute | solution.py:23
  149.7 27.4 %collective-permute-start.9 = (bf16[1024,512]{1,0:T(8,128)(2,1)S(1)}, bf16[1024,512]{1,0:T(8,128)(2,1)}, u32[]{:S(2)}, u32[]{:S(2)}) collective-permute-start(bf16[1024,512]{1,0:T(8,128)(2,1)S(1)} %constant_dynamic-update-slice_fusion.5.refs_1_), channel_id=1, source_target_pairs={{0,8},{8,16},{16,24},{24,0},{1,9},{9,17},{17,25},{25,1},{2,10},{10... | collective-permute-start | bytes 3145736 | tf_op jit(solution)/shard_map/ppermute | solution.py:23
  149.7 41.4 %collective-permute-start.10 = (bf16[1024,512]{1,0:T(8,128)(2,1)S(1)}, bf16[1024,512]{1,0:T(8,128)(2,1)}, u32[]{:S(2)}, u32[]{:S(2)}) collective-permute-start(bf16[1024,512]{1,0:T(8,128)(2,1)S(1)} %collective-permute-done.8.refs_2_), channel_id=1, source_target_pairs={{0,8},{8,16},{16,24},{24,0},{1,9},{9,17},{17,25},{25,1},{2,10},{10... | collective-permute-start | bytes 3145736 | tf_op jit(solution)/shard_map/ppermute | solution.py:23
  150.1 41.0 %collective-permute-start.12 = (bf16[1024,512]{1,0:T(8,128)(2,1)}, bf16[1024,512]{1,0:T(8,128)(2,1)}, u32[]{:S(2)}, u32[]{:S(2)}) collective-permute-start(bf16[1024,512]{1,0:T(8,128)(2,1)} %collective-permute-done.11.refs_7_), channel_id=1, source_target_pairs={{0,24},{8,0},{16,8},{24,16},{1,25},{9,1},{17,9},{25,17},{2,26},{10... | collective-permute-start | bytes 3145736 | tf_op jit(solution)/shard_map/ppermute | solution.py:23
  211.2 22.1 %all-to-all-start.2 = ((f32[64,1,128]{2,1,0:T(1,128)}), f32[64,1,128]{2,1,0:T(1,128)S(1)}, u32[]{:S(2)}, u32[]{:S(2)}) async-start(f32[64,1,128]{2,1,0:T(1,128)} %broadcast_in_dim.15), calls=%async_computation.2 | async-start | bytes 65536 | tf_op jit(solution)/shard_map/all_to_all | solution.py:245
  (16 other events, 186.3 us)

commit v2 on v1

--- a/solution.py
+++ b/solution.py
@@ -23,33 +23,18 @@
     return lax.ppermute(value, axis, [(i, (i + step) % n) for i in range(n)])
 
 
-def gather(own, axis, last):
-    n = SIZE[axis]
-    blocks = {0: own}
-    right = left = own
-    for hop in range(1, n // 2):
-        right, left = shift(right, axis, 1), shift(left, axis, -1)
-        blocks[hop], blocks[n - hop] = right, left
-    blocks[n // 2] = shift(right if last > 0 else left, axis, last)
-    return [blocks[i] for i in range(n)]
-
-
-def scatter_sum(part, axis, dim):
-    n = SIZE[axis]
-
-    def term(step):
-        at = (lax.axis_index(axis) + step) & (n - 1)
-        return lax.dynamic_slice_in_dim(part, at, 1, dim)
-
-    left = shift(term(-(n // 2)).astype(BF16), axis, -1)
-    right = None
-    for hop in range(n // 2 - 1, 0, -1):
-        ahead, behind = term(hop), term(-hop) + left.astype(F32)
-        if right is not None:
-            ahead = ahead + right.astype(F32)
-        right = shift(ahead.astype(BF16), axis, 1)
-        left = shift(behind.astype(BF16), axis, -1)
-    return term(0) + right.astype(F32) + left.astype(F32)
+def together(*values):
+    return lax.optimization_barrier(values)
+
+
+def term(part, axis, dim, step):
+    at = (lax.axis_index(axis) + step) & (SIZE[axis] - 1)
+    return lax.dynamic_slice_in_dim(part, at, 1, dim)
+
+
+def onward(part, axis, dim, step, received):
+    total = term(part, axis, dim, step) + received.astype(F32)
+    return shift(total.astype(BF16), axis, 1 if step > 0 else -1)
 
 
 def exchange_sum(part, axes):
@@ -109,7 +94,7 @@
             pl.BlockSpec((tokens, LANES), whole),
         ),
         scratch_shapes=[pltpu.VMEM((tokens, LANES), F32), pltpu.VMEM((keys, tokens), BF16)],
-        compiler_params=pltpu.CompilerParams(vmem_limit_bytes=32 * 1024 * 1024),
+        compiler_params=pltpu.CompilerParams(vmem_limit_bytes=56 * 1024 * 1024),
         cost_estimate=pl.CostEstimate(
             flops=2 * tokens * width * keys, bytes_accessed=22 * 1024 * 1024, transcendentals=0
         ),
@@ -221,32 +206,70 @@
     chosen = fragment_index[0]
     current = lax.dynamic_index_in_dim(outer_params, chosen, 0, keepdims=False)
     inner_now = lax.dynamic_index_in_dim(inner_params[0], chosen, 0, keepdims=False)
-    summed = current - inner_now
-    for axis in REPL:
-        summed = summed + lax.ppermute(summed, axis, [(0, 1), (1, 0)])
-
-    pair = jnp.concatenate([own, shift(own, "xh", 1)])
-    along_z = gather(pair, "z", 1)
-    first = gather(jnp.concatenate([along_z[i] for i in FIRST]), "y", 1)
-    second = gather(jnp.concatenate([along_z[i] for i in SECOND]), "y", -1)
-    weights = [block for both in zip(first, second) for block in both]
-
     part_a, part_b, inverse = weight_grad(hidden, norm_gain, cotangent)
     part_a = part_a.reshape(*groups, cut, rows)
     part_b = part_b.reshape(*groups, cut, rows)
-    sum_a = exchange_sum(scatter_sum(part_a, "z", 2).reshape(-1, cut, rows), ("xh", "y"))
-    sum_b = exchange_sum(scatter_sum(part_b, "y", 1).reshape(-1, cut, rows), ("xh", "z"))
-    sum_a, sum_b = lax.optimization_barrier((sum_a, sum_b))
+    half = cut // 2
+
+    mine = current - inner_now
+    over_x = shift(own, "xh", 1)
+    core = lax.ppermute(mine, "core", [(0, 1), (1, 0)])
+    over_x, part_a, part_b, inverse, core = together(over_x, part_a, part_b, inverse, core)
+    pair = jnp.concatenate([own, over_x])
+
+    far_a = term(part_a, "z", 2, -4).astype(BF16)
+    far_b = term(part_b, "y", 1, 2).astype(BF16)
+    a_left = shift(far_a, "z", -1)
+    z1, z7 = shift(pair, "z", 1), shift(pair, "z", -1)
+    b_left = shift(far_b[..., half:, :], "y", -1)
+    b_right = shift(far_b[..., :half, :], "y", 1)
+    a_left, z1, z7, b_left, b_right = together(a_left, z1, z7, b_left, b_right)
+
+    a_left = onward(part_a, "z", 2, -3, a_left)
+    a_right = shift(term(part_a, "z", 2, 3).astype(BF16), "z", 1)
+    z2, z6 = shift(z1, "z", 1), shift(z7, "z", -1)
+    none = jnp.zeros_like(b_left)
+    b_left = onward(part_b, "y", 1, -1, jnp.concatenate([none, b_left], axis=3))
+    b_right = onward(part_b, "y", 1, 1, jnp.concatenate([b_right, none], axis=3))
+    a_left, a_right, z2, z6 = together(a_left, a_right, z2, z6)
+
+    a_left = onward(part_a, "z", 2, -2, a_left)
+    a_right = onward(part_a, "z", 2, 2, a_right)
+    z3, z5 = shift(z2, "z", 1), shift(z6, "z", -1)
+    first = jnp.concatenate([pair, z1, z7, z2])
+    first1, first3 = shift(first, "y", 1), shift(first, "y", -1)
+    a_left, a_right, z3, z5, b_left, b_right = together(a_left, a_right, z3, z5, b_left, b_right)
+
+    sum_b = term(part_b, "y", 1, 0) + b_left.astype(F32) + b_right.astype(F32)
+    sum_b = exchange_sum(sum_b.reshape(-1, cut, rows), ("xh", "z"))
+    a_left = onward(part_a, "z", 2, -1, a_left)
+    a_right = onward(part_a, "z", 2, 1, a_right)
+    z4 = shift(z3, "z", 1)
+    a_left, a_right, z4, first1, first3, sum_b, core = together(
+        a_left, a_right, z4, first1, first3, sum_b, core
+    )
+
+    sum_a = term(part_a, "z", 2, 0) + a_left.astype(F32) + a_right.astype(F32)
+    sum_a = exchange_sum(sum_a.reshape(-1, cut, rows), ("xh", "y"))
+    second = jnp.concatenate([z6, z3, z5, z4])
+    second1, second3 = shift(second, "y", 1), shift(second, "y", -1)
+    first2 = shift(first1, "y", 1)
+    both = mine + core
+    summed = both + lax.ppermute(both, "xl", [(0, 1), (1, 0)])
+    sum_a, second1, second3, summed = together(sum_a, second1, second3, summed)
+    second2 = shift(second3, "y", -1)
+    weights = [first, second, first1, second1, first2, second2, first3, second3]
+
     grad_weight = jnp.concatenate([sum_a.T, sum_b.T], axis=-1) * factor
 
     me = lax.axis_index(GROUP)
     own_gain = lax.dynamic_slice_in_dim(norm_gain[0], me * rows, rows)
     own_sum = jnp.sum(own.astype(F32) * grad_weight, axis=-1) / own_gain
+    place = jnp.stack([lax.axis_index(axis) for axis in GROUP])
+    own_sum, weights[-1], weights[-3] = together(own_sum, weights[-1], weights[-3])
     grad_gain = lax.all_to_all(
         jnp.broadcast_to(own_sum[None], (devices, rows)), GROUP, 0, 0, tiled=True
     ).reshape(-1)
-
-    place = jnp.stack([lax.axis_index(axis) for axis in GROUP])
     key_out, grad_hidden = tail(place, hidden, norm_gain, cotangent, inverse, weights)
 
     moment = lax.dynamic_index_in_dim(outer_momentum, chosen, 0, keepdims=False)

time: 235 us -> 226 us (0.962)
  waiting for transfers between devices: 106 us -> 83.6 us
  Pallas kernels: 19.7 us -> 25.4 us
  other arithmetic: 25.3 us -> 30 us
  starting transfers between devices: 60.4 us -> 65 us
  local copies, waits for them, and re-layouts: 20.7 us -> 18.1 us
    ppermute x24 -> x25, waiting for transfers between devices: 71.2 us -> 52.4 us  [shift(): return lax.ppermute(value, axis, [(i, (i + step) % n) for i in range(n)])]
    all_to_all x1, waiting for transfers between devices: 11.2 us -> 0.01 us  [per_device(): lax.all_to_all(jnp.broadcast_to(own_sum[None], (devices, rows)), GROUP, 0...]
    unnamed x30 -> x20, local copies, waits for them, and re-layouts: 15.2 us -> 7.67 us
    all_to_all x2, waiting for transfers between devices: 15.1 us -> 22.4 us  [exchange_sum(): blocks = lax.all_to_all(part.astype(BF16), axes, 0, 0, tiled=True)]
    pallas_call x1, Pallas kernels: 5.91 us -> 11.6 us  [weight_grad(): pl.pallas_call(weight_grad_kernel, grid=(blocks // per_step,), out_shape=...]
    ppermute x24 -> x25, starting transfers between devices: 37.8 us -> 40 us  [shift(): return lax.ppermute(value, axis, [(i, (i + step) % n) for i in range(n)])]
    convert_element_type x5 -> x4, other arithmetic: 9.83 us -> 11.9 us  [onward(): return shift(total.astype(BF16), axis, 1 if step > 0 else -1)]
  transfers between devices with their start and end apart: 29 -> 30, of which waited for: 15 -> 11; matrix products, arithmetic and copies ran while one was open for 12% -> 16% of each run, Pallas kernels for 6% -> 11%
where the time goes in v2:
time: 226 us; the launch traced here: 223 us
  waiting for transfers between devices  83.6 us (37%)
  starting transfers between devices  65 us (29%)
  other arithmetic  30 us (13%)
  Pallas kernels  25.4 us (11%)
  local copies, waits for them, and re-layouts  18.1 us (8%)
    ppermute x25, waiting for transfers between devices, shift(): return lax.ppermute(value, axis, [(i, (i + step) % n) for i in range(n)])  52.4 us
    ppermute x25, starting transfers between devices, shift(): return lax.ppermute(value, axis, [(i, (i + step) % n) for i in range(n)])  40 us
    all_to_all x2, waiting for transfers between devices, exchange_sum(): blocks = lax.all_to_all(part.astype(BF16), axes, 0, 0, tiled=True)  22.4 us
    pallas_call x1, Pallas kernels, tail(): pl.pallas_call(functools.partial(tail_kernel, count), out_shape=(jax.Shap...  13.8 us
    all_to_all x1, starting transfers between devices, per_device(): lax.all_to_all(jnp.broadcast_to(own_sum[None], (devices, rows)), GROUP, 0...  12.5 us
    convert_element_type x4, other arithmetic, onward(): return shift(total.astype(BF16), axis, 1 if step > 0 else -1)  11.9 us
    all_to_all x2, starting transfers between devices, exchange_sum(): blocks = lax.all_to_all(part.astype(BF16), axes, 0, 0, tiled=True)  11.8 us
    pallas_call x1, Pallas kernels, weight_grad(): pl.pallas_call(weight_grad_kernel, grid=(blocks // per_step,), out_shape=...  11.6 us
  transfers between devices with their start and end apart: 30, of which 11 were waited for; matrix products, arithmetic and copies ran while one was open for 16% of the time, Pallas kernels for 11%

profile of v2, /device:TPU:2, one launch (start us, length us, event | category | flops | bytes accessed | tf_op | source)
XLA Modules:
  0.0 223.5 jit_solution(2644261189799141469)
XLA Ops:
  4.7 11.6 %weight_grad.1 = (f32[64,256,128]{2,1,0:T(8,128)}, f32[64,256,128]{2,1,0:T(8,128)}, f32[256,128]{1,0:T(8,128)}) custom-call(bf16[256,8192]{1,0:T(8,128)(2,1)} %bitcast.37, f32[1,8192]{1,0:T(1,128)} %gain.3, bf16[256,512]{1,0:T(8,128)(2,1)} %bitcast.39), custom_call_target="tpu_custom_call" | custom-call | flops 2147483648 | bytes 23068672 | tf_op jit(solution)/shard_map/weight_grad/pallas_call | solution.py:82
  18.9 5.9 %collective-permute-start.2 = (bf16[2,4,1,256,128]{4,3,2,1,0:T(8,128)(2,1)S(1)}, bf16[2,4,1,256,128]{4,3,2,1,0:T(8,128)(2,1)S(1)}, u32[]{:S(2)}, u32[]{:S(2)}) collective-permute-start(bf16[2,4,1,256,128]{4,3,2,1,0:T(8,128)(2,1)S(1)} %get-tuple-element.93), channel_id=1, source_target_pairs={{0,7},{1,0},{2,1},{3,2},{4,3},{5,4},{6,5},{7,6},{8,15},{9,8},{10,9... | collective-permute-start | bytes 1572872 | tf_op jit(solution)/shard_map/ppermute | solution.py:23
  26.6 3.1 %collective-permute-start.5 = (bf16[2,1,8,128,128]{4,3,2,1,0:T(8,128)(2,1)S(1)}, bf16[2,1,8,128,128]{4,3,2,1,0:T(8,128)(2,1)}, u32[]{:S(2)}, u32[]{:S(2)}) collective-permute-start(bf16[2,1,8,128,128]{4,3,2,1,0:T(8,128)(2,1)S(1)} %get-tuple-element.95), channel_id=1, source_target_pairs={{0,24},{8,0},{16,8},{24,16},{1,25},{9,1},{17,9},{25,17},{2,26},{10... | collective-permute-start | bytes 1572872 | tf_op jit(solution)/shard_map/ppermute | solution.py:23
  30.5 3.2 %collective-permute-start.4 = (bf16[256,512]{1,0:T(8,128)(2,1)}, bf16[256,512]{1,0:T(8,128)(2,1)}, u32[]{:S(2)}, u32[]{:S(2)}) collective-permute-start(bf16[256,512]{1,0:T(8,128)(2,1)} %pad_maximum_fusion), channel_id=1, source_target_pairs={{0,7},{1,0},{2,1},{3,2},{4,3},{5,4},{6,5},{7,6},{8,15},{9,8},{10,9... | collective-permute-start | bytes 786440 | tf_op jit(solution)/shard_map/ppermute | solution.py:23
  33.7 6.0 %collective-permute-done.3 = bf16[256,512]{1,0:T(8,128)(2,1)S(1)} collective-permute-done((bf16[256,512]{1,0:T(8,128)(2,1)}, bf16[256,512]{1,0:T(8,128)(2,1)S(1)}, u32[]{:S(2)}, u32[]{:S(2)}) %collective-permute-start.3) | collective-permute-done | bytes 262176 | tf_op jit(solution)/shard_map/ppermute | solution.py:23
  49.8 3.9 %add_convert_fusion.1 = (bf16[2,1,8,256,128]{4,3,2,1,0:T(8,128)(2,1)S(1)}, bf16[2,1,8,256,128]{4,3,2,1,0:T(8,128)(2,1)}) fusion(f32[2,4,8,256,128]{4,3,2,1,0:T(8,128)} %bitcast.47, s32[]{:T(128)S(6)} %select_n.53, bf16[2,1,8,128,128]{4,3,2,1,0:T(8,128)(2,1)} %collective-permute-done.6, bf16[2,1,8,128,128]{4,3,2,1,0:T(8,128)(2,1)} %collective-permute-done.5, ...), kind=kLoop, calls=%fused_computation.2 | loop fusion | flops 3145728 | bytes 7340040 | tf_op jit(solution)/shard_map/convert_element_type | solution.py:37
  53.7 3.0 %collective-permute-start.15 = (bf16[2,1,8,256,128]{4,3,2,1,0:T(8,128)(2,1)}, bf16[2,1,8,256,128]{4,3,2,1,0:T(8,128)(2,1)S(1)}, u32[]{:S(2)}, u32[]{:S(2)}) collective-permute-start(bf16[2,1,8,256,128]{4,3,2,1,0:T(8,128)(2,1)} %get-tuple-element.89), channel_id=1, source_target_pairs={{0,24},{8,0},{16,8},{24,16},{1,25},{9,1},{17,9},{25,17},{2,26},{10... | collective-permute-start | bytes 3145736 | tf_op jit(solution)/shard_map/ppermute | solution.py:23
  56.7 8.3 %collective-permute-done.10 = bf16[256,512]{1,0:T(8,128)(2,1)} collective-permute-done((bf16[256,512]{1,0:T(8,128)(2,1)}, bf16[256,512]{1,0:T(8,128)(2,1)}, u32[]{:S(2)}, u32[]{:S(2)}) %collective-permute-start.10) | collective-permute-done | bytes 262176 | tf_op jit(solution)/shard_map/ppermute | solution.py:23
  65.1 3.0 %add_convert_fusion.6 = (bf16[2,4,1,256,128]{4,3,2,1,0:T(8,128)(2,1)}, bf16[2,4,1,256,128]{4,3,2,1,0:T(8,128)(2,1)}) fusion(bf16[2,4,1,256,128]{4,3,2,1,0:T(8,128)(2,1)S(1)} %collective-permute-done.8, f32[2,4,8,256,128]{4,3,2,1,0:T(8,128)} %bitcast.43, s32[]{:T(128)S(6)} %select_n.51, bf16[2,4,1,256,128]{4,3,2,1,0:T(8,128)(2,1)} %collective-permute-done.7, ...), kind=kLoop, calls=%fused_computation.9 | loop fusion | flops 1572864 | bytes 4194312 | tf_op jit(solution)/shard_map/convert_element_type | solution.py:37
  68.0 3.2 %collective-permute-start.11 = (bf16[2,4,1,256,128]{4,3,2,1,0:T(8,128)(2,1)}, bf16[2,4,1,256,128]{4,3,2,1,0:T(8,128)(2,1)S(1)}, u32[]{:S(2)}, u32[]{:S(2)}) collective-permute-start(bf16[2,4,1,256,128]{4,3,2,1,0:T(8,128)(2,1)} %get-tuple-element.91), channel_id=1, source_target_pairs={{0,7},{1,0},{2,1},{3,2},{4,3},{5,4},{6,5},{7,6},{8,15},{9,8},{10,9... | collective-permute-start | bytes 1572872 | tf_op jit(solution)/shard_map/ppermute | solution.py:23
  73.3 2.9 %collective-permute-start.14 = (bf16[256,512]{1,0:T(8,128)(2,1)}, bf16[256,512]{1,0:T(8,128)(2,1)}, u32[]{:S(2)}, u32[]{:S(2)}) collective-permute-start(bf16[256,512]{1,0:T(8,128)(2,1)} %collective-permute-done.10), channel_id=1, source_target_pairs={{0,7},{1,0},{2,1},{3,2},{4,3},{5,4},{6,5},{7,6},{8,15},{9,8},{10,9... | collective-permute-start | bytes 786440 | tf_op jit(solution)/shard_map/ppermute | solution.py:23
  76.2 10.6 %collective-permute-done.14 = bf16[256,512]{1,0:T(8,128)(2,1)} collective-permute-done((bf16[256,512]{1,0:T(8,128)(2,1)}, bf16[256,512]{1,0:T(8,128)(2,1)}, u32[]{:S(2)}, u32[]{:S(2)}) %collective-permute-start.14) | collective-permute-done | bytes 262176 | tf_op jit(solution)/shard_map/ppermute | solution.py:23
  86.8 3.3 %add_convert_fusion = bf16[2,1,8,256,128]{4,3,2,1,0:T(8,128)(2,1)} fusion(bf16[2,1,8,256,128]{4,3,2,1,0:T(8,128)(2,1)} %collective-permute-done.16, bf16[2,1,8,256,128]{4,3,2,1,0:T(8,128)(2,1)S(1)} %collective-permute-done.15, f32[2,4,8,256,128]{4,3,2,1,0:T(8,128)} %bitcast.48, s32[]{:T(128)S(6)} %select_n.56), kind=kLoop, calls=%fused_computation.1 | loop fusion | flops 2621440 | bytes 5242884 | tf_op jit(solution)/shard_map/convert_element_type | solution.py:41
  90.0 6.0 %all-to-all-start = ((bf16[16,256,128]{2,1,0:T(8,128)(2,1)}), bf16[16,256,128]{2,1,0:T(8,128)(2,1)}, u32[]{:S(2)}, u32[]{:S(2)}) async-start(bf16[16,256,128]{2,1,0:T(8,128)(2,1)} %bitcast.11), calls=%async_computation | async-start | bytes 2097152 | tf_op jit(solution)/shard_map/all_to_all | solution.py:41
  101.3 2.9 %add_convert_fusion.4 = (bf16[2,4,1,256,128]{4,3,2,1,0:T(8,128)(2,1)}, bf16[2,4,1,256,128]{4,3,2,1,0:T(8,128)(2,1)}) fusion(bf16[2,4,1,256,128]{4,3,2,1,0:T(8,128)(2,1)} %collective-permute-done.12, f32[2,4,8,256,128]{4,3,2,1,0:T(8,128)} %bitcast.44, s32[]{:T(128)S(6)} %select_n.55, bf16[2,4,1,256,128]{4,3,2,1,0:T(8,128)(2,1)S(1)} %collective-permute-done.11, ...), kind=kLoop, calls=%fused_computation.7 | loop fusion | flops 1572864 | bytes 4194312 | tf_op jit(solution)/shard_map/convert_element_type | solution.py:37
  104.3 3.1 %collective-permute-start.17 = (bf16[2,4,1,256,128]{4,3,2,1,0:T(8,128)(2,1)}, bf16[2,4,1,256,128]{4,3,2,1,0:T(8,128)(2,1)}, u32[]{:S(2)}, u32[]{:S(2)}) collective-permute-start(bf16[2,4,1,256,128]{4,3,2,1,0:T(8,128)(2,1)} %get-tuple-element.87), channel_id=1, source_target_pairs={{0,7},{1,0},{2,1},{3,2},{4,3},{5,4},{6,5},{7,6},{8,15},{9,8},{10,9... | collective-permute-start | bytes 1572872 | tf_op jit(solution)/shard_map/ppermute | solution.py:23
  111.2 14.1 %all-to-all-done = bf16[16,256,128]{2,1,0:T(8,128)(2,1)} async-done(((bf16[16,256,128]{2,1,0:T(8,128)(2,1)}), bf16[16,256,128]{2,1,0:T(8,128)(2,1)}, u32[]{:S(2)}, u32[]{:S(2)}) %all-to-all-start) | async-done | bytes 1048608 | tf_op jit(solution)/shard_map/all_to_all | solution.py:41
  127.3 9.1 %collective-permute-done.19 = bf16[256,512]{1,0:T(8,128)(2,1)} collective-permute-done((bf16[256,512]{1,0:T(8,128)(2,1)}, bf16[256,512]{1,0:T(8,128)(2,1)}, u32[]{:S(2)}, u32[]{:S(2)}) %collective-permute-start.19) | collective-permute-done | bytes 262176 | tf_op jit(solution)/shard_map/ppermute | solution.py:23
  143.2 5.8 %all-to-all-start.1 = ((bf16[8,256,128]{2,1,0:T(8,128)(2,1)}), bf16[8,256,128]{2,1,0:T(8,128)(2,1)}, u32[]{:S(2)}, u32[]{:S(2)}) async-start(bf16[8,256,128]{2,1,0:T(8,128)(2,1)} %bitcast.49), calls=%async_computation.1 | async-start | bytes 1048576 | tf_op jit(solution)/shard_map/all_to_all | solution.py:41
  150.7 8.8 %collective-permute-done.24 = f32[128,512]{1,0:T(8,128)S(1)} collective-permute-done((f32[128,512]{1,0:T(8,128)S(1)}, f32[128,512]{1,0:T(8,128)S(1)}, u32[]{:S(2)}, u32[]{:S(2)}) %collective-permute-start.24) | collective-permute-done | bytes 262176 | tf_op jit(solution)/shard_map/ppermute | solution.py:258
  160.2 8.3 %all-to-all-done.1 = bf16[8,256,128]{2,1,0:T(8,128)(2,1)} async-done(((bf16[8,256,128]{2,1,0:T(8,128)(2,1)}), bf16[8,256,128]{2,1,0:T(8,128)(2,1)}, u32[]{:S(2)}, u32[]{:S(2)}) %all-to-all-start.1) | async-done | bytes 524320 | tf_op jit(solution)/shard_map/all_to_all | solution.py:41
  181.2 11.6 %collective-permute-done.26.refs_5_ = bf16[1024,512]{1,0:T(8,128)(2,1)} collective-permute-done((bf16[1024,512]{1,0:T(8,128)(2,1)}, bf16[1024,512]{1,0:T(8,128)(2,1)}, u32[]{:S(2)}, u32[]{:S(2)}) %collective-permute-start.26) | collective-permute-done | bytes 1048608 | tf_op jit(solution)/shard_map/ppermute | solution.py:23
  193.4 12.5 %all-to-all-start.2 = ((f32[64,1,128]{2,1,0:T(1,128)}), f32[64,1,128]{2,1,0:T(1,128)S(1)}, u32[]{:S(2)}, u32[]{:S(2)}) async-start(f32[64,1,128]{2,1,0:T(1,128)} %broadcast_in_dim.16), calls=%async_computation.2 | async-start | bytes 65536 | tf_op jit(solution)/shard_map/all_to_all | solution.py:270
  209.1 13.8 %tail.1 = (bf16[256,512]{1,0:T(8,128)(2,1)}, bf16[256,8192]{1,0:T(8,128)(2,1)}) custom-call(s32[3]{0:T(128)S(1)} %pad_add_fusion.place, bf16[256,8192]{1,0:T(8,128)(2,1)S(1)} %bitcast.38, f32[1,8192]{1,0:T(1,128)S(1)} %copy-done, bf16[256,512]{1,0:T(8,128)(2,1)S(1)} %bitcast.40, f32[256,128]{1,0:T(8,128)S(1)} %copy-done.3, ...), custom_call_target="tpu_custom_call" | custom-call | flops 4294967296 | bytes 18874368 | tf_op jit(solution)/shard_map/tail/pallas_call | solution.py:157
  (83 shorter events, 58.2 us)
Async XLA Ops:
  2.4 13.9 %collective-permute-start.1 = (f32[128,512]{1,0:T(8,128)S(1)}, f32[128,512]{1,0:T(8,128)S(1)}, u32[]{:S(2)}, u32[]{:S(2)}) collective-permute-start(f32[128,512]{1,0:T(8,128)S(1)} %bitcast_subtract_fusion), channel_id=1, source_target_pairs={{0,64},{64,0},{1,65},{65,1},{2,66},{66,2},{3,67},{67,3},{4,68},{68... | collective-permute-start | bytes 786440 | tf_op jit(solution)/shard_map/ppermute | solution.py:216
  18.9 23.1 %collective-permute-start.2 = (bf16[2,4,1,256,128]{4,3,2,1,0:T(8,128)(2,1)S(1)}, bf16[2,4,1,256,128]{4,3,2,1,0:T(8,128)(2,1)S(1)}, u32[]{:S(2)}, u32[]{:S(2)}) collective-permute-start(bf16[2,4,1,256,128]{4,3,2,1,0:T(8,128)(2,1)S(1)} %get-tuple-element.93), channel_id=1, source_target_pairs={{0,7},{1,0},{2,1},{3,2},{4,3},{5,4},{6,5},{7,6},{8,15},{9,8},{10,9... | collective-permute-start | bytes 1572872 | tf_op jit(solution)/shard_map/ppermute | solution.py:23
  26.6 15.3 %collective-permute-start.5 = (bf16[2,1,8,128,128]{4,3,2,1,0:T(8,128)(2,1)S(1)}, bf16[2,1,8,128,128]{4,3,2,1,0:T(8,128)(2,1)}, u32[]{:S(2)}, u32[]{:S(2)}) collective-permute-start(bf16[2,1,8,128,128]{4,3,2,1,0:T(8,128)(2,1)S(1)} %get-tuple-element.95), channel_id=1, source_target_pairs={{0,24},{8,0},{16,8},{24,16},{1,25},{9,1},{17,9},{25,17},{2,26},{10... | collective-permute-start | bytes 1572872 | tf_op jit(solution)/shard_map/ppermute | solution.py:23
  29.7 14.7 %collective-permute-start.6 = (bf16[2,1,8,128,128]{4,3,2,1,0:T(8,128)(2,1)S(1)}, bf16[2,1,8,128,128]{4,3,2,1,0:T(8,128)(2,1)}, u32[]{:S(2)}, u32[]{:S(2)}) collective-permute-start(bf16[2,1,8,128,128]{4,3,2,1,0:T(8,128)(2,1)S(1)} %get-tuple-element.94), channel_id=1, source_target_pairs={{0,8},{8,16},{16,24},{24,0},{1,9},{9,17},{17,25},{25,1},{2,10},{10... | collective-permute-start | bytes 1572872 | tf_op jit(solution)/shard_map/ppermute | solution.py:23
  39.7 17.1 %collective-permute-start.8 = (bf16[2,4,1,256,128]{4,3,2,1,0:T(8,128)(2,1)}, bf16[2,4,1,256,128]{4,3,2,1,0:T(8,128)(2,1)S(1)}, u32[]{:S(2)}, u32[]{:S(2)}) collective-permute-start(bf16[2,4,1,256,128]{4,3,2,1,0:T(8,128)(2,1)} %get-tuple-element.92), channel_id=1, source_target_pairs={{0,1},{1,2},{2,3},{3,4},{4,5},{5,6},{6,7},{7,0},{8,9},{9,10},{10,1... | collective-permute-start | bytes 1572872 | tf_op jit(solution)/shard_map/ppermute | solution.py:23
  46.6 18.5 %collective-permute-start.7 = (bf16[2,4,1,256,128]{4,3,2,1,0:T(8,128)(2,1)}, bf16[2,4,1,256,128]{4,3,2,1,0:T(8,128)(2,1)}, u32[]{:S(2)}, u32[]{:S(2)}) collective-permute-start(bf16[2,4,1,256,128]{4,3,2,1,0:T(8,128)(2,1)} %add_convert_fusion.8), channel_id=1, source_target_pairs={{0,7},{1,0},{2,1},{3,2},{4,3},{5,4},{6,5},{7,6},{8,15},{9,8},{10,9... | collective-permute-start | bytes 1572872 | tf_op jit(solution)/shard_map/ppermute | solution.py:23
  47.8 17.2 %collective-permute-start.10 = (bf16[256,512]{1,0:T(8,128)(2,1)}, bf16[256,512]{1,0:T(8,128)(2,1)}, u32[]{:S(2)}, u32[]{:S(2)}) collective-permute-start(bf16[256,512]{1,0:T(8,128)(2,1)} %collective-permute-done.4), channel_id=1, source_target_pairs={{0,7},{1,0},{2,1},{3,2},{4,3},{5,4},{6,5},{7,6},{8,15},{9,8},{10,9... | collective-permute-start | bytes 786440 | tf_op jit(solution)/shard_map/ppermute | solution.py:23
  48.6 16.4 %collective-permute-start.9 = (bf16[256,512]{1,0:T(8,128)(2,1)S(1)}, bf16[256,512]{1,0:T(8,128)(2,1)}, u32[]{:S(2)}, u32[]{:S(2)}) collective-permute-start(bf16[256,512]{1,0:T(8,128)(2,1)S(1)} %collective-permute-done.3), channel_id=1, source_target_pairs={{0,1},{1,2},{2,3},{3,4},{4,5},{5,6},{6,7},{7,0},{8,9},{9,10},{10,1... | collective-permute-start | bytes 786440 | tf_op jit(solution)/shard_map/ppermute | solution.py:23
  53.7 33.0 %collective-permute-start.15 = (bf16[2,1,8,256,128]{4,3,2,1,0:T(8,128)(2,1)}, bf16[2,1,8,256,128]{4,3,2,1,0:T(8,128)(2,1)S(1)}, u32[]{:S(2)}, u32[]{:S(2)}) collective-permute-start(bf16[2,1,8,256,128]{4,3,2,1,0:T(8,128)(2,1)} %get-tuple-element.89), channel_id=1, source_target_pairs={{0,24},{8,0},{16,8},{24,16},{1,25},{9,1},{17,9},{25,17},{2,26},{10... | collective-permute-start | bytes 3145736 | tf_op jit(solution)/shard_map/ppermute | solution.py:23
  56.7 30.0 %collective-permute-start.16 = (bf16[2,1,8,256,128]{4,3,2,1,0:T(8,128)(2,1)S(1)}, bf16[2,1,8,256,128]{4,3,2,1,0:T(8,128)(2,1)}, u32[]{:S(2)}, u32[]{:S(2)}) collective-permute-start(bf16[2,1,8,256,128]{4,3,2,1,0:T(8,128)(2,1)S(1)} %get-tuple-element.88), channel_id=1, source_target_pairs={{0,8},{8,16},{16,24},{24,0},{1,9},{9,17},{17,25},{25,1},{2,10},{10... | collective-permute-start | bytes 3145736 | tf_op jit(solution)/shard_map/ppermute | solution.py:23
  68.0 18.7 %collective-permute-start.11 = (bf16[2,4,1,256,128]{4,3,2,1,0:T(8,128)(2,1)}, bf16[2,4,1,256,128]{4,3,2,1,0:T(8,128)(2,1)S(1)}, u32[]{:S(2)}, u32[]{:S(2)}) collective-permute-start(bf16[2,4,1,256,128]{4,3,2,1,0:T(8,128)(2,1)} %get-tuple-element.91), channel_id=1, source_target_pairs={{0,7},{1,0},{2,1},{3,2},{4,3},{5,4},{6,5},{7,6},{8,15},{9,8},{10,9... | collective-permute-start | bytes 1572872 | tf_op jit(solution)/shard_map/ppermute | solution.py:23
  71.2 15.5 %collective-permute-start.12 = (bf16[2,4,1,256,128]{4,3,2,1,0:T(8,128)(2,1)}, bf16[2,4,1,256,128]{4,3,2,1,0:T(8,128)(2,1)}, u32[]{:S(2)}, u32[]{:S(2)}) collective-permute-start(bf16[2,4,1,256,128]{4,3,2,1,0:T(8,128)(2,1)} %get-tuple-element.90), channel_id=1, source_target_pairs={{0,1},{1,2},{2,3},{3,4},{4,5},{5,6},{6,7},{7,0},{8,9},{9,10},{10,1... | collective-permute-start | bytes 1572872 | tf_op jit(solution)/shard_map/ppermute | solution.py:23
  90.0 35.2 %all-to-all-start = ((bf16[16,256,128]{2,1,0:T(8,128)(2,1)}), bf16[16,256,128]{2,1,0:T(8,128)(2,1)}, u32[]{:S(2)}, u32[]{:S(2)}) async-start(bf16[16,256,128]{2,1,0:T(8,128)(2,1)} %bitcast.11), calls=%async_computation | async-start | bytes 2097152 | tf_op jit(solution)/shard_map/all_to_all | solution.py:41
  98.0 38.3 %collective-permute-start.20 = (bf16[1024,512]{1,0:T(8,128)(2,1)S(1)}, bf16[1024,512]{1,0:T(8,128)(2,1)S(1)}, u32[]{:S(2)}, u32[]{:S(2)}) collective-permute-start(bf16[1024,512]{1,0:T(8,128)(2,1)S(1)} %constant_dynamic-update-slice_fusion.refs_0_), channel_id=1, source_target_pairs={{0,8},{8,16},{16,24},{24,0},{1,9},{9,17},{17,25},{25,1},{2,10},{10... | collective-permute-start | bytes 3145736 | tf_op jit(solution)/shard_map/ppermute | solution.py:23
  99.7 36.7 %collective-permute-start.21 = (bf16[1024,512]{1,0:T(8,128)(2,1)S(1)}, bf16[1024,512]{1,0:T(8,128)(2,1)}, u32[]{:S(2)}, u32[]{:S(2)}) collective-permute-start(bf16[1024,512]{1,0:T(8,128)(2,1)S(1)} %constant_dynamic-update-slice_fusion.refs_0_), channel_id=1, source_target_pairs={{0,24},{8,0},{16,8},{24,16},{1,25},{9,1},{17,9},{25,17},{2,26},{10... | collective-permute-start | bytes 3145736 | tf_op jit(solution)/shard_map/ppermute | solution.py:23
  104.3 32.1 %collective-permute-start.17 = (bf16[2,4,1,256,128]{4,3,2,1,0:T(8,128)(2,1)}, bf16[2,4,1,256,128]{4,3,2,1,0:T(8,128)(2,1)}, u32[]{:S(2)}, u32[]{:S(2)}) collective-permute-start(bf16[2,4,1,256,128]{4,3,2,1,0:T(8,128)(2,1)} %get-tuple-element.87), channel_id=1, source_target_pairs={{0,7},{1,0},{2,1},{3,2},{4,3},{5,4},{6,5},{7,6},{8,15},{9,8},{10,9... | collective-permute-start | bytes 1572872 | tf_op jit(solution)/shard_map/ppermute | solution.py:23
  107.4 29.0 %collective-permute-start.18 = (bf16[2,4,1,256,128]{4,3,2,1,0:T(8,128)(2,1)}, bf16[2,4,1,256,128]{4,3,2,1,0:T(8,128)(2,1)}, u32[]{:S(2)}, u32[]{:S(2)}) collective-permute-start(bf16[2,4,1,256,128]{4,3,2,1,0:T(8,128)(2,1)} %get-tuple-element.86), channel_id=1, source_target_pairs={{0,1},{1,2},{2,3},{3,4},{4,5},{5,6},{6,7},{7,0},{8,9},{9,10},{10,1... | collective-permute-start | bytes 1572872 | tf_op jit(solution)/shard_map/ppermute | solution.py:23
  108.3 28.0 %collective-permute-start.19 = (bf16[256,512]{1,0:T(8,128)(2,1)}, bf16[256,512]{1,0:T(8,128)(2,1)}, u32[]{:S(2)}, u32[]{:S(2)}) collective-permute-start(bf16[256,512]{1,0:T(8,128)(2,1)} %collective-permute-done.13), channel_id=1, source_target_pairs={{0,1},{1,2},{2,3},{3,4},{4,5},{5,6},{6,7},{7,0},{8,9},{9,10},{10,1... | collective-permute-start | bytes 786440 | tf_op jit(solution)/shard_map/ppermute | solution.py:23
  137.3 33.0 %collective-permute-start.22 = (bf16[1024,512]{1,0:T(8,128)(2,1)S(1)}, bf16[1024,512]{1,0:T(8,128)(2,1)}, u32[]{:S(2)}, u32[]{:S(2)}) collective-permute-start(bf16[1024,512]{1,0:T(8,128)(2,1)S(1)} %constant_dynamic-update-slice_fusion.5.refs_1_), channel_id=1, source_target_pairs={{0,8},{8,16},{16,24},{24,0},{1,9},{9,17},{17,25},{25,1},{2,10},{10... | collective-permute-start | bytes 3145736 | tf_op jit(solution)/shard_map/ppermute | solution.py:23
  139.1 31.2 %collective-permute-start.23 = (bf16[1024,512]{1,0:T(8,128)(2,1)S(1)}, bf16[1024,512]{1,0:T(8,128)(2,1)}, u32[]{:S(2)}, u32[]{:S(2)}) collective-permute-start(bf16[1024,512]{1,0:T(8,128)(2,1)S(1)} %constant_dynamic-update-slice_fusion.5.refs_1_), channel_id=1, source_target_pairs={{0,24},{8,0},{16,8},{24,16},{1,25},{9,1},{17,9},{25,17},{2,26},{10... | collective-permute-start | bytes 3145736 | tf_op jit(solution)/shard_map/ppermute | solution.py:23
  143.2 25.4 %all-to-all-start.1 = ((bf16[8,256,128]{2,1,0:T(8,128)(2,1)}), bf16[8,256,128]{2,1,0:T(8,128)(2,1)}, u32[]{:S(2)}, u32[]{:S(2)}) async-start(bf16[8,256,128]{2,1,0:T(8,128)(2,1)} %bitcast.49), calls=%async_computation.1 | async-start | bytes 1048576 | tf_op jit(solution)/shard_map/all_to_all | solution.py:41
  170.3 22.4 %collective-permute-start.26 = (bf16[1024,512]{1,0:T(8,128)(2,1)}, bf16[1024,512]{1,0:T(8,128)(2,1)}, u32[]{:S(2)}, u32[]{:S(2)}) collective-permute-start(bf16[1024,512]{1,0:T(8,128)(2,1)} %collective-permute-done.23.refs_7_), channel_id=1, source_target_pairs={{0,24},{8,0},{16,8},{24,16},{1,25},{9,1},{17,9},{25,17},{2,26},{10... | collective-permute-start | bytes 3145736 | tf_op jit(solution)/shard_map/ppermute | solution.py:23
  172.9 33.0 %collective-permute-start.25 = (bf16[1024,512]{1,0:T(8,128)(2,1)S(1)}, bf16[1024,512]{1,0:T(8,128)(2,1)}, u32[]{:S(2)}, u32[]{:S(2)}) collective-permute-start(bf16[1024,512]{1,0:T(8,128)(2,1)S(1)} %collective-permute-done.20.refs_2_), channel_id=1, source_target_pairs={{0,8},{8,16},{16,24},{24,0},{1,9},{9,17},{17,25},{25,1},{2,10},{10... | collective-permute-start | bytes 3145736 | tf_op jit(solution)/shard_map/ppermute | solution.py:23
  193.4 29.5 %all-to-all-start.2 = ((f32[64,1,128]{2,1,0:T(1,128)}), f32[64,1,128]{2,1,0:T(1,128)S(1)}, u32[]{:S(2)}, u32[]{:S(2)}) async-start(f32[64,1,128]{2,1,0:T(1,128)} %broadcast_in_dim.16), calls=%async_computation.2 | async-start | bytes 65536 | tf_op jit(solution)/shard_map/all_to_all | solution.py:270
  (12 other events, 176.0 us)

commit v3 on v2

--- a/solution.py
+++ b/solution.py
@@ -14,8 +14,7 @@
 BF16 = jnp.bfloat16
 F32 = jnp.float32
 LANES = 128
-FIRST = (0, 1, 7, 2)
-SECOND = (6, 3, 5, 4)
+ORDER = (0, 1, 7, 2, 6, 3, 5, 4)
 
 
 def shift(value, axis, step):
@@ -32,9 +31,9 @@
     return lax.dynamic_slice_in_dim(part, at, 1, dim)
 
 
-def onward(part, axis, dim, step, received):
-    total = term(part, axis, dim, step) + received.astype(F32)
-    return shift(total.astype(BF16), axis, 1 if step > 0 else -1)
+def added(part, axis, dim, step, received):
+    mine = term(part, axis, dim, step).reshape(received.shape)
+    return (mine.astype(F32) + received.astype(F32)).astype(BF16)
 
 
 def exchange_sum(part, axes):
@@ -69,8 +68,8 @@
         both = jnp.dot(turned[...], scaled, preferred_element_type=F32)
         for i in range(2):
             lanes = slice(i * LANES, (i + 1) * LANES)
-            a_out[j + i] = both[:cut, lanes]
-            b_out[j + i] = both[cut:, lanes]
+            a_out[j + i] = both[:cut, lanes].astype(BF16)
+            b_out[j + i] = both[cut:, lanes].astype(BF16)
 
 
 def weight_grad(hidden, gain, cotangent):
@@ -78,7 +77,7 @@
     keys = cotangent.shape[1]
     blocks, per_step, cut = width // LANES, 8, keys // 2
     whole = lambda i: (0, 0)
-    part = jax.ShapeDtypeStruct((blocks, cut, LANES), F32)
+    part = jax.ShapeDtypeStruct((blocks, cut, LANES), BF16)
     return pl.pallas_call(
         weight_grad_kernel,
         grid=(blocks // per_step,),
@@ -107,22 +106,32 @@
     key_out, grad_hidden, held, grad, keys, dots, sems = refs[count:]
     tokens, width = hidden.shape
     x, y, z = place[0], place[1], place[2]
+    split = weights[0].shape[1]
+    places = (pl.ds(0, split), pl.ds(split, weights[1].shape[1]))
     for i, ref in enumerate(weights):
-        pltpu.make_async_copy(ref, held.at[i], sems.at[i]).start()
+        for group in range(ref.shape[0]):
+            lanes = pl.ds(group * LANES, LANES)
+            there = held.at[i // 2, places[i % 2], lanes]
+            pltpu.make_async_copy(ref.at[group], there, sems.at[i // 2]).start()
     keys[...] = jnp.zeros_like(keys)
     dots[...] = jnp.zeros_like(dots)
 
     def block(i, carry):
-        pltpu.make_async_copy(held.at[i], held.at[i], sems.at[i]).wait()
-        rows = held[i]
+        yr, half = i // 2, i % 2
+
+        @pl.when(half == 0)
+        def _():
+            pltpu.make_async_copy(held.at[yr], held.at[yr], sems.at[yr]).wait()
+
+        rows = held[yr, pl.ds(pl.multiple_of(half * 1024, 1024), 1024), :]
         grads = lax.dot_general(
             cotangent[...], rows, (((1,), (1,)), ((), ())), preferred_element_type=F32
         )
         scaled = []
         total = dots[...]
         for j in range(8):
-            zr = jnp.where(i % 2 == 0, FIRST[j // 2], SECOND[j // 2])
-            feature = (x ^ (j % 2)) * 32 + ((y - i // 2) & 3) * 8 + ((z - zr) & 7)
+            zr = jnp.where(half == 0, ORDER[j // 2], ORDER[4 + j // 2])
+            feature = (x ^ (j % 2)) * 32 + ((y - yr) & 3) * 8 + ((z - zr) & 7)
             at = pl.ds(pl.multiple_of(feature * LANES, LANES), LANES)
             normed = hidden[:, at].astype(F32) * inverse[...]
             weighted = grads[:, j * LANES : (j + 1) * LANES] * gain[:, at]
@@ -165,11 +174,11 @@
         + [pl.BlockSpec(memory_space=pl.ANY)] * count,
         out_specs=(vmem, vmem),
         scratch_shapes=[
-            pltpu.VMEM((count, width // count, keys), BF16),
+            pltpu.VMEM((count // 2, 2 * width // count, keys), BF16),
             pltpu.VMEM((tokens, width), F32),
             pltpu.VMEM((tokens, keys), F32),
             pltpu.VMEM((tokens, LANES), F32),
-            pltpu.SemaphoreType.DMA((count,)),
+            pltpu.SemaphoreType.DMA((count // 2,)),
         ],
         compiler_params=pltpu.CompilerParams(vmem_limit_bytes=40 * 1024 * 1024),
         cost_estimate=pl.CostEstimate(
@@ -212,51 +221,57 @@
     half = cut // 2
 
     mine = current - inner_now
-    over_x = shift(own, "xh", 1)
+    slabs = own.reshape(rows, -1, LANES).transpose(1, 0, 2)
+    over_x = shift(slabs, "xh", 1)
     core = lax.ppermute(mine, "core", [(0, 1), (1, 0)])
     over_x, part_a, part_b, inverse, core = together(over_x, part_a, part_b, inverse, core)
-    pair = jnp.concatenate([own, over_x])
-
-    far_a = term(part_a, "z", 2, -4).astype(BF16)
-    far_b = term(part_b, "y", 1, 2).astype(BF16)
-    a_left = shift(far_a, "z", -1)
-    z1, z7 = shift(pair, "z", 1), shift(pair, "z", -1)
+    pair = jnp.concatenate([slabs, over_x], axis=1)
+
+    sums = groups[0] * groups[1]
+
+    def along_z(total, slab, step):
+        moved = shift(jnp.concatenate([total.reshape(sums, cut, rows), slab]), "z", step)
+        return moved[:sums], moved[sums:]
+
+    far_b = term(part_b, "y", 1, 2)
+    left, z7 = along_z(term(part_a, "z", 2, -4), pair, -1)
+    right, z1 = along_z(term(part_a, "z", 2, 3), pair, 1)
     b_left = shift(far_b[..., half:, :], "y", -1)
     b_right = shift(far_b[..., :half, :], "y", 1)
-    a_left, z1, z7, b_left, b_right = together(a_left, z1, z7, b_left, b_right)
-
-    a_left = onward(part_a, "z", 2, -3, a_left)
-    a_right = shift(term(part_a, "z", 2, 3).astype(BF16), "z", 1)
-    z2, z6 = shift(z1, "z", 1), shift(z7, "z", -1)
+    left, z7, right, z1, b_left, b_right = together(left, z7, right, z1, b_left, b_right)
+
+    left, z6 = along_z(added(part_a, "z", 2, -3, left), z7, -1)
+    right, z2 = along_z(added(part_a, "z", 2, 2, right), z1, 1)
     none = jnp.zeros_like(b_left)
-    b_left = onward(part_b, "y", 1, -1, jnp.concatenate([none, b_left], axis=3))
-    b_right = onward(part_b, "y", 1, 1, jnp.concatenate([b_right, none], axis=3))
-    a_left, a_right, z2, z6 = together(a_left, a_right, z2, z6)
-
-    a_left = onward(part_a, "z", 2, -2, a_left)
-    a_right = onward(part_a, "z", 2, 2, a_right)
-    z3, z5 = shift(z2, "z", 1), shift(z6, "z", -1)
-    first = jnp.concatenate([pair, z1, z7, z2])
+    b_left = shift(
+        added(part_b, "y", 1, -1, jnp.concatenate([none, b_left], axis=3)), "y", -1
+    )
+    b_right = shift(
+        added(part_b, "y", 1, 1, jnp.concatenate([b_right, none], axis=3)), "y", 1
+    )
+    left, z6, right, z2 = together(left, z6, right, z2)
+
+    left, z5 = along_z(added(part_a, "z", 2, -2, left), z6, -1)
+    right, z3 = along_z(added(part_a, "z", 2, 1, right), z2, 1)
+    first = jnp.concatenate([pair, z1, z7, z2, z6], axis=1)
     first1, first3 = shift(first, "y", 1), shift(first, "y", -1)
-    a_left, a_right, z3, z5, b_left, b_right = together(a_left, a_right, z3, z5, b_left, b_right)
-
-    sum_b = term(part_b, "y", 1, 0) + b_left.astype(F32) + b_right.astype(F32)
+    left, z5, right, z3, b_left, b_right = together(left, z5, right, z3, b_left, b_right)
+
+    sum_b = term(part_b, "y", 1, 0).astype(F32) + b_left.astype(F32) + b_right.astype(F32)
     sum_b = exchange_sum(sum_b.reshape(-1, cut, rows), ("xh", "z"))
-    a_left = onward(part_a, "z", 2, -1, a_left)
-    a_right = onward(part_a, "z", 2, 1, a_right)
+    left = shift(added(part_a, "z", 2, -1, left), "z", -1)
     z4 = shift(z3, "z", 1)
-    a_left, a_right, z4, first1, first3, sum_b, core = together(
-        a_left, a_right, z4, first1, first3, sum_b, core
-    )
-
-    sum_a = term(part_a, "z", 2, 0) + a_left.astype(F32) + a_right.astype(F32)
+    left, right, z4, first1, first3, core = together(left, right, z4, first1, first3, core)
+
+    sum_a = term(part_a, "z", 2, 0).reshape(left.shape).astype(F32)
+    sum_a = sum_a + left.astype(F32) + right.astype(F32)
     sum_a = exchange_sum(sum_a.reshape(-1, cut, rows), ("xh", "y"))
-    second = jnp.concatenate([z6, z3, z5, z4])
+    second = jnp.concatenate([z3, z5, z4], axis=1)
     second1, second3 = shift(second, "y", 1), shift(second, "y", -1)
     first2 = shift(first1, "y", 1)
     both = mine + core
     summed = both + lax.ppermute(both, "xl", [(0, 1), (1, 0)])
-    sum_a, second1, second3, summed = together(sum_a, second1, second3, summed)
+    sum_a, sum_b, second1, second3, summed = together(sum_a, sum_b, second1, second3, summed)
     second2 = shift(second3, "y", -1)
     weights = [first, second, first1, second1, first2, second2, first3, second3]
 
@@ -266,7 +281,6 @@
     own_gain = lax.dynamic_slice_in_dim(norm_gain[0], me * rows, rows)
     own_sum = jnp.sum(own.astype(F32) * grad_weight, axis=-1) / own_gain
     place = jnp.stack([lax.axis_index(axis) for axis in GROUP])
-    own_sum, weights[-1], weights[-3] = together(own_sum, weights[-1], weights[-3])
     grad_gain = lax.all_to_all(
         jnp.broadcast_to(own_sum[None], (devices, rows)), GROUP, 0, 0, tiled=True
     ).reshape(-1)

time: 226 us -> 221 us (0.978)
  local copies, waits for them, and re-layouts: 18.1 us -> 30.6 us
  starting transfers between devices: 65 us -> 54.7 us
  other arithmetic: 30 us -> 23.4 us
    all_to_all x2, waiting for transfers between devices: 22.4 us -> 10.9 us  [exchange_sum(): blocks = lax.all_to_all(part.astype(BF16), axes, 0, 0, tiled=True)]
    convert_element_type x4 -> x6, other arithmetic: 11.9 us -> 3.08 us  [added(): return (mine.astype(F32) + received.astype(F32)).astype(BF16)]
    unnamed x20 -> x50, local copies, waits for them, and re-layouts: 7.67 us -> 16 us
    ppermute x25 -> x19, waiting for transfers between devices: 52.4 us -> 60.5 us  [shift(): return lax.ppermute(value, axis, [(i, (i + step) % n) for i in range(n)])]
    slice x0 -> x12, local copies, waits for them, and re-layouts: none -> 7.95 us  [along_z(): return (moved[:sums], moved[sums:])]
    ppermute x25 -> x19, starting transfers between devices: 40 us -> 33 us  [shift(): return lax.ppermute(value, axis, [(i, (i + step) % n) for i in range(n)])]
    all_to_all x1, waiting for transfers between devices: 0.01 us -> 6.42 us  [per_device(): lax.all_to_all(jnp.broadcast_to(own_sum[None], (devices, rows)), GROUP, 0...]
    convert_element_type x2 -> x0, local copies, waits for them, and re-layouts: 4.39 us -> none  [the longest x1 2.62 us: per_device(): a_right = shift(term(part_a, 'z', 2, 3).astype(BF16), 'z', 1)]
  transfers between devices with their start and end apart: 30 -> 24, of which waited for: 11 -> 12; matrix products, arithmetic and copies ran while one was open for 16% -> 16% of each run, Pallas kernels for 11% -> 5%
where the time goes in v3:
time: 221 us; the launch traced here: 220 us
  waiting for transfers between devices  84.8 us (38%)
  starting transfers between devices  54.7 us (25%)
  local copies, waits for them, and re-layouts  30.6 us (14%)
  Pallas kernels  24.5 us (11%)
  other arithmetic  23.4 us (11%)
    ppermute x19, waiting for transfers between devices, shift(): return lax.ppermute(value, axis, [(i, (i + step) % n) for i in range(n)])  60.5 us
    ppermute x19, starting transfers between devices, shift(): return lax.ppermute(value, axis, [(i, (i + step) % n) for i in range(n)])  33 us
    unnamed x50, local copies, waits for them, and re-layouts  16 us
    pallas_call x1, Pallas kernels, tail(): pl.pallas_call(functools.partial(tail_kernel, count), out_shape=(jax.Shap...  14.4 us
    all_to_all x2, starting transfers between devices, exchange_sum(): blocks = lax.all_to_all(part.astype(BF16), axes, 0, 0, tiled=True)  11.1 us
    all_to_all x2, waiting for transfers between devices, exchange_sum(): blocks = lax.all_to_all(part.astype(BF16), axes, 0, 0, tiled=True)  10.9 us
    pallas_call x1, Pallas kernels, weight_grad(): pl.pallas_call(weight_grad_kernel, grid=(blocks // per_step,), out_shape=...  10.1 us
    all_to_all x1, starting transfers between devices, per_device(): lax.all_to_all(jnp.broadcast_to(own_sum[None], (devices, rows)), GROUP, 0...  9.89 us
  transfers between devices with their start and end apart: 24, of which 12 were waited for; matrix products, arithmetic and copies ran while one was open for 16% of the time, Pallas kernels for 5%

profile of v3, /device:TPU:2, one launch (start us, length us, event | category | flops | bytes accessed | tf_op | source)
XLA Modules:
  0.0 219.7 jit_solution(9194359270715839782)
XLA Ops:
  5.9 10.1 %weight_grad.1 = (bf16[64,256,128]{2,1,0:T(8,128)(2,1)}, bf16[64,256,128]{2,1,0:T(8,128)(2,1)}, f32[256,128]{1,0:T(8,128)}) custom-call(bf16[256,8192]{1,0:T(8,128)(2,1)} %bitcast.61, f32[1,8192]{1,0:T(1,128)} %gain.3, bf16[256,512]{1,0:T(8,128)(2,1)} %bitcast.63), custom_call_target="tpu_custom_call" | custom-call | flops 2147483648 | bytes 23068672 | tf_op jit(solution)/shard_map/weight_grad/pallas_call | solution.py:81
  16.7 3.5 %constant_dynamic-slice_fusion.2 = (bf16[2,4,1,256,128]{4,3,1,0,2:T(8,128)(2,1)}, bf16[2,4,1,256,128]{4,3,1,0,2:T(8,128)(2,1)S(1)}, bf16[2,4,1,256,128]{4,3,1,0,...) fusion(s32[]{:T(128)S(6)} %select_n.56, ...), kind=kLoop, calls=%fused_computation.43 | loop fusion | bytes 8388640 | tf_op jit(solution)/shard_map/dynamic_slice | solution.py:31
  21.6 5.9 %collective-permute-start.2 = (bf16[12,256,128]{2,1,0:T(8,128)(2,1)}, bf16[12,256,128]{2,1,0:T(8,128)(2,1)S(1)}, u32[]{:S(2)}, u32[]{:S(2)}) collective-permute-start(bf16[12,256,128]{2,1,0:T(8,128)(2,1)} %get-tuple-element.101), channel_id=1, source_target_pairs={{0,7},{1,0},{2,1},{3,2},{4,3},{5,4},{6,5},{7,6},{8,15},{9,8},{10,9... | collective-permute-start | bytes 2359304 | tf_op jit(solution)/shard_map/ppermute | solution.py:22
  28.7 3.1 %collective-permute-start.4 = (bf16[2,1,8,128,128]{4,3,2,1,0:T(8,128)(2,1)S(1)}, bf16[2,1,8,128,128]{4,3,2,1,0:T(8,128)(2,1)S(1)}, u32[]{:S(2)}, u32[]{:S(2)}) collective-permute-start(bf16[2,1,8,128,128]{4,3,2,1,0:T(8,128)(2,1)S(1)} %get-tuple-element.99), channel_id=1, source_target_pairs={{0,24},{8,0},{16,8},{24,16},{1,25},{9,1},{17,9},{25,17},{2,26},{10... | collective-permute-start | bytes 1572872 | tf_op jit(solution)/shard_map/ppermute | solution.py:22
  31.8 13.1 %collective-permute-done.2 = bf16[12,256,128]{2,1,0:T(8,128)(2,1)S(1)} collective-permute-done((bf16[12,256,128]{2,1,0:T(8,128)(2,1)}, bf16[12,256,128]{2,1,0:T(8,128)(2,1)S(1)}, u32[]{:S(2)}, u32[]{:S(2)}) %collective-permute-start.2) | collective-permute-done | bytes 786464 | tf_op jit(solution)/shard_map/ppermute | solution.py:22
  54.3 3.2 %collective-permute-start.6 = (bf16[12,256,128]{2,1,0:T(8,128)(2,1)}, bf16[12,256,128]{2,1,0:T(8,128)(2,1)}, u32[]{:S(2)}, u32[]{:S(2)}) collective-permute-start(bf16[12,256,128]{2,1,0:T(8,128)(2,1)} %pad_maximum_fusion.3), channel_id=1, source_target_pairs={{0,7},{1,0},{2,1},{3,2},{4,3},{5,4},{6,5},{7,6},{8,15},{9,8},{10,9... | collective-permute-start | bytes 2359304 | tf_op jit(solution)/shard_map/ppermute | solution.py:22
  59.8 3.1 %collective-permute-start.10 = (bf16[2,1,8,256,128]{4,3,2,1,0:T(8,128)(2,1)S(1)}, bf16[2,1,8,256,128]{4,3,2,1,0:T(8,128)(2,1)S(1)}, u32[]{:S(2)}, u32[]{:S(2)}) collective-permute-start(bf16[2,1,8,256,128]{4,3,2,1,0:T(8,128)(2,1)S(1)} %get-tuple-element.97), channel_id=1, source_target_pairs={{0,24},{8,0},{16,8},{24,16},{1,25},{9,1},{17,9},{25,17},{2,26},{10... | collective-permute-start | bytes 3145736 | tf_op jit(solution)/shard_map/ppermute | solution.py:22
  62.9 10.3 %collective-permute-done.7 = bf16[12,256,128]{2,1,0:T(8,128)(2,1)} collective-permute-done((bf16[12,256,128]{2,1,0:T(8,128)(2,1)}, bf16[12,256,128]{2,1,0:T(8,128)(2,1)}, u32[]{:S(2)}, u32[]{:S(2)}) %collective-permute-start.7) | collective-permute-done | bytes 786464 | tf_op jit(solution)/shard_map/ppermute | solution.py:22
  78.0 3.5 %collective-permute-start.8 = (bf16[12,256,128]{2,1,0:T(8,128)(2,1)S(1)}, bf16[12,256,128]{2,1,0:T(8,128)(2,1)S(1)}, u32[]{:S(2)}, u32[]{:S(2)}) collective-permute-start(bf16[12,256,128]{2,1,0:T(8,128)(2,1)S(1)} %pad_maximum_fusion.5), channel_id=1, source_target_pairs={{0,7},{1,0},{2,1},{3,2},{4,3},{5,4},{6,5},{7,6},{8,15},{9,8},{10,9... | collective-permute-start | bytes 2359304 | tf_op jit(solution)/shard_map/ppermute | solution.py:22
  83.3 13.2 %collective-permute-done.9 = bf16[12,256,128]{2,1,0:T(8,128)(2,1)S(1)} collective-permute-done((bf16[12,256,128]{2,1,0:T(8,128)(2,1)S(1)}, bf16[12,256,128]{2,1,0:T(8,128)(2,1)S(1)}, u32[]{:S(2)}, u32[]{:S(2)}) %collective-permute-start.9) | collective-permute-done | bytes 786464 | tf_op jit(solution)/shard_map/ppermute | solution.py:22
  96.5 3.0 %collective-permute-start.15 = (bf16[4,1280,128]{2,1,0:T(8,128)(2,1)S(1)}, bf16[4,1280,128]{2,1,0:T(8,128)(2,1)S(1)}, u32[]{:S(2)}, u32[]{:S(2)}) collective-permute-start(bf16[4,1280,128]{2,1,0:T(8,128)(2,1)S(1)} %constant_dynamic-update-slice_fusion.refs_0_), channel_id=1, source_target_pairs={{0,24},{8,0},{16,8},{24,16},{1,25},{9,1},{17,9},{25,17},{2,26},{10... | collective-permute-start | bytes 3932168 | tf_op jit(solution)/shard_map/ppermute | solution.py:22
  102.7 6.1 %collective-permute-done.13 = bf16[4,256,128]{2,1,0:T(8,128)(2,1)S(1)} collective-permute-done((bf16[4,256,128]{2,1,0:T(8,128)(2,1)S(1)}, bf16[4,256,128]{2,1,0:T(8,128)(2,1)S(1)}, u32[]{:S(2)}, u32[]{:S(2)}) %collective-permute-start.13) | collective-permute-done | bytes 262176 | tf_op jit(solution)/shard_map/ppermute | solution.py:22
  108.8 2.7 %collective-permute-done.12 = bf16[8,256,128]{2,1,0:T(8,128)(2,1)S(1)} collective-permute-done((bf16[8,256,128]{2,1,0:T(8,128)(2,1)S(1)}, bf16[8,256,128]{2,1,0:T(8,128)(2,1)S(1)}, u32[]{:S(2)}, u32[]{:S(2)}) %collective-permute-start.12) | collective-permute-done | bytes 524320 | tf_op jit(solution)/shard_map/ppermute | solution.py:22
  111.5 4.0 %collective-permute-done.14.refs_2_ = bf16[4,1280,128]{2,1,0:T(8,128)(2,1)S(1)} collective-permute-done((bf16[4,1280,128]{2,1,0:T(8,128)(2,1)S(1)}, bf16[4,1280,128]{2,1,0:T(8,128)(2,1)S(1)}, u32[]{:S(2)}, u32[]{:S(2)}) %collective-permute-start.14) | collective-permute-done | bytes 1310752 | tf_op jit(solution)/shard_map/ppermute | solution.py:22
  115.5 9.5 %collective-permute-done.15.refs_6_ = bf16[4,1280,128]{2,1,0:T(8,128)(2,1)S(1)} collective-permute-done((bf16[4,1280,128]{2,1,0:T(8,128)(2,1)S(1)}, bf16[4,1280,128]{2,1,0:T(8,128)(2,1)S(1)}, u32[]{:S(2)}, u32[]{:S(2)}) %collective-permute-start.15) | collective-permute-done | bytes 1310752 | tf_op jit(solution)/shard_map/ppermute | solution.py:22
  127.1 5.8 %all-to-all-start = ((bf16[8,256,128]{2,1,0:T(8,128)(2,1)}), bf16[8,256,128]{2,1,0:T(8,128)(2,1)S(1)}, u32[]{:S(2)}, u32[]{:S(2)}) async-start(bf16[8,256,128]{2,1,0:T(8,128)(2,1)} %fusion.1), calls=%async_computation | async-start | bytes 1048576 | tf_op jit(solution)/shard_map/all_to_all | solution.py:40
  132.9 3.3 %add_convert_fusion = bf16[2,1,8,256,128]{4,3,2,1,0:T(8,128)(2,1)} fusion(bf16[2,1,8,256,128]{4,3,2,1,0:T(8,128)(2,1)} %copy-done.12, bf16[2,1,8,256,128]{4,3,2,1,0:T(8,128)(2,1)} %copy-done.11, bf16[2,4,8,256,128]{4,3,2,1,0:T(8,128)(2,1)} %bitcast.68, s32[]{:T(128)S(6)} %select_n.57), kind=kLoop, calls=%fused_computation.1 | loop fusion | flops 3145728 | bytes 4194308 | tf_op jit(solution)/shard_map/convert_element_type | solution.py:40
  136.2 6.5 %all-to-all-done = bf16[8,256,128]{2,1,0:T(8,128)(2,1)S(1)} async-done(((bf16[8,256,128]{2,1,0:T(8,128)(2,1)}), bf16[8,256,128]{2,1,0:T(8,128)(2,1)S(1)}, u32[]{:S(2)}, u32[]{:S(2)}) %all-to-all-start) | async-done | bytes 524320 | tf_op jit(solution)/shard_map/all_to_all | solution.py:40
  143.5 5.3 %all-to-all-start.1 = ((bf16[16,256,128]{2,1,0:T(8,128)(2,1)}), bf16[16,256,128]{2,1,0:T(8,128)(2,1)}, u32[]{:S(2)}, u32[]{:S(2)}) async-start(bf16[16,256,128]{2,1,0:T(8,128)(2,1)} %bitcast.65), calls=%async_computation.1 | async-start | bytes 2097152 | tf_op jit(solution)/shard_map/all_to_all | solution.py:40
  157.5 7.0 %collective-permute-done.18 = f32[128,512]{1,0:T(8,128)} collective-permute-done((f32[128,512]{1,0:T(8,128)}, f32[128,512]{1,0:T(8,128)}, u32[]{:S(2)}, u32[]{:S(2)}) %collective-permute-start.18) | collective-permute-done | bytes 262176 | tf_op jit(solution)/shard_map/ppermute | solution.py:273
  168.0 4.5 %all-to-all-done.1 = bf16[16,256,128]{2,1,0:T(8,128)(2,1)} async-done(((bf16[16,256,128]{2,1,0:T(8,128)(2,1)}), bf16[16,256,128]{2,1,0:T(8,128)(2,1)}, u32[]{:S(2)}, u32[]{:S(2)}) %all-to-all-start.1) | async-done | bytes 1048608 | tf_op jit(solution)/shard_map/all_to_all | solution.py:40
  177.5 9.9 %all-to-all-start.2 = ((f32[64,1,128]{2,1,0:T(1,128)}), f32[64,1,128]{2,1,0:T(1,128)S(1)}, u32[]{:S(2)}, u32[]{:S(2)}) async-start(f32[64,1,128]{2,1,0:T(1,128)} %broadcast_in_dim.16), calls=%async_computation.2 | async-start | bytes 65536 | tf_op jit(solution)/shard_map/all_to_all | solution.py:284
  192.9 6.4 %all-to-all-done.2 = f32[64,1,128]{2,1,0:T(1,128)S(1)} async-done(((f32[64,1,128]{2,1,0:T(1,128)}), f32[64,1,128]{2,1,0:T(1,128)S(1)}, u32[]{:S(2)}, u32[]{:S(2)}) %all-to-all-start.2) | async-done | bytes 32800 | tf_op jit(solution)/shard_map/all_to_all | solution.py:284
  204.7 14.4 %tail.1 = (bf16[256,512]{1,0:T(8,128)(2,1)}, bf16[256,8192]{1,0:T(8,128)(2,1)}) custom-call(s32[3]{0:T(128)S(1)} %pad_add_fusion.place, bf16[256,8192]{1,0:T(8,128)(2,1)S(1)} %bitcast.62, f32[1,8192]{1,0:T(1,128)S(1)} %copy-done, bf16[256,512]{1,0:T(8,128)(2,1)S(1)} %bitcast.64, f32[256,128]{1,0:T(8,128)S(1)} %copy-done.5, ...), custom_call_target="tpu_custom_call" | custom-call | flops 4294967296 | bytes 18874368 | tf_op jit(solution)/shard_map/tail/pallas_call | solution.py:166
  (117 shorter events, 60.6 us)
Async XLA Ops:
  2.4 13.6 %collective-permute-start.1 = (f32[128,512]{1,0:T(8,128)S(1)}, f32[128,512]{1,0:T(8,128)S(1)}, u32[]{:S(2)}, u32[]{:S(2)}) collective-permute-start(f32[128,512]{1,0:T(8,128)S(1)} %bitcast_subtract_fusion), channel_id=1, source_target_pairs={{0,64},{64,0},{1,65},{65,1},{2,66},{66,2},{3,67},{67,3},{4,68},{68... | collective-permute-start | bytes 786440 | tf_op jit(solution)/shard_map/ppermute | solution.py:226
  3.6 12.3 %collective-permute-start = (bf16[4,128,128]{2,1,0:T(8,128)(2,1)S(1)}, bf16[4,128,128]{2,1,0:T(8,128)(2,1)S(1)}, u32[]{:S(2)}, u32[]{:S(2)}) collective-permute-start(bf16[4,128,128]{2,1,0:T(8,128)(2,1)S(1)} %bitcast.72), channel_id=1, source_target_pairs={{0,32},{32,0},{1,33},{33,1},{2,34},{34,2},{3,35},{35,3},{4,36},{36... | collective-permute-start | bytes 393224 | tf_op jit(solution)/shard_map/ppermute | solution.py:22
  21.6 23.4 %collective-permute-start.2 = (bf16[12,256,128]{2,1,0:T(8,128)(2,1)}, bf16[12,256,128]{2,1,0:T(8,128)(2,1)S(1)}, u32[]{:S(2)}, u32[]{:S(2)}) collective-permute-start(bf16[12,256,128]{2,1,0:T(8,128)(2,1)} %get-tuple-element.101), channel_id=1, source_target_pairs={{0,7},{1,0},{2,1},{3,2},{4,3},{5,4},{6,5},{7,6},{8,15},{9,8},{10,9... | collective-permute-start | bytes 2359304 | tf_op jit(solution)/shard_map/ppermute | solution.py:22
  27.4 20.9 %collective-permute-start.3 = (bf16[12,256,128]{2,1,0:T(8,128)(2,1)}, bf16[12,256,128]{2,1,0:T(8,128)(2,1)}, u32[]{:S(2)}, u32[]{:S(2)}) collective-permute-start(bf16[12,256,128]{2,1,0:T(8,128)(2,1)} %get-tuple-element.100), channel_id=1, source_target_pairs={{0,1},{1,2},{2,3},{3,4},{4,5},{5,6},{6,7},{7,0},{8,9},{9,10},{10,1... | collective-permute-start | bytes 2359304 | tf_op jit(solution)/shard_map/ppermute | solution.py:22
  28.7 21.7 %collective-permute-start.4 = (bf16[2,1,8,128,128]{4,3,2,1,0:T(8,128)(2,1)S(1)}, bf16[2,1,8,128,128]{4,3,2,1,0:T(8,128)(2,1)S(1)}, u32[]{:S(2)}, u32[]{:S(2)}) collective-permute-start(bf16[2,1,8,128,128]{4,3,2,1,0:T(8,128)(2,1)S(1)} %get-tuple-element.99), channel_id=1, source_target_pairs={{0,24},{8,0},{16,8},{24,16},{1,25},{9,1},{17,9},{25,17},{2,26},{10... | collective-permute-start | bytes 1572872 | tf_op jit(solution)/shard_map/ppermute | solution.py:22
  31.8 18.6 %collective-permute-start.5 = (bf16[2,1,8,128,128]{4,3,2,1,0:T(8,128)(2,1)S(1)}, bf16[2,1,8,128,128]{4,3,2,1,0:T(8,128)(2,1)S(1)}, u32[]{:S(2)}, u32[]{:S(2)}) collective-permute-start(bf16[2,1,8,128,128]{4,3,2,1,0:T(8,128)(2,1)S(1)} %get-tuple-element.98), channel_id=1, source_target_pairs={{0,8},{8,16},{16,24},{24,0},{1,9},{9,17},{17,25},{25,1},{2,10},{10... | collective-permute-start | bytes 1572872 | tf_op jit(solution)/shard_map/ppermute | solution.py:22
  53.2 20.0 %collective-permute-start.7 = (bf16[12,256,128]{2,1,0:T(8,128)(2,1)}, bf16[12,256,128]{2,1,0:T(8,128)(2,1)}, u32[]{:S(2)}, u32[]{:S(2)}) collective-permute-start(bf16[12,256,128]{2,1,0:T(8,128)(2,1)} %pad_maximum_fusion.4), channel_id=1, source_target_pairs={{0,1},{1,2},{2,3},{3,4},{4,5},{5,6},{6,7},{7,0},{8,9},{9,10},{10,1... | collective-permute-start | bytes 2359304 | tf_op jit(solution)/shard_map/ppermute | solution.py:22
  54.3 21.0 %collective-permute-start.6 = (bf16[12,256,128]{2,1,0:T(8,128)(2,1)}, bf16[12,256,128]{2,1,0:T(8,128)(2,1)}, u32[]{:S(2)}, u32[]{:S(2)}) collective-permute-start(bf16[12,256,128]{2,1,0:T(8,128)(2,1)} %pad_maximum_fusion.3), channel_id=1, source_target_pairs={{0,7},{1,0},{2,1},{3,2},{4,3},{5,4},{6,5},{7,6},{8,15},{9,8},{10,9... | collective-permute-start | bytes 2359304 | tf_op jit(solution)/shard_map/ppermute | solution.py:22
  59.8 40.6 %collective-permute-start.10 = (bf16[2,1,8,256,128]{4,3,2,1,0:T(8,128)(2,1)S(1)}, bf16[2,1,8,256,128]{4,3,2,1,0:T(8,128)(2,1)S(1)}, u32[]{:S(2)}, u32[]{:S(2)}) collective-permute-start(bf16[2,1,8,256,128]{4,3,2,1,0:T(8,128)(2,1)S(1)} %get-tuple-element.97), channel_id=1, source_target_pairs={{0,24},{8,0},{16,8},{24,16},{1,25},{9,1},{17,9},{25,17},{2,26},{10... | collective-permute-start | bytes 3145736 | tf_op jit(solution)/shard_map/ppermute | solution.py:22
  62.9 37.5 %collective-permute-start.11 = (bf16[2,1,8,256,128]{4,3,2,1,0:T(8,128)(2,1)S(1)}, bf16[2,1,8,256,128]{4,3,2,1,0:T(8,128)(2,1)S(1)}, u32[]{:S(2)}, u32[]{:S(2)}) collective-permute-start(bf16[2,1,8,256,128]{4,3,2,1,0:T(8,128)(2,1)S(1)} %get-tuple-element.96), channel_id=1, source_target_pairs={{0,8},{8,16},{16,24},{24,0},{1,9},{9,17},{17,25},{25,1},{2,10},{10... | collective-permute-start | bytes 3145736 | tf_op jit(solution)/shard_map/ppermute | solution.py:22
  77.6 18.9 %collective-permute-start.9 = (bf16[12,256,128]{2,1,0:T(8,128)(2,1)S(1)}, bf16[12,256,128]{2,1,0:T(8,128)(2,1)S(1)}, u32[]{:S(2)}, u32[]{:S(2)}) collective-permute-start(bf16[12,256,128]{2,1,0:T(8,128)(2,1)S(1)} %pad_maximum_fusion.6), channel_id=1, source_target_pairs={{0,1},{1,2},{2,3},{3,4},{4,5},{5,6},{6,7},{7,0},{8,9},{9,10},{10,1... | collective-permute-start | bytes 2359304 | tf_op jit(solution)/shard_map/ppermute | solution.py:22
  78.0 21.6 %collective-permute-start.8 = (bf16[12,256,128]{2,1,0:T(8,128)(2,1)S(1)}, bf16[12,256,128]{2,1,0:T(8,128)(2,1)S(1)}, u32[]{:S(2)}, u32[]{:S(2)}) collective-permute-start(bf16[12,256,128]{2,1,0:T(8,128)(2,1)S(1)} %pad_maximum_fusion.5), channel_id=1, source_target_pairs={{0,7},{1,0},{2,1},{3,2},{4,3},{5,4},{6,5},{7,6},{8,15},{9,8},{10,9... | collective-permute-start | bytes 2359304 | tf_op jit(solution)/shard_map/ppermute | solution.py:22
  81.6 33.9 %collective-permute-start.14 = (bf16[4,1280,128]{2,1,0:T(8,128)(2,1)S(1)}, bf16[4,1280,128]{2,1,0:T(8,128)(2,1)S(1)}, u32[]{:S(2)}, u32[]{:S(2)}) collective-permute-start(bf16[4,1280,128]{2,1,0:T(8,128)(2,1)S(1)} %constant_dynamic-update-slice_fusion.refs_0_), channel_id=1, source_target_pairs={{0,8},{8,16},{16,24},{24,0},{1,9},{9,17},{17,25},{25,1},{2,10},{10... | collective-permute-start | bytes 3932168 | tf_op jit(solution)/shard_map/ppermute | solution.py:22
  96.5 28.5 %collective-permute-start.15 = (bf16[4,1280,128]{2,1,0:T(8,128)(2,1)S(1)}, bf16[4,1280,128]{2,1,0:T(8,128)(2,1)S(1)}, u32[]{:S(2)}, u32[]{:S(2)}) collective-permute-start(bf16[4,1280,128]{2,1,0:T(8,128)(2,1)S(1)} %constant_dynamic-update-slice_fusion.refs_0_), channel_id=1, source_target_pairs={{0,24},{8,0},{16,8},{24,16},{1,25},{9,1},{17,9},{25,17},{2,26},{10... | collective-permute-start | bytes 3932168 | tf_op jit(solution)/shard_map/ppermute | solution.py:22
  100.6 10.9 %collective-permute-start.12 = (bf16[8,256,128]{2,1,0:T(8,128)(2,1)S(1)}, bf16[8,256,128]{2,1,0:T(8,128)(2,1)S(1)}, u32[]{:S(2)}, u32[]{:S(2)}) collective-permute-start(bf16[8,256,128]{2,1,0:T(8,128)(2,1)S(1)} %fusion.2), channel_id=1, source_target_pairs={{0,7},{1,0},{2,1},{3,2},{4,3},{5,4},{6,5},{7,6},{8,15},{9,8},{10,9... | collective-permute-start | bytes 1572872 | tf_op jit(solution)/shard_map/ppermute | solution.py:22
  101.2 7.6 %collective-permute-start.13 = (bf16[4,256,128]{2,1,0:T(8,128)(2,1)S(1)}, bf16[4,256,128]{2,1,0:T(8,128)(2,1)S(1)}, u32[]{:S(2)}, u32[]{:S(2)}) collective-permute-start(bf16[4,256,128]{2,1,0:T(8,128)(2,1)S(1)} %slice.67), channel_id=1, source_target_pairs={{0,1},{1,2},{2,3},{3,4},{4,5},{5,6},{6,7},{7,0},{8,9},{9,10},{10,1... | collective-permute-start | bytes 786440 | tf_op jit(solution)/shard_map/ppermute | solution.py:22
  127.1 15.6 %all-to-all-start = ((bf16[8,256,128]{2,1,0:T(8,128)(2,1)}), bf16[8,256,128]{2,1,0:T(8,128)(2,1)S(1)}, u32[]{:S(2)}, u32[]{:S(2)}) async-start(bf16[8,256,128]{2,1,0:T(8,128)(2,1)} %fusion.1), calls=%async_computation | async-start | bytes 1048576 | tf_op jit(solution)/shard_map/all_to_all | solution.py:40
  143.5 29.0 %all-to-all-start.1 = ((bf16[16,256,128]{2,1,0:T(8,128)(2,1)}), bf16[16,256,128]{2,1,0:T(8,128)(2,1)}, u32[]{:S(2)}, u32[]{:S(2)}) async-start(bf16[16,256,128]{2,1,0:T(8,128)(2,1)} %bitcast.65), calls=%async_computation.1 | async-start | bytes 2097152 | tf_op jit(solution)/shard_map/all_to_all | solution.py:40
  151.8 22.1 %collective-permute-start.16 = (bf16[4,768,128]{2,1,0:T(8,128)(2,1)S(1)}, bf16[4,768,128]{2,1,0:T(8,128)(2,1)}, u32[]{:S(2)}, u32[]{:S(2)}) collective-permute-start(bf16[4,768,128]{2,1,0:T(8,128)(2,1)S(1)} %constant_dynamic-update-slice_fusion.6.refs_1_), channel_id=1, source_target_pairs={{0,8},{8,16},{16,24},{24,0},{1,9},{9,17},{17,25},{25,1},{2,10},{10... | collective-permute-start | bytes 2359304 | tf_op jit(solution)/shard_map/ppermute | solution.py:22
  152.7 21.2 %collective-permute-start.17 = (bf16[4,768,128]{2,1,0:T(8,128)(2,1)S(1)}, bf16[4,768,128]{2,1,0:T(8,128)(2,1)}, u32[]{:S(2)}, u32[]{:S(2)}) collective-permute-start(bf16[4,768,128]{2,1,0:T(8,128)(2,1)S(1)} %constant_dynamic-update-slice_fusion.6.refs_1_), channel_id=1, source_target_pairs={{0,24},{8,0},{16,8},{24,16},{1,25},{9,1},{17,9},{25,17},{2,26},{10... | collective-permute-start | bytes 2359304 | tf_op jit(solution)/shard_map/ppermute | solution.py:22
  156.9 7.6 %collective-permute-start.18 = (f32[128,512]{1,0:T(8,128)}, f32[128,512]{1,0:T(8,128)}, u32[]{:S(2)}, u32[]{:S(2)}) collective-permute-start(f32[128,512]{1,0:T(8,128)} %add.164), channel_id=1, source_target_pairs={{0,128},{128,0},{1,129},{129,1},{2,130},{130,2},{3,131},{131,3},{4... | collective-permute-start | bytes 786440 | tf_op jit(solution)/shard_map/ppermute | solution.py:273
  157.5 41.8 %collective-permute-start.19 = (bf16[4,1280,128]{2,1,0:T(8,128)(2,1)S(1)}, bf16[4,1280,128]{2,1,0:T(8,128)(2,1)}, u32[]{:S(2)}, u32[]{:S(2)}) collective-permute-start(bf16[4,1280,128]{2,1,0:T(8,128)(2,1)S(1)} %collective-permute-done.14.refs_2_), channel_id=1, source_target_pairs={{0,8},{8,16},{16,24},{24,0},{1,9},{9,17},{17,25},{25,1},{2,10},{10... | collective-permute-start | bytes 3932168 | tf_op jit(solution)/shard_map/ppermute | solution.py:22
  173.9 25.4 %collective-permute-start.20 = (bf16[4,768,128]{2,1,0:T(8,128)(2,1)}, bf16[4,768,128]{2,1,0:T(8,128)(2,1)}, u32[]{:S(2)}, u32[]{:S(2)}) collective-permute-start(bf16[4,768,128]{2,1,0:T(8,128)(2,1)} %collective-permute-done.17.refs_7_), channel_id=1, source_target_pairs={{0,24},{8,0},{16,8},{24,16},{1,25},{9,1},{17,9},{25,17},{2,26},{10... | collective-permute-start | bytes 2359304 | tf_op jit(solution)/shard_map/ppermute | solution.py:22
  177.5 21.8 %all-to-all-start.2 = ((f32[64,1,128]{2,1,0:T(1,128)}), f32[64,1,128]{2,1,0:T(1,128)S(1)}, u32[]{:S(2)}, u32[]{:S(2)}) async-start(f32[64,1,128]{2,1,0:T(1,128)} %broadcast_in_dim.16), calls=%async_computation.2 | async-start | bytes 65536 | tf_op jit(solution)/shard_map/all_to_all | solution.py:284
  (20 other events, 200.4 us)

commit v4 on v3

--- a/solution.py
+++ b/solution.py
@@ -101,10 +101,7 @@
     )(hidden, gain, cotangent)
 
 
-def tail_kernel(count, place, hidden, gain, cotangent, inverse, *refs):
-    weights = refs[:count]
-    key_out, grad_hidden, held, grad, keys, dots, sems = refs[count:]
-    tokens, width = hidden.shape
+def use_blocks(steps, place, hidden, gain, cotangent, inverse, weights, held, sems, keys, dots, keep):
     x, y, z = place[0], place[1], place[2]
     split = weights[0].shape[1]
     places = (pl.ds(0, split), pl.ds(split, weights[1].shape[1]))
@@ -113,17 +110,18 @@
             lanes = pl.ds(group * LANES, LANES)
             there = held.at[i // 2, places[i % 2], lanes]
             pltpu.make_async_copy(ref.at[group], there, sems.at[i // 2]).start()
-    keys[...] = jnp.zeros_like(keys)
-    dots[...] = jnp.zeros_like(dots)
 
     def block(i, carry):
-        yr, half = i // 2, i % 2
+        index, half = i // 2, i % 2
 
         @pl.when(half == 0)
         def _():
-            pltpu.make_async_copy(held.at[yr], held.at[yr], sems.at[yr]).wait()
-
-        rows = held[yr, pl.ds(pl.multiple_of(half * 1024, 1024), 1024), :]
+            pltpu.make_async_copy(held.at[index], held.at[index], sems.at[index]).wait()
+
+        yr = steps[0]
+        for k in range(1, len(steps)):
+            yr = jnp.where(index == k, steps[k], yr)
+        rows = held[index, pl.ds(pl.multiple_of(half * 1024, 1024), 1024), :]
         grads = lax.dot_general(
             cotangent[...], rows, (((1,), (1,)), ((), ())), preferred_element_type=F32
         )
@@ -131,11 +129,12 @@
         total = dots[...]
         for j in range(8):
             zr = jnp.where(half == 0, ORDER[j // 2], ORDER[4 + j // 2])
-            feature = (x ^ (j % 2)) * 32 + ((y - yr) & 3) * 8 + ((z - zr) & 7)
+            near = x ^ (j % 2), (y - yr) & 3, (z - zr) & 7
+            feature = near[0] * 32 + near[1] * 8 + near[2]
             at = pl.ds(pl.multiple_of(feature * LANES, LANES), LANES)
             normed = hidden[:, at].astype(F32) * inverse[...]
             weighted = grads[:, j * LANES : (j + 1) * LANES] * gain[:, at]
-            grad[:, at] = weighted
+            keep(feature, near, weighted)
             total = total + weighted * normed
             scaled.append((normed * gain[:, at]).astype(BF16))
         dots[...] = total
@@ -144,48 +143,86 @@
         )
         return carry
 
-    lax.fori_loop(0, count, block, 0)
+    lax.fori_loop(0, 2 * len(steps), block, 0)
+
+
+def early_kernel(steps, place, hidden, gain, cotangent, inverse, *refs):
+    count = 2 * len(steps)
+    grad, keys, dots, held, sems = refs[count:]
+    keys[...] = jnp.zeros_like(keys)
+    dots[...] = jnp.zeros_like(dots)
+
+    def keep(feature, near, weighted):
+        grad[:, pl.ds(pl.multiple_of(feature * LANES, LANES), LANES)] = weighted
+
+    use_blocks(
+        steps, place, hidden, gain, cotangent, inverse, refs[:count], held, sems, keys, dots, keep
+    )
+
+
+def late_kernel(steps, place, hidden, gain, cotangent, inverse, grad, keys_in, dots_in, *refs):
+    count = 2 * len(steps)
+    key_out, grad_hidden, held, sems, keys, dots, fresh = refs[count:]
+    width = hidden.shape[1]
+    keys[...] = keys_in[...]
+    dots[...] = dots_in[...]
+
+    def keep(feature, near, weighted):
+        at = (near[0] * 8 + near[2]) * LANES
+        fresh[:, pl.ds(pl.multiple_of(at, LANES), LANES)] = weighted
+
+    use_blocks(
+        steps, place, hidden, gain, cotangent, inverse, refs[:count], held, sems, keys, dots, keep
+    )
     key_out[...] = keys[...].astype(BF16)
     mean = jnp.sum(dots[...], axis=-1, keepdims=True) / width
-
-    def finish(i, carry):
+    inv = inverse[:, :1]
+
+    def result(at, weighted):
+        normed = hidden[:, at].astype(F32) * inv
+        grad_hidden[:, at] = (inv * (weighted - normed * mean)).astype(BF16)
+
+    def early(i, carry):
         at = pl.ds(pl.multiple_of(i * 512, 512), 512)
-        inv = inverse[:, :1]
-        normed = hidden[:, at].astype(F32) * inv
-        grad_hidden[:, at] = (inv * (grad[:, at] - normed * mean)).astype(BF16)
+        result(at, grad[:, at])
         return carry
 
-    lax.fori_loop(0, width // 512, finish, 0)
-
-
-def tail(place, hidden, gain, cotangent, inverse, weights):
+    lax.fori_loop(0, width // 512, early, 0)
+
+    def late(i, carry):
+        y = (place[1] - steps[0]) & 3
+        at = pl.ds(pl.multiple_of((i // 2) * 4096 + y * 1024 + (i % 2) * 512, 512), 512)
+        result(at, fresh[:, pl.ds(pl.multiple_of(i * 512, 512), 512)])
+        return carry
+
+    lax.fori_loop(0, 4, late, 0)
+
+
+def rows_call(kernel, steps, outs, scratch, operands, weights, name):
+    hidden, cotangent = operands[1], operands[3]
     tokens, width = hidden.shape
     keys = cotangent.shape[1]
-    count = len(weights)
     vmem = pl.BlockSpec(memory_space=pltpu.VMEM)
     return pl.pallas_call(
-        functools.partial(tail_kernel, count),
-        out_shape=(
-            jax.ShapeDtypeStruct((tokens, keys), BF16),
-            jax.ShapeDtypeStruct((tokens, width), BF16),
-        ),
+        functools.partial(kernel, steps),
+        out_shape=outs,
         in_specs=[pl.BlockSpec(memory_space=pltpu.SMEM)]
-        + [vmem] * 4
-        + [pl.BlockSpec(memory_space=pl.ANY)] * count,
-        out_specs=(vmem, vmem),
+        + [vmem] * (len(operands) - 1)
+        + [pl.BlockSpec(memory_space=pl.ANY)] * len(weights),
+        out_specs=(vmem,) * len(outs),
         scratch_shapes=[
-            pltpu.VMEM((count // 2, 2 * width // count, keys), BF16),
-            pltpu.VMEM((tokens, width), F32),
-            pltpu.VMEM((tokens, keys), F32),
-            pltpu.VMEM((tokens, LANES), F32),
-            pltpu.SemaphoreType.DMA((count // 2,)),
+            pltpu.VMEM((len(steps), width // 4, keys), BF16),
+            pltpu.SemaphoreType.DMA((len(steps),)),
+            *scratch,
         ],
-        compiler_params=pltpu.CompilerParams(vmem_limit_bytes=40 * 1024 * 1024),
+        compiler_params=pltpu.CompilerParams(vmem_limit_bytes=36 * 1024 * 1024),
         cost_estimate=pl.CostEstimate(
-            flops=4 * tokens * width * keys, bytes_accessed=18 * 1024 * 1024, transcendentals=0
-        ),
-        name="tail",
-    )(place, hidden, gain, cotangent, inverse, *weights)
+            flops=len(steps) * tokens * width * keys,
+            bytes_accessed=(12 + 2 * len(steps)) * 1024 * 1024,
+            transcendentals=0,
+        ),
+        name=name,
+    )(*operands, *weights)
 
 
 def outer_step(current, moment, average):
@@ -230,18 +267,18 @@
     sums = groups[0] * groups[1]
 
     def along_z(total, slab, step):
-        moved = shift(jnp.concatenate([total.reshape(sums, cut, rows), slab]), "z", step)
-        return moved[:sums], moved[sums:]
+        return shift(jnp.concatenate([total.reshape(sums, cut, rows), slab]), "z", step)
 
     far_b = term(part_b, "y", 1, 2)
-    left, z7 = along_z(term(part_a, "z", 2, -4), pair, -1)
-    right, z1 = along_z(term(part_a, "z", 2, 3), pair, 1)
+    left = along_z(term(part_a, "z", 2, -4), pair, -1)
+    right = along_z(term(part_a, "z", 2, 3), pair, 1)
     b_left = shift(far_b[..., half:, :], "y", -1)
     b_right = shift(far_b[..., :half, :], "y", 1)
-    left, z7, right, z1, b_left, b_right = together(left, z7, right, z1, b_left, b_right)
-
-    left, z6 = along_z(added(part_a, "z", 2, -3, left), z7, -1)
-    right, z2 = along_z(added(part_a, "z", 2, 2, right), z1, 1)
+    left, right, b_left, b_right = together(left, right, b_left, b_right)
+
+    z7, z1 = left[sums:], right[sums:]
+    left = along_z(added(part_a, "z", 2, -3, left[:sums]), z7, -1)
+    right = along_z(added(part_a, "z", 2, 2, right[:sums]), z1, 1)
     none = jnp.zeros_like(b_left)
     b_left = shift(
         added(part_b, "y", 1, -1, jnp.concatenate([none, b_left], axis=3)), "y", -1
@@ -249,31 +286,34 @@
     b_right = shift(
         added(part_b, "y", 1, 1, jnp.concatenate([b_right, none], axis=3)), "y", 1
     )
-    left, z6, right, z2 = together(left, z6, right, z2)
-
-    left, z5 = along_z(added(part_a, "z", 2, -2, left), z6, -1)
-    right, z3 = along_z(added(part_a, "z", 2, 1, right), z2, 1)
+    left, right, b_left, b_right = together(left, right, b_left, b_right)
+
+    z6, z2 = left[sums:], right[sums:]
+    left = along_z(added(part_a, "z", 2, -2, left[:sums]), z6, -1)
+    right = along_z(added(part_a, "z", 2, 1, right[:sums]), z2, 1)
     first = jnp.concatenate([pair, z1, z7, z2, z6], axis=1)
     first1, first3 = shift(first, "y", 1), shift(first, "y", -1)
-    left, z5, right, z3, b_left, b_right = together(left, z5, right, z3, b_left, b_right)
-
     sum_b = term(part_b, "y", 1, 0).astype(F32) + b_left.astype(F32) + b_right.astype(F32)
     sum_b = exchange_sum(sum_b.reshape(-1, cut, rows), ("xh", "z"))
-    left = shift(added(part_a, "z", 2, -1, left), "z", -1)
+    left, right, first1, first3, sum_b, core = together(
+        left, right, first1, first3, sum_b, core
+    )
+
+    z5, z3 = left[sums:], right[sums:]
+    left = shift(added(part_a, "z", 2, -1, left[:sums]), "z", -1)
     z4 = shift(z3, "z", 1)
-    left, right, z4, first1, first3, core = together(left, right, z4, first1, first3, core)
-
-    sum_a = term(part_a, "z", 2, 0).reshape(left.shape).astype(F32)
-    sum_a = sum_a + left.astype(F32) + right.astype(F32)
-    sum_a = exchange_sum(sum_a.reshape(-1, cut, rows), ("xh", "y"))
-    second = jnp.concatenate([z3, z5, z4], axis=1)
-    second1, second3 = shift(second, "y", 1), shift(second, "y", -1)
     first2 = shift(first1, "y", 1)
     both = mine + core
     summed = both + lax.ppermute(both, "xl", [(0, 1), (1, 0)])
-    sum_a, sum_b, second1, second3, summed = together(sum_a, sum_b, second1, second3, summed)
+    left, right, z4, summed = together(left, right, z4, summed)
+
+    second = jnp.concatenate([z3, z5, z4], axis=1)
+    second1, second3 = shift(second, "y", 1), shift(second, "y", -1)
+    sum_a = term(part_a, "z", 2, 0).reshape(left.shape).astype(F32)
+    sum_a = sum_a + left.astype(F32) + right[:sums].astype(F32)
+    sum_a = exchange_sum(sum_a.reshape(-1, cut, rows), ("xh", "y"))
+    sum_a, sum_b, second1, second3 = together(sum_a, sum_b, second1, second3)
     second2 = shift(second3, "y", -1)
-    weights = [first, second, first1, second1, first2, second2, first3, second3]
 
     grad_weight = jnp.concatenate([sum_a.T, sum_b.T], axis=-1) * factor
 
@@ -284,7 +324,38 @@
     grad_gain = lax.all_to_all(
         jnp.broadcast_to(own_sum[None], (devices, rows)), GROUP, 0, 0, tiled=True
     ).reshape(-1)
-    key_out, grad_hidden = tail(place, hidden, norm_gain, cotangent, inverse, weights)
+    keys = cotangent.shape[1]
+    tokens, features = hidden.shape
+    operands = (place, hidden, norm_gain, cotangent, inverse)
+    partial = rows_call(
+        early_kernel,
+        (0, 1, 3),
+        (
+            jax.ShapeDtypeStruct((tokens, features), F32),
+            jax.ShapeDtypeStruct((tokens, keys), F32),
+            jax.ShapeDtypeStruct((tokens, LANES), F32),
+        ),
+        (),
+        operands,
+        (first, second, first1, second1, first3, second3),
+        "early_rows",
+    )
+    key_out, grad_hidden = rows_call(
+        late_kernel,
+        (2,),
+        (
+            jax.ShapeDtypeStruct((tokens, keys), BF16),
+            jax.ShapeDtypeStruct((tokens, features), BF16),
+        ),
+        (
+            pltpu.VMEM((tokens, keys), F32),
+            pltpu.VMEM((tokens, LANES), F32),
+            pltpu.VMEM((tokens, features // 4), F32),
+        ),
+        (*operands, *partial),
+        (first2, second2),
+        "late_rows",
+    )
 
     moment = lax.dynamic_index_in_dim(outer_momentum, chosen, 0, keepdims=False)
     new_params, new_momentum = outer_step(current, moment, summed / 4.0)

time: 221 us -> 227 us (1.027)
  waiting for transfers between devices: 84.8 us -> 78.9 us
  Pallas kernels: 24.5 us -> 29 us
  other arithmetic: 23.4 us -> 27.5 us
  local copies, waits for them, and re-layouts: 30.6 us -> 33.1 us
    all_to_all x2, waiting for transfers between devices: 10.9 us -> 31.4 us  [exchange_sum(): blocks = lax.all_to_all(part.astype(BF16), axes, 0, 0, tiled=True)]
    ppermute x19, waiting for transfers between devices: 60.5 us -> 44.5 us  [shift(): return lax.ppermute(value, axis, [(i, (i + step) % n) for i in range(n)])]
    convert_element_type x6, other arithmetic: 3.08 us -> 10 us  [added(): return (mine.astype(F32) + received.astype(F32)).astype(BF16)]
    all_to_all x1, waiting for transfers between devices: 6.42 us -> 0.01 us  [per_device(): lax.all_to_all(jnp.broadcast_to(own_sum[None], (devices, rows)), GROUP, 0...]
    unnamed x50 -> x61, local copies, waits for them, and re-layouts: 16 us -> 21.4 us
    pallas_call x1 -> x2, Pallas kernels: 14.4 us -> 18.9 us  [rows_call(): pl.pallas_call(functools.partial(kernel, steps), out_shape=outs, in_specs...]
    ppermute x1, waiting for transfers between devices: 6.98 us -> 3.01 us  [per_device(): summed = both + lax.ppermute(both, 'xl', [(0, 1), (1, 0)])]
    slice x12 -> x6, local copies, waits for them, and re-layouts: 7.95 us -> 5.18 us  [the longest x2 2.07 us: per_device(): z7, z1 = (left[sums:], right[sums:])]
  transfers between devices with their start and end apart: 24 -> 24, of which waited for: 12 -> 11; matrix products, arithmetic and copies ran while one was open for 16% -> 12% of each run, Pallas kernels for 5% -> 9%
where the time goes in v4:
time: 227 us; the launch traced here: 225 us
  waiting for transfers between devices  78.9 us (35%)
  starting transfers between devices  54.9 us (24%)
  local copies, waits for them, and re-layouts  33.1 us (15%)
  Pallas kernels  29 us (13%)
  other arithmetic  27.5 us (12%)
    ppermute x19, waiting for transfers between devices, shift(): return lax.ppermute(value, axis, [(i, (i + step) % n) for i in range(n)])  44.5 us
    ppermute x19, starting transfers between devices, shift(): return lax.ppermute(value, axis, [(i, (i + step) % n) for i in range(n)])  33 us
    all_to_all x2, waiting for transfers between devices, exchange_sum(): blocks = lax.all_to_all(part.astype(BF16), axes, 0, 0, tiled=True)  31.4 us
    unnamed x61, local copies, waits for them, and re-layouts  21.4 us
    pallas_call x2, Pallas kernels, rows_call(): pl.pallas_call(functools.partial(kernel, steps), out_shape=outs, in_specs...  18.9 us
    all_to_all x2, starting transfers between devices, exchange_sum(): blocks = lax.all_to_all(part.astype(BF16), axes, 0, 0, tiled=True)  11.2 us
    pallas_call x1, Pallas kernels, weight_grad(): pl.pallas_call(weight_grad_kernel, grid=(blocks // per_step,), out_shape=...  10.1 us
    convert_element_type x6, other arithmetic, added(): return (mine.astype(F32) + received.astype(F32)).astype(BF16)  10 us
  transfers between devices with their start and end apart: 24, of which 11 were waited for; matrix products, arithmetic and copies ran while one was open for 12% of the time, Pallas kernels for 9%

profile of v4, /device:TPU:2, one launch (start us, length us, event | category | flops | bytes accessed | tf_op | source)
XLA Modules:
  0.0 225.0 jit_solution(17663655647594365058)
XLA Ops:
  5.8 10.1 %weight_grad.1 = (bf16[64,256,128]{2,1,0:T(8,128)(2,1)}, bf16[64,256,128]{2,1,0:T(8,128)(2,1)}, f32[256,128]{1,0:T(8,128)}) custom-call(bf16[256,8192]{1,0:T(8,128)(2,1)} %bitcast.61, f32[1,8192]{1,0:T(1,128)} %gain.5, bf16[256,512]{1,0:T(8,128)(2,1)} %bitcast.64), custom_call_target="tpu_custom_call" | custom-call | flops 2147483648 | bytes 23068672 | tf_op jit(solution)/shard_map/weight_grad/pallas_call | solution.py:81
  16.7 3.5 %constant_dynamic-slice_fusion.2 = (bf16[2,4,1,256,128]{4,3,1,0,2:T(8,128)(2,1)}, bf16[2,4,1,256,128]{4,3,1,0,2:T(8,128)(2,1)S(1)}, bf16[2,4,1,256,128]{4,3,1,0,...) fusion(s32[]{:T(128)S(6)} %select_n.57, ...), kind=kLoop, calls=%fused_computation.41 | loop fusion | bytes 8388640 | tf_op jit(solution)/shard_map/dynamic_slice | solution.py:31
  21.5 5.9 %collective-permute-start.2 = (bf16[12,256,128]{2,1,0:T(8,128)(2,1)}, bf16[12,256,128]{2,1,0:T(8,128)(2,1)}, u32[]{:S(2)}, u32[]{:S(2)}) collective-permute-start(bf16[12,256,128]{2,1,0:T(8,128)(2,1)} %get-tuple-element.105), channel_id=1, source_target_pairs={{0,7},{1,0},{2,1},{3,2},{4,3},{5,4},{6,5},{7,6},{8,15},{9,8},{10,9... | collective-permute-start | bytes 2359304 | tf_op jit(solution)/shard_map/ppermute | solution.py:22
  29.7 3.0 %collective-permute-start.4 = (bf16[2,1,8,128,128]{4,3,2,1,0:T(8,128)(2,1)}, bf16[2,1,8,128,128]{4,3,2,1,0:T(8,128)(2,1)}, u32[]{:S(2)}, u32[]{:S(2)}) collective-permute-start(bf16[2,1,8,128,128]{4,3,2,1,0:T(8,128)(2,1)} %get-tuple-element.95), channel_id=1, source_target_pairs={{0,24},{8,0},{16,8},{24,16},{1,25},{9,1},{17,9},{25,17},{2,26},{10... | collective-permute-start | bytes 1572872 | tf_op jit(solution)/shard_map/ppermute | solution.py:22
  32.7 11.6 %collective-permute-done.4 = bf16[2,1,8,128,128]{4,3,2,1,0:T(8,128)(2,1)} collective-permute-done((bf16[2,1,8,128,128]{4,3,2,1,0:T(8,128)(2,1)}, bf16[2,1,8,128,128]{4,3,2,1,0:T(8,128)(2,1)}, u32[]{:S(2)}, u32[]{:S(2)}) %collective-permute-start.4) | collective-permute-done | bytes 524320 | tf_op jit(solution)/shard_map/ppermute | solution.py:22
  44.3 3.4 %collective-permute-done.5 = bf16[2,1,8,128,128]{4,3,2,1,0:T(8,128)(2,1)} collective-permute-done((bf16[2,1,8,128,128]{4,3,2,1,0:T(8,128)(2,1)}, bf16[2,1,8,128,128]{4,3,2,1,0:T(8,128)(2,1)}, u32[]{:S(2)}, u32[]{:S(2)}) %collective-permute-start.5) | collective-permute-done | bytes 524320 | tf_op jit(solution)/shard_map/ppermute | solution.py:22
  48.3 3.5 %add_convert_fusion.1 = (bf16[2,1,8,256,128]{4,3,2,1,0:T(8,128)(2,1)}, bf16[2,1,8,256,128]{4,3,2,1,0:T(8,128)(2,1)}) fusion(bf16[2,1,8,128,128]{4,3,2,1,0:T(8,128)(2,1)} %collective-permute-done.5, bf16[2,4,8,256,128]{4,3,2,1,0:T(8,128)(2,1)} %bitcast.68, s32[]{:T(128)S(6)} %select_n.52, bf16[2,1,8,128,128]{4,3,2,1,0:T(8,128)(2,1)} %collective-permute-done.4, ...), kind=kLoop, calls=%fused_computation.2 | loop fusion | flops 4194304 | bytes 5242888 | tf_op jit(solution)/shard_map/convert_element_type | solution.py:36
  51.8 3.0 %collective-permute-start.8 = (bf16[2,1,8,256,128]{4,3,2,1,0:T(8,128)(2,1)}, bf16[2,1,8,256,128]{4,3,2,1,0:T(8,128)(2,1)}, u32[]{:S(2)}, u32[]{:S(2)}) collective-permute-start(bf16[2,1,8,256,128]{4,3,2,1,0:T(8,128)(2,1)} %get-tuple-element.93), channel_id=1, source_target_pairs={{0,24},{8,0},{16,8},{24,16},{1,25},{9,1},{17,9},{25,17},{2,26},{10... | collective-permute-start | bytes 3145736 | tf_op jit(solution)/shard_map/ppermute | solution.py:22
  61.3 3.2 %collective-permute-start.6 = (bf16[12,256,128]{2,1,0:T(8,128)(2,1)}, bf16[12,256,128]{2,1,0:T(8,128)(2,1)}, u32[]{:S(2)}, u32[]{:S(2)}) collective-permute-start(bf16[12,256,128]{2,1,0:T(8,128)(2,1)} %pad_maximum_fusion.3), channel_id=1, source_target_pairs={{0,7},{1,0},{2,1},{3,2},{4,3},{5,4},{6,5},{7,6},{8,15},{9,8},{10,9... | collective-permute-start | bytes 2359304 | tf_op jit(solution)/shard_map/ppermute | solution.py:22
  64.5 13.2 %collective-permute-done.7 = bf16[12,256,128]{2,1,0:T(8,128)(2,1)S(1)} collective-permute-done((bf16[12,256,128]{2,1,0:T(8,128)(2,1)}, bf16[12,256,128]{2,1,0:T(8,128)(2,1)S(1)}, u32[]{:S(2)}, u32[]{:S(2)}) %collective-permute-start.7) | collective-permute-done | bytes 786464 | tf_op jit(solution)/shard_map/ppermute | solution.py:22
  77.7 2.6 %collective-permute-done.6 = bf16[12,256,128]{2,1,0:T(8,128)(2,1)} collective-permute-done((bf16[12,256,128]{2,1,0:T(8,128)(2,1)}, bf16[12,256,128]{2,1,0:T(8,128)(2,1)}, u32[]{:S(2)}, u32[]{:S(2)}) %collective-permute-start.6) | collective-permute-done | bytes 786464 | tf_op jit(solution)/shard_map/ppermute | solution.py:22
  80.3 3.3 %add_convert_fusion = bf16[2,1,8,256,128]{4,3,2,1,0:T(8,128)(2,1)} fusion(bf16[2,1,8,256,128]{4,3,2,1,0:T(8,128)(2,1)} %collective-permute-done.9, bf16[2,1,8,256,128]{4,3,2,1,0:T(8,128)(2,1)} %collective-permute-done.8, bf16[2,4,8,256,128]{4,3,2,1,0:T(8,128)(2,1)} %bitcast.69, s32[]{:T(128)S(6)} %select_n.55), kind=kLoop, calls=%fused_computation.1 | loop fusion | flops 3145728 | bytes 4194308 | tf_op jit(solution)/shard_map/convert_element_type | solution.py:40
  83.6 6.0 %all-to-all-start = ((bf16[16,256,128]{2,1,0:T(8,128)(2,1)}), bf16[16,256,128]{2,1,0:T(8,128)(2,1)}, u32[]{:S(2)}, u32[]{:S(2)}) async-start(bf16[16,256,128]{2,1,0:T(8,128)(2,1)} %bitcast.18), calls=%async_computation | async-start | bytes 2097152 | tf_op jit(solution)/shard_map/all_to_all | solution.py:40
  91.2 2.9 %collective-permute-start.13 = (bf16[4,1280,128]{2,1,0:T(8,128)(2,1)S(1)}, bf16[4,1280,128]{2,1,0:T(8,128)(2,1)S(1)}, u32[]{:S(2)}, u32[]{:S(2)}) collective-permute-start(bf16[4,1280,128]{2,1,0:T(8,128)(2,1)S(1)} %get-tuple-element.99.refs_0_), channel_id=1, source_target_pairs={{0,24},{8,0},{16,8},{24,16},{1,25},{9,1},{17,9},{25,17},{2,26},{10... | collective-permute-start | bytes 3932168 | tf_op jit(solution)/shard_map/ppermute | solution.py:22
  101.8 16.8 %all-to-all-done = bf16[16,256,128]{2,1,0:T(8,128)(2,1)} async-done(((bf16[16,256,128]{2,1,0:T(8,128)(2,1)}), bf16[16,256,128]{2,1,0:T(8,128)(2,1)}, u32[]{:S(2)}, u32[]{:S(2)}) %all-to-all-start) | async-done | bytes 1048608 | tf_op jit(solution)/shard_map/all_to_all | solution.py:40
  120.7 9.5 %collective-permute-done.11 = bf16[12,256,128]{2,1,0:T(8,128)(2,1)} collective-permute-done((bf16[12,256,128]{2,1,0:T(8,128)(2,1)}, bf16[12,256,128]{2,1,0:T(8,128)(2,1)}, u32[]{:S(2)}, u32[]{:S(2)}) %collective-permute-start.11) | collective-permute-done | bytes 786464 | tf_op jit(solution)/shard_map/ppermute | solution.py:22
  136.9 3.0 %collective-permute-done.16 = f32[128,512]{1,0:T(8,128)S(1)} collective-permute-done((f32[128,512]{1,0:T(8,128)S(1)}, f32[128,512]{1,0:T(8,128)S(1)}, u32[]{:S(2)}, u32[]{:S(2)}) %collective-permute-start.16) | collective-permute-done | bytes 262176 | tf_op jit(solution)/shard_map/ppermute | solution.py:307
  144.4 3.2 %collective-permute-start.18 = (bf16[4,768,128]{2,1,0:T(8,128)(2,1)S(1)}, bf16[4,768,128]{2,1,0:T(8,128)(2,1)}, u32[]{:S(2)}, u32[]{:S(2)}) collective-permute-start(bf16[4,768,128]{2,1,0:T(8,128)(2,1)S(1)} %pad_maximum_fusion.7.refs_1_), channel_id=1, source_target_pairs={{0,24},{8,0},{16,8},{24,16},{1,25},{9,1},{17,9},{25,17},{2,26},{10... | collective-permute-start | bytes 2359304 | tf_op jit(solution)/shard_map/ppermute | solution.py:22
  149.6 5.3 %all-to-all-start.1 = ((bf16[8,256,128]{2,1,0:T(8,128)(2,1)}), bf16[8,256,128]{2,1,0:T(8,128)(2,1)S(1)}, u32[]{:S(2)}, u32[]{:S(2)}) async-start(bf16[8,256,128]{2,1,0:T(8,128)(2,1)} %fusion.1), calls=%async_computation.1 | async-start | bytes 1048576 | tf_op jit(solution)/shard_map/all_to_all | solution.py:40
  157.0 14.6 %all-to-all-done.1 = bf16[8,256,128]{2,1,0:T(8,128)(2,1)S(1)} async-done(((bf16[8,256,128]{2,1,0:T(8,128)(2,1)}), bf16[8,256,128]{2,1,0:T(8,128)(2,1)S(1)}, u32[]{:S(2)}, u32[]{:S(2)}) %all-to-all-start.1) | async-done | bytes 524320 | tf_op jit(solution)/shard_map/all_to_all | solution.py:40
  177.4 9.9 %all-to-all-start.2 = ((f32[64,1,128]{2,1,0:T(1,128)}), f32[64,1,128]{2,1,0:T(1,128)}, u32[]{:S(2)}, u32[]{:S(2)}) async-start(f32[64,1,128]{2,1,0:T(1,128)} %broadcast_in_dim.16), calls=%async_computation.2 | async-start | bytes 65536 | tf_op jit(solution)/shard_map/all_to_all | solution.py:324
  195.0 10.3 %early_rows.1 = (f32[256,8192]{1,0:T(8,128)}, f32[256,512]{1,0:T(8,128)S(1)}, f32[256,128]{1,0:T(8,128)S(1)}) custom-call(s32[3]{0:T(128)S(1)} %pad_add_fusion.place, bf16[256,8192]{1,0:T(8,128)(2,1)S(1)} %bitcast.62, f32[1,8192]{1,0:T(1,128)S(1)} %copy-done.8, bf16[256,512]{1,0:T(8,128)(2,1)S(1)} %bitcast.65, f32[256,128]{1,0:T(8,128)S(1)} %copy-done.5, ...), custom_call_target="tpu_custom_call" | custom-call | flops 3221225472 | bytes 18874368 | tf_op jit(solution)/shard_map/early_rows/pallas_call | solution.py:206
  206.8 3.4 %copy-done = f32[256,8192]{1,0:T(8,128)S(1)} copy-done((f32[256,8192]{1,0:T(8,128)S(1)}, f32[256,8192]{1,0:T(8,128)}, u32[]{:S(2)}) %copy-start) | copy-done | bytes 8388632
  215.0 8.7 %late_rows.1 = (bf16[256,512]{1,0:T(8,128)(2,1)}, bf16[256,8192]{1,0:T(8,128)(2,1)}) custom-call(s32[3]{0:T(128)S(1)} %pad_add_fusion.place, bf16[256,8192]{1,0:T(8,128)(2,1)S(1)} %bitcast.63, f32[1,8192]{1,0:T(1,128)S(1)} %copy-done.9, bf16[256,512]{1,0:T(8,128)(2,1)S(1)} %bitcast.66, f32[256,128]{1,0:T(8,128)S(1)} %copy-done.5, f32[256,8192]{1,0:T(8,128)S(1)} %copy-done, ...), custom_call_target="tpu_custom_call" | custom-call | flops 1073741824 | bytes 14680064 | tf_op jit(solution)/shard_map/late_rows/pallas_call | solution.py:206
  (122 shorter events, 63.6 us)
Async XLA Ops:
  2.4 13.6 %collective-permute-start.1 = (f32[128,512]{1,0:T(8,128)S(1)}, f32[128,512]{1,0:T(8,128)S(1)}, u32[]{:S(2)}, u32[]{:S(2)}) collective-permute-start(f32[128,512]{1,0:T(8,128)S(1)} %bitcast_subtract_fusion), channel_id=1, source_target_pairs={{0,64},{64,0},{1,65},{65,1},{2,66},{66,2},{3,67},{67,3},{4,68},{68... | collective-permute-start | bytes 786440 | tf_op jit(solution)/shard_map/ppermute | solution.py:263
  3.6 12.3 %collective-permute-start = (bf16[4,128,128]{2,1,0:T(8,128)(2,1)S(1)}, bf16[4,128,128]{2,1,0:T(8,128)(2,1)S(1)}, u32[]{:S(2)}, u32[]{:S(2)}) collective-permute-start(bf16[4,128,128]{2,1,0:T(8,128)(2,1)S(1)} %bitcast.73), channel_id=1, source_target_pairs={{0,32},{32,0},{1,33},{33,1},{2,34},{34,2},{3,35},{35,3},{4,36},{36... | collective-permute-start | bytes 393224 | tf_op jit(solution)/shard_map/ppermute | solution.py:22
  21.5 26.2 %collective-permute-start.2 = (bf16[12,256,128]{2,1,0:T(8,128)(2,1)}, bf16[12,256,128]{2,1,0:T(8,128)(2,1)}, u32[]{:S(2)}, u32[]{:S(2)}) collective-permute-start(bf16[12,256,128]{2,1,0:T(8,128)(2,1)} %get-tuple-element.105), channel_id=1, source_target_pairs={{0,7},{1,0},{2,1},{3,2},{4,3},{5,4},{6,5},{7,6},{8,15},{9,8},{10,9... | collective-permute-start | bytes 2359304 | tf_op jit(solution)/shard_map/ppermute | solution.py:22
  27.4 20.9 %collective-permute-start.3 = (bf16[12,256,128]{2,1,0:T(8,128)(2,1)}, bf16[12,256,128]{2,1,0:T(8,128)(2,1)}, u32[]{:S(2)}, u32[]{:S(2)}) collective-permute-start(bf16[12,256,128]{2,1,0:T(8,128)(2,1)} %get-tuple-element.104), channel_id=1, source_target_pairs={{0,1},{1,2},{2,3},{3,4},{4,5},{5,6},{6,7},{7,0},{8,9},{9,10},{10,1... | collective-permute-start | bytes 2359304 | tf_op jit(solution)/shard_map/ppermute | solution.py:22
  29.7 14.6 %collective-permute-start.4 = (bf16[2,1,8,128,128]{4,3,2,1,0:T(8,128)(2,1)}, bf16[2,1,8,128,128]{4,3,2,1,0:T(8,128)(2,1)}, u32[]{:S(2)}, u32[]{:S(2)}) collective-permute-start(bf16[2,1,8,128,128]{4,3,2,1,0:T(8,128)(2,1)} %get-tuple-element.95), channel_id=1, source_target_pairs={{0,24},{8,0},{16,8},{24,16},{1,25},{9,1},{17,9},{25,17},{2,26},{10... | collective-permute-start | bytes 1572872 | tf_op jit(solution)/shard_map/ppermute | solution.py:22
  32.7 15.0 %collective-permute-start.5 = (bf16[2,1,8,128,128]{4,3,2,1,0:T(8,128)(2,1)}, bf16[2,1,8,128,128]{4,3,2,1,0:T(8,128)(2,1)}, u32[]{:S(2)}, u32[]{:S(2)}) collective-permute-start(bf16[2,1,8,128,128]{4,3,2,1,0:T(8,128)(2,1)} %get-tuple-element.94), channel_id=1, source_target_pairs={{0,8},{8,16},{16,24},{24,0},{1,9},{9,17},{17,25},{25,1},{2,10},{10... | collective-permute-start | bytes 1572872 | tf_op jit(solution)/shard_map/ppermute | solution.py:22
  51.8 28.5 %collective-permute-start.8 = (bf16[2,1,8,256,128]{4,3,2,1,0:T(8,128)(2,1)}, bf16[2,1,8,256,128]{4,3,2,1,0:T(8,128)(2,1)}, u32[]{:S(2)}, u32[]{:S(2)}) collective-permute-start(bf16[2,1,8,256,128]{4,3,2,1,0:T(8,128)(2,1)} %get-tuple-element.93), channel_id=1, source_target_pairs={{0,24},{8,0},{16,8},{24,16},{1,25},{9,1},{17,9},{25,17},{2,26},{10... | collective-permute-start | bytes 3145736 | tf_op jit(solution)/shard_map/ppermute | solution.py:22
  54.8 25.5 %collective-permute-start.9 = (bf16[2,1,8,256,128]{4,3,2,1,0:T(8,128)(2,1)}, bf16[2,1,8,256,128]{4,3,2,1,0:T(8,128)(2,1)}, u32[]{:S(2)}, u32[]{:S(2)}) collective-permute-start(bf16[2,1,8,256,128]{4,3,2,1,0:T(8,128)(2,1)} %get-tuple-element.92), channel_id=1, source_target_pairs={{0,8},{8,16},{16,24},{24,0},{1,9},{9,17},{17,25},{25,1},{2,10},{10... | collective-permute-start | bytes 3145736 | tf_op jit(solution)/shard_map/ppermute | solution.py:22
  58.1 19.7 %collective-permute-start.7 = (bf16[12,256,128]{2,1,0:T(8,128)(2,1)}, bf16[12,256,128]{2,1,0:T(8,128)(2,1)S(1)}, u32[]{:S(2)}, u32[]{:S(2)}) collective-permute-start(bf16[12,256,128]{2,1,0:T(8,128)(2,1)} %pad_maximum_fusion.4), channel_id=1, source_target_pairs={{0,1},{1,2},{2,3},{3,4},{4,5},{5,6},{6,7},{7,0},{8,9},{9,10},{10,1... | collective-permute-start | bytes 2359304 | tf_op jit(solution)/shard_map/ppermute | solution.py:22
  61.3 19.0 %collective-permute-start.6 = (bf16[12,256,128]{2,1,0:T(8,128)(2,1)}, bf16[12,256,128]{2,1,0:T(8,128)(2,1)}, u32[]{:S(2)}, u32[]{:S(2)}) collective-permute-start(bf16[12,256,128]{2,1,0:T(8,128)(2,1)} %pad_maximum_fusion.3), channel_id=1, source_target_pairs={{0,7},{1,0},{2,1},{3,2},{4,3},{5,4},{6,5},{7,6},{8,15},{9,8},{10,9... | collective-permute-start | bytes 2359304 | tf_op jit(solution)/shard_map/ppermute | solution.py:22
  83.6 35.0 %all-to-all-start = ((bf16[16,256,128]{2,1,0:T(8,128)(2,1)}), bf16[16,256,128]{2,1,0:T(8,128)(2,1)}, u32[]{:S(2)}, u32[]{:S(2)}) async-start(bf16[16,256,128]{2,1,0:T(8,128)(2,1)} %bitcast.18), calls=%async_computation | async-start | bytes 2097152 | tf_op jit(solution)/shard_map/all_to_all | solution.py:40
  90.8 39.4 %collective-permute-start.12 = (bf16[4,1280,128]{2,1,0:T(8,128)(2,1)S(1)}, bf16[4,1280,128]{2,1,0:T(8,128)(2,1)}, u32[]{:S(2)}, u32[]{:S(2)}) collective-permute-start(bf16[4,1280,128]{2,1,0:T(8,128)(2,1)S(1)} %get-tuple-element.99.refs_0_), channel_id=1, source_target_pairs={{0,8},{8,16},{16,24},{24,0},{1,9},{9,17},{17,25},{25,1},{2,10},{10... | collective-permute-start | bytes 3932168 | tf_op jit(solution)/shard_map/ppermute | solution.py:22
  91.2 39.0 %collective-permute-start.13 = (bf16[4,1280,128]{2,1,0:T(8,128)(2,1)S(1)}, bf16[4,1280,128]{2,1,0:T(8,128)(2,1)S(1)}, u32[]{:S(2)}, u32[]{:S(2)}) collective-permute-start(bf16[4,1280,128]{2,1,0:T(8,128)(2,1)S(1)} %get-tuple-element.99.refs_0_), channel_id=1, source_target_pairs={{0,24},{8,0},{16,8},{24,16},{1,25},{9,1},{17,9},{25,17},{2,26},{10... | collective-permute-start | bytes 3932168 | tf_op jit(solution)/shard_map/ppermute | solution.py:22
  96.4 33.8 %collective-permute-start.11 = (bf16[12,256,128]{2,1,0:T(8,128)(2,1)}, bf16[12,256,128]{2,1,0:T(8,128)(2,1)}, u32[]{:S(2)}, u32[]{:S(2)}) collective-permute-start(bf16[12,256,128]{2,1,0:T(8,128)(2,1)} %pad_maximum_fusion.6), channel_id=1, source_target_pairs={{0,1},{1,2},{2,3},{3,4},{4,5},{5,6},{6,7},{7,0},{8,9},{9,10},{10,1... | collective-permute-start | bytes 2359304 | tf_op jit(solution)/shard_map/ppermute | solution.py:22
  100.4 29.8 %collective-permute-start.10 = (bf16[12,256,128]{2,1,0:T(8,128)(2,1)}, bf16[12,256,128]{2,1,0:T(8,128)(2,1)}, u32[]{:S(2)}, u32[]{:S(2)}) collective-permute-start(bf16[12,256,128]{2,1,0:T(8,128)(2,1)} %pad_maximum_fusion.5), channel_id=1, source_target_pairs={{0,7},{1,0},{2,1},{3,2},{4,3},{5,4},{6,5},{7,6},{8,15},{9,8},{10,9... | collective-permute-start | bytes 2359304 | tf_op jit(solution)/shard_map/ppermute | solution.py:22
  131.8 12.4 %collective-permute-start.14 = (bf16[8,256,128]{2,1,0:T(8,128)(2,1)S(1)}, bf16[8,256,128]{2,1,0:T(8,128)(2,1)S(1)}, u32[]{:S(2)}, u32[]{:S(2)}) collective-permute-start(bf16[8,256,128]{2,1,0:T(8,128)(2,1)S(1)} %fusion.2), channel_id=1, source_target_pairs={{0,7},{1,0},{2,1},{3,2},{4,3},{5,4},{6,5},{7,6},{8,15},{9,8},{10,9... | collective-permute-start | bytes 1572872 | tf_op jit(solution)/shard_map/ppermute | solution.py:22
  133.4 6.5 %collective-permute-start.16 = (f32[128,512]{1,0:T(8,128)S(1)}, f32[128,512]{1,0:T(8,128)S(1)}, u32[]{:S(2)}, u32[]{:S(2)}) collective-permute-start(f32[128,512]{1,0:T(8,128)S(1)} %add.161), channel_id=1, source_target_pairs={{0,128},{128,0},{1,129},{129,1},{2,130},{130,2},{3,131},{131,3},{4... | collective-permute-start | bytes 786440 | tf_op jit(solution)/shard_map/ppermute | solution.py:307
  135.1 7.7 %collective-permute-start.15 = (bf16[4,256,128]{2,1,0:T(8,128)(2,1)S(1)}, bf16[4,256,128]{2,1,0:T(8,128)(2,1)S(1)}, u32[]{:S(2)}, u32[]{:S(2)}) collective-permute-start(bf16[4,256,128]{2,1,0:T(8,128)(2,1)S(1)} %slice.52), channel_id=1, source_target_pairs={{0,1},{1,2},{2,3},{3,4},{4,5},{5,6},{6,7},{7,0},{8,9},{9,10},{10,1... | collective-permute-start | bytes 786440 | tf_op jit(solution)/shard_map/ppermute | solution.py:22
  144.2 27.5 %collective-permute-start.17 = (bf16[4,768,128]{2,1,0:T(8,128)(2,1)S(1)}, bf16[4,768,128]{2,1,0:T(8,128)(2,1)S(1)}, u32[]{:S(2)}, u32[]{:S(2)}) collective-permute-start(bf16[4,768,128]{2,1,0:T(8,128)(2,1)S(1)} %pad_maximum_fusion.7.refs_1_), channel_id=1, source_target_pairs={{0,8},{8,16},{16,24},{24,0},{1,9},{9,17},{17,25},{25,1},{2,10},{10... | collective-permute-start | bytes 2359304 | tf_op jit(solution)/shard_map/ppermute | solution.py:22
  144.4 28.2 %collective-permute-start.18 = (bf16[4,768,128]{2,1,0:T(8,128)(2,1)S(1)}, bf16[4,768,128]{2,1,0:T(8,128)(2,1)}, u32[]{:S(2)}, u32[]{:S(2)}) collective-permute-start(bf16[4,768,128]{2,1,0:T(8,128)(2,1)S(1)} %pad_maximum_fusion.7.refs_1_), channel_id=1, source_target_pairs={{0,24},{8,0},{16,8},{24,16},{1,25},{9,1},{17,9},{25,17},{2,26},{10... | collective-permute-start | bytes 2359304 | tf_op jit(solution)/shard_map/ppermute | solution.py:22
  149.6 22.0 %all-to-all-start.1 = ((bf16[8,256,128]{2,1,0:T(8,128)(2,1)}), bf16[8,256,128]{2,1,0:T(8,128)(2,1)S(1)}, u32[]{:S(2)}, u32[]{:S(2)}) async-start(bf16[8,256,128]{2,1,0:T(8,128)(2,1)} %fusion.1), calls=%async_computation.1 | async-start | bytes 1048576 | tf_op jit(solution)/shard_map/all_to_all | solution.py:40
  154.9 51.9 %collective-permute-start.19 = (bf16[4,1280,128]{2,1,0:T(8,128)(2,1)}, bf16[4,1280,128]{2,1,0:T(8,128)(2,1)S(1)}, u32[]{:S(2)}, u32[]{:S(2)}) collective-permute-start(bf16[4,1280,128]{2,1,0:T(8,128)(2,1)} %collective-permute-done.12.refs_2_), channel_id=1, source_target_pairs={{0,8},{8,16},{16,24},{24,0},{1,9},{9,17},{17,25},{25,1},{2,10},{10... | collective-permute-start | bytes 3932168 | tf_op jit(solution)/shard_map/ppermute | solution.py:22
  172.6 34.2 %collective-permute-start.20 = (bf16[4,768,128]{2,1,0:T(8,128)(2,1)}, bf16[4,768,128]{2,1,0:T(8,128)(2,1)S(1)}, u32[]{:S(2)}, u32[]{:S(2)}) collective-permute-start(bf16[4,768,128]{2,1,0:T(8,128)(2,1)} %collective-permute-done.18.refs_5_), channel_id=1, source_target_pairs={{0,24},{8,0},{16,8},{24,16},{1,25},{9,1},{17,9},{25,17},{2,26},{10... | collective-permute-start | bytes 2359304 | tf_op jit(solution)/shard_map/ppermute | solution.py:22
  177.4 29.4 %all-to-all-start.2 = ((f32[64,1,128]{2,1,0:T(1,128)}), f32[64,1,128]{2,1,0:T(1,128)}, u32[]{:S(2)}, u32[]{:S(2)}) async-start(f32[64,1,128]{2,1,0:T(1,128)} %broadcast_in_dim.16), calls=%async_computation.2 | async-start | bytes 65536 | tf_op jit(solution)/shard_map/all_to_all | solution.py:324
  (28 other events, 164.5 us)

commit v5 on v4

--- a/solution.py
+++ b/solution.py
@@ -160,8 +160,9 @@
     )
 
 
-def late_kernel(steps, place, hidden, gain, cotangent, inverse, grad, keys_in, dots_in, *refs):
+def late_kernel(steps, place, hidden, gain, cotangent, inverse, grad, keys_in, dots_in, after, *refs):
     count = 2 * len(steps)
+    del after
     key_out, grad_hidden, held, sems, keys, dots, fresh = refs[count:]
     width = hidden.shape[1]
     keys[...] = keys_in[...]
@@ -215,7 +216,7 @@
             pltpu.SemaphoreType.DMA((len(steps),)),
             *scratch,
         ],
-        compiler_params=pltpu.CompilerParams(vmem_limit_bytes=36 * 1024 * 1024),
+        compiler_params=pltpu.CompilerParams(vmem_limit_bytes=60 * 1024 * 1024),
         cost_estimate=pl.CostEstimate(
             flops=len(steps) * tokens * width * keys,
             bytes_accessed=(12 + 2 * len(steps)) * 1024 * 1024,
@@ -293,33 +294,37 @@
     right = along_z(added(part_a, "z", 2, 1, right[:sums]), z2, 1)
     first = jnp.concatenate([pair, z1, z7, z2, z6], axis=1)
     first1, first3 = shift(first, "y", 1), shift(first, "y", -1)
-    sum_b = term(part_b, "y", 1, 0).astype(F32) + b_left.astype(F32) + b_right.astype(F32)
-    sum_b = exchange_sum(sum_b.reshape(-1, cut, rows), ("xh", "z"))
-    left, right, first1, first3, sum_b, core = together(
-        left, right, first1, first3, sum_b, core
-    )
+    left, right = together(left, right)
 
     z5, z3 = left[sums:], right[sums:]
     left = shift(added(part_a, "z", 2, -1, left[:sums]), "z", -1)
     z4 = shift(z3, "z", 1)
-    first2 = shift(first1, "y", 1)
-    both = mine + core
-    summed = both + lax.ppermute(both, "xl", [(0, 1), (1, 0)])
-    left, right, z4, summed = together(left, right, z4, summed)
+    left, right, z4, first1, first3, b_left, b_right, core = together(
+        left, right, z4, first1, first3, b_left, b_right, core
+    )
 
     second = jnp.concatenate([z3, z5, z4], axis=1)
     second1, second3 = shift(second, "y", 1), shift(second, "y", -1)
     sum_a = term(part_a, "z", 2, 0).reshape(left.shape).astype(F32)
     sum_a = sum_a + left.astype(F32) + right[:sums].astype(F32)
     sum_a = exchange_sum(sum_a.reshape(-1, cut, rows), ("xh", "y"))
-    sum_a, sum_b, second1, second3 = together(sum_a, sum_b, second1, second3)
+    sum_b = term(part_b, "y", 1, 0).astype(F32) + b_left.astype(F32) + b_right.astype(F32)
+    sum_b = sum_b.reshape(-1, cut, rows).astype(BF16)
+    first2 = shift(first1, "y", 1)
+    sum_a, sum_b, second1, second3, core = together(sum_a, sum_b, second1, second3, core)
+
     second2 = shift(second3, "y", -1)
+    both = mine + core
+    summed = both + lax.ppermute(both, "xl", [(0, 1), (1, 0)])
+    sum_b = exchange_sum(sum_b, ("xh", "z"))
+    sum_b, summed = together(sum_b, summed)
 
     grad_weight = jnp.concatenate([sum_a.T, sum_b.T], axis=-1) * factor
 
     me = lax.axis_index(GROUP)
     own_gain = lax.dynamic_slice_in_dim(norm_gain[0], me * rows, rows)
     own_sum = jnp.sum(own.astype(F32) * grad_weight, axis=-1) / own_gain
+    place = jnp.stack([lax.axis_index(axis) for axis in GROUP])
     place = jnp.stack([lax.axis_index(axis) for axis in GROUP])
     grad_gain = lax.all_to_all(
         jnp.broadcast_to(own_sum[None], (devices, rows)), GROUP, 0, 0, tiled=True
@@ -340,6 +345,7 @@
         (first, second, first1, second1, first3, second3),
         "early_rows",
     )
+
     key_out, grad_hidden = rows_call(
         late_kernel,
         (2,),
@@ -352,7 +358,7 @@
             pltpu.VMEM((tokens, LANES), F32),
             pltpu.VMEM((tokens, features // 4), F32),
         ),
-        (*operands, *partial),
+        (*operands, *partial, own_sum[None]),
         (first2, second2),
         "late_rows",
     )

time: 227 us -> 193 us (0.85)
  local copies, waits for them, and re-layouts: 33.1 us -> 12.8 us
  other arithmetic: 27.5 us -> 16.2 us
  Pallas kernels: 29 us -> 37.3 us
  waiting for transfers between devices: 78.9 us -> 72.2 us
  starting transfers between devices: 54.9 us -> 51.4 us
    unnamed x61 -> x31, local copies, waits for them, and re-layouts: 21.4 us -> 4.93 us
    all_to_all x2, waiting for transfers between devices: 31.4 us -> 17.7 us  [exchange_sum(): blocks = lax.all_to_all(part.astype(BF16), axes, 0, 0, tiled=True)]
    ppermute x19, waiting for transfers between devices: 44.5 us -> 54.5 us  [shift(): return lax.ppermute(value, axis, [(i, (i + step) % n) for i in range(n)])]
    pallas_call x2, Pallas kernels: 18.9 us -> 27.2 us  [rows_call(): pl.pallas_call(functools.partial(kernel, steps), out_shape=outs, in_specs...]
    convert_element_type x6, other arithmetic: 10 us -> 5.14 us  [added(): return (mine.astype(F32) + received.astype(F32)).astype(BF16)]
    convert_element_type x2 -> x1, other arithmetic: 5.42 us -> 1.04 us  [exchange_sum(): blocks = lax.all_to_all(part.astype(BF16), axes, 0, 0, tiled=True)]
    concatenate x5, other arithmetic: 5.18 us -> 1.65 us  [along_z(): jnp.concatenate([total.reshape(sums, cut, rows), slab])]
    ppermute x1, waiting for transfers between devices: 3.01 us -> 0.01 us  [per_device(): summed = both + lax.ppermute(both, 'xl', [(0, 1), (1, 0)])]
  transfers between devices with their start and end apart: 24 -> 24, of which waited for: 11 -> 12; matrix products, arithmetic and copies ran while one was open for 12% -> 9% of each run, Pallas kernels for 9% -> 19%
where the time goes in v5:
time: 193 us; the launch traced here: 192 us
  waiting for transfers between devices  72.2 us (37%)
  starting transfers between devices  51.4 us (27%)
  Pallas kernels  37.3 us (19%)
  other arithmetic  16.2 us (8%)
  local copies, waits for them, and re-layouts  12.8 us (7%)
    ppermute x19, waiting for transfers between devices, shift(): return lax.ppermute(value, axis, [(i, (i + step) % n) for i in range(n)])  54.5 us
    ppermute x19, starting transfers between devices, shift(): return lax.ppermute(value, axis, [(i, (i + step) % n) for i in range(n)])  34.6 us
    pallas_call x2, Pallas kernels, rows_call(): pl.pallas_call(functools.partial(kernel, steps), out_shape=outs, in_specs...  27.2 us
    all_to_all x2, waiting for transfers between devices, exchange_sum(): blocks = lax.all_to_all(part.astype(BF16), axes, 0, 0, tiled=True)  17.7 us
    pallas_call x1, Pallas kernels, weight_grad(): pl.pallas_call(weight_grad_kernel, grid=(blocks // per_step,), out_shape=...  10.1 us
    all_to_all x2, starting transfers between devices, exchange_sum(): blocks = lax.all_to_all(part.astype(BF16), axes, 0, 0, tiled=True)  8.27 us
    all_to_all x1, starting transfers between devices, per_device(): lax.all_to_all(jnp.broadcast_to(own_sum[None], (devices, rows)), GROUP, 0...  7.77 us
    convert_element_type x6, other arithmetic, added(): return (mine.astype(F32) + received.astype(F32)).astype(BF16)  5.14 us
  transfers between devices with their start and end apart: 24, of which 12 were waited for; matrix products, arithmetic and copies ran while one was open for 9% of the time, Pallas kernels for 19%

profile of v5, /device:TPU:2, one launch (start us, length us, event | category | flops | bytes accessed | tf_op | source)
XLA Modules:
  0.0 191.6 jit_solution(7728384148256457361)
XLA Ops:
  5.8 10.1 %weight_grad.1 = (bf16[64,256,128]{2,1,0:T(8,128)(2,1)}, bf16[64,256,128]{2,1,0:T(8,128)(2,1)}, f32[256,128]{1,0:T(8,128)}) custom-call(bf16[256,8192]{1,0:T(8,128)(2,1)} %bitcast.62, f32[1,8192]{1,0:T(1,128)} %gain.5, bf16[256,512]{1,0:T(8,128)(2,1)} %bitcast.74), custom_call_target="tpu_custom_call" | custom-call | flops 2147483648 | bytes 23068672 | tf_op jit(solution)/shard_map/weight_grad/pallas_call | solution.py:81
  16.7 2.5 %constant_dynamic-slice_fusion.2 = (bf16[2,4,1,256,128]{4,3,1,0,2:T(8,128)(2,1)S(1)}, bf16[2,4,1,256,128]{4,3,1,0,2:T(8,128)(2,1)S(1)}, bf16[2,4,1,256,128]{4,3,...) fusion(s32[]{:T(128)S(6)} %select_n.56, ...), kind=kLoop, calls=%fused_computation.41 | loop fusion | bytes 8388640 | tf_op jit(solution)/shard_map/dynamic_slice | solution.py:31
  20.5 5.9 %collective-permute-start.2 = (bf16[12,256,128]{2,1,0:T(8,128)(2,1)}, bf16[12,256,128]{2,1,0:T(8,128)(2,1)}, u32[]{:S(2)}, u32[]{:S(2)}) collective-permute-start(bf16[12,256,128]{2,1,0:T(8,128)(2,1)} %get-tuple-element.111), channel_id=1, source_target_pairs={{0,7},{1,0},{2,1},{3,2},{4,3},{5,4},{6,5},{7,6},{8,15},{9,8},{10,9... | collective-permute-start | bytes 2359304 | tf_op jit(solution)/shard_map/ppermute | solution.py:22
  28.7 3.0 %collective-permute-start.4 = (bf16[2,1,8,128,128]{4,3,2,1,0:T(8,128)(2,1)}, bf16[2,1,8,128,128]{4,3,2,1,0:T(8,128)(2,1)}, u32[]{:S(2)}, u32[]{:S(2)}) collective-permute-start(bf16[2,1,8,128,128]{4,3,2,1,0:T(8,128)(2,1)} %get-tuple-element.101), channel_id=1, source_target_pairs={{0,24},{8,0},{16,8},{24,16},{1,25},{9,1},{17,9},{25,17},{2,26},{10... | collective-permute-start | bytes 1572872 | tf_op jit(solution)/shard_map/ppermute | solution.py:22
  31.8 11.6 %collective-permute-done.4 = bf16[2,1,8,128,128]{4,3,2,1,0:T(8,128)(2,1)} collective-permute-done((bf16[2,1,8,128,128]{4,3,2,1,0:T(8,128)(2,1)}, bf16[2,1,8,128,128]{4,3,2,1,0:T(8,128)(2,1)}, u32[]{:S(2)}, u32[]{:S(2)}) %collective-permute-start.4) | collective-permute-done | bytes 524320 | tf_op jit(solution)/shard_map/ppermute | solution.py:22
  43.4 3.4 %collective-permute-done.5 = bf16[2,1,8,128,128]{4,3,2,1,0:T(8,128)(2,1)} collective-permute-done((bf16[2,1,8,128,128]{4,3,2,1,0:T(8,128)(2,1)}, bf16[2,1,8,128,128]{4,3,2,1,0:T(8,128)(2,1)}, u32[]{:S(2)}, u32[]{:S(2)}) %collective-permute-start.5) | collective-permute-done | bytes 524320 | tf_op jit(solution)/shard_map/ppermute | solution.py:22
  49.5 3.1 %collective-permute-start.8 = (bf16[2,1,8,256,128]{4,3,2,1,0:T(8,128)(2,1)S(1)}, bf16[2,1,8,256,128]{4,3,2,1,0:T(8,128)(2,1)S(1)}, u32[]{:S(2)}, u32[]{:S(2)}) collective-permute-start(bf16[2,1,8,256,128]{4,3,2,1,0:T(8,128)(2,1)S(1)} %get-tuple-element.99), channel_id=1, source_target_pairs={{0,24},{8,0},{16,8},{24,16},{1,25},{9,1},{17,9},{25,17},{2,26},{10... | collective-permute-start | bytes 3145736 | tf_op jit(solution)/shard_map/ppermute | solution.py:22
  57.3 3.3 %collective-permute-start.6 = (bf16[12,256,128]{2,1,0:T(8,128)(2,1)S(1)}, bf16[12,256,128]{2,1,0:T(8,128)(2,1)S(1)}, u32[]{:S(2)}, u32[]{:S(2)}) collective-permute-start(bf16[12,256,128]{2,1,0:T(8,128)(2,1)S(1)} %pad_maximum_fusion.3), channel_id=1, source_target_pairs={{0,7},{1,0},{2,1},{3,2},{4,3},{5,4},{6,5},{7,6},{8,15},{9,8},{10,9... | collective-permute-start | bytes 2359304 | tf_op jit(solution)/shard_map/ppermute | solution.py:22
  60.6 13.8 %collective-permute-done.7 = bf16[12,256,128]{2,1,0:T(8,128)(2,1)S(1)} collective-permute-done((bf16[12,256,128]{2,1,0:T(8,128)(2,1)S(1)}, bf16[12,256,128]{2,1,0:T(8,128)(2,1)S(1)}, u32[]{:S(2)}, u32[]{:S(2)}) %collective-permute-start.7) | collective-permute-done | bytes 786464 | tf_op jit(solution)/shard_map/ppermute | solution.py:22
  79.0 3.5 %collective-permute-start.10 = (bf16[12,256,128]{2,1,0:T(8,128)(2,1)S(1)}, bf16[12,256,128]{2,1,0:T(8,128)(2,1)S(1)}, u32[]{:S(2)}, u32[]{:S(2)}) collective-permute-start(bf16[12,256,128]{2,1,0:T(8,128)(2,1)S(1)} %pad_maximum_fusion.5), channel_id=1, source_target_pairs={{0,7},{1,0},{2,1},{3,2},{4,3},{5,4},{6,5},{7,6},{8,15},{9,8},{10,9... | collective-permute-start | bytes 2359304 | tf_op jit(solution)/shard_map/ppermute | solution.py:22
  82.5 3.2 %collective-permute-start.15 = (bf16[4,1280,128]{2,1,0:T(8,128)(2,1)S(1)}, bf16[4,1280,128]{2,1,0:T(8,128)(2,1)S(1)}, u32[]{:S(2)}, u32[]{:S(2)}) collective-permute-start(bf16[4,1280,128]{2,1,0:T(8,128)(2,1)S(1)} %get-tuple-element.105.refs_0_), channel_id=1, source_target_pairs={{0,24},{8,0},{16,8},{24,16},{1,25},{9,1},{17,9},{25,17},{2,26},{10... | collective-permute-start | bytes 3932168 | tf_op jit(solution)/shard_map/ppermute | solution.py:22
  85.7 11.4 %collective-permute-done.11 = bf16[12,256,128]{2,1,0:T(8,128)(2,1)S(1)} collective-permute-done((bf16[12,256,128]{2,1,0:T(8,128)(2,1)S(1)}, bf16[12,256,128]{2,1,0:T(8,128)(2,1)S(1)}, u32[]{:S(2)}, u32[]{:S(2)}) %collective-permute-start.11) | collective-permute-done | bytes 786464 | tf_op jit(solution)/shard_map/ppermute | solution.py:22
  97.4 3.6 %collective-permute-start.12 = (bf16[8,256,128]{2,1,0:T(8,128)(2,1)S(1)}, bf16[8,256,128]{2,1,0:T(8,128)(2,1)S(1)}, u32[]{:S(2)}, u32[]{:S(2)}) collective-permute-start(bf16[8,256,128]{2,1,0:T(8,128)(2,1)S(1)} %fusion.2), channel_id=1, source_target_pairs={{0,7},{1,0},{2,1},{3,2},{4,3},{5,4},{6,5},{7,6},{8,15},{9,8},{10,9... | collective-permute-start | bytes 1572872 | tf_op jit(solution)/shard_map/ppermute | solution.py:22
  101.2 7.5 %collective-permute-done.13 = bf16[4,256,128]{2,1,0:T(8,128)(2,1)S(1)} collective-permute-done((bf16[4,256,128]{2,1,0:T(8,128)(2,1)S(1)}, bf16[4,256,128]{2,1,0:T(8,128)(2,1)S(1)}, u32[]{:S(2)}, u32[]{:S(2)}) %collective-permute-start.13) | collective-permute-done | bytes 262176 | tf_op jit(solution)/shard_map/ppermute | solution.py:22
  109.0 2.7 %collective-permute-done.14.refs_2_ = bf16[4,1280,128]{2,1,0:T(8,128)(2,1)S(1)} collective-permute-done((bf16[4,1280,128]{2,1,0:T(8,128)(2,1)S(1)}, bf16[4,1280,128]{2,1,0:T(8,128)(2,1)S(1)}, u32[]{:S(2)}, u32[]{:S(2)}) %collective-permute-start.14) | collective-permute-done | bytes 1310752 | tf_op jit(solution)/shard_map/ppermute | solution.py:22
  112.9 3.1 %collective-permute-start.17 = (bf16[4,768,128]{2,1,0:T(8,128)(2,1)}, bf16[4,768,128]{2,1,0:T(8,128)(2,1)}, u32[]{:S(2)}, u32[]{:S(2)}) collective-permute-start(bf16[4,768,128]{2,1,0:T(8,128)(2,1)} %pad_maximum_fusion.7.refs_1_), channel_id=1, source_target_pairs={{0,24},{8,0},{16,8},{24,16},{1,25},{9,1},{17,9},{25,17},{2,26},{10... | collective-permute-start | bytes 2359304 | tf_op jit(solution)/shard_map/ppermute | solution.py:22
  117.0 3.8 %all-to-all-start = ((bf16[8,256,128]{2,1,0:T(8,128)(2,1)}), bf16[8,256,128]{2,1,0:T(8,128)(2,1)S(1)}, u32[]{:S(2)}, u32[]{:S(2)}) async-start(bf16[8,256,128]{2,1,0:T(8,128)(2,1)} %fusion.1), calls=%async_computation | async-start | bytes 1048576 | tf_op jit(solution)/shard_map/all_to_all | solution.py:40
  120.9 2.7 %add_convert_fusion = bf16[2,1,8,256,128]{4,3,2,1,0:T(8,128)(2,1)} fusion(bf16[2,1,8,256,128]{4,3,2,1,0:T(8,128)(2,1)S(1)} %copy-done.4, bf16[2,1,8,256,128]{4,3,2,1,0:T(8,128)(2,1)S(1)} %copy-done.2, bf16[2,4,8,256,128]{4,3,2,1,0:T(8,128)(2,1)} %bitcast.60, s32[]{:T(128)S(6)} %select_n.57), kind=kLoop, calls=%fused_computation.1 | loop fusion | flops 3145728 | bytes 4194308 | tf_op jit(solution)/shard_map/convert_element_type | solution.py:312
  123.5 12.3 %all-to-all-done = bf16[8,256,128]{2,1,0:T(8,128)(2,1)S(1)} async-done(((bf16[8,256,128]{2,1,0:T(8,128)(2,1)}), bf16[8,256,128]{2,1,0:T(8,128)(2,1)S(1)}, u32[]{:S(2)}, u32[]{:S(2)}) %all-to-all-start) | async-done | bytes 524320 | tf_op jit(solution)/shard_map/all_to_all | solution.py:40
  135.9 4.4 %all-to-all-start.1 = ((bf16[16,256,128]{2,1,0:T(8,128)(2,1)}), bf16[16,256,128]{2,1,0:T(8,128)(2,1)S(1)}, u32[]{:S(2)}, u32[]{:S(2)}) async-start(bf16[16,256,128]{2,1,0:T(8,128)(2,1)} %bitcast.20), calls=%async_computation.1 | async-start | bytes 2097152 | tf_op jit(solution)/shard_map/all_to_all | solution.py:40
  145.1 13.0 %early_rows.1 = (f32[256,8192]{1,0:T(8,128)}, f32[256,512]{1,0:T(8,128)}, f32[256,128]{1,0:T(8,128)}) custom-call(s32[3]{0:T(128)} %pad_add_fusion.place, bf16[256,8192]{1,0:T(8,128)(2,1)} %bitcast.63, f32[1,8192]{1,0:T(1,128)} %gain.5, bf16[256,512]{1,0:T(8,128)(2,1)} %bitcast.75, f32[256,128]{1,0:T(8,128)} %get-tuple-element.47.inverse, ...), custom_call_target="tpu_custom_call" | custom-call | flops 3221225472 | bytes 18874368 | tf_op jit(solution)/shard_map/early_rows/pallas_call | solution.py:207
  158.1 5.5 %all-to-all-done.1 = bf16[16,256,128]{2,1,0:T(8,128)(2,1)S(1)} async-done(((bf16[16,256,128]{2,1,0:T(8,128)(2,1)}), bf16[16,256,128]{2,1,0:T(8,128)(2,1)S(1)}, u32[]{:S(2)}, u32[]{:S(2)}) %all-to-all-start.1) | async-done | bytes 1048608 | tf_op jit(solution)/shard_map/all_to_all | solution.py:40
  166.0 7.8 %all-to-all-start.2 = ((f32[64,1,128]{2,1,0:T(1,128)}), f32[64,1,128]{2,1,0:T(1,128)S(1)}, u32[]{:S(2)}, u32[]{:S(2)}) async-start(f32[64,1,128]{2,1,0:T(1,128)} %broadcast_in_dim.8), calls=%async_computation.2 | async-start | bytes 65536 | tf_op jit(solution)/shard_map/all_to_all | solution.py:329
  176.7 14.2 %late_rows.1 = (bf16[256,512]{1,0:T(8,128)(2,1)}, bf16[256,8192]{1,0:T(8,128)(2,1)}) custom-call(s32[3]{0:T(128)} %pad_add_fusion.place, bf16[256,8192]{1,0:T(8,128)(2,1)} %bitcast.64, f32[1,8192]{1,0:T(1,128)} %gain.5, bf16[256,512]{1,0:T(8,128)(2,1)} %bitcast.76, f32[256,128]{1,0:T(8,128)} %get-tuple-element.47.inverse, ...), custom_call_target="tpu_custom_call" | custom-call | flops 1073741824 | bytes 14680064 | tf_op jit(solution)/shard_map/late_rows/pallas_call | solution.py:207
  (92 shorter events, 34.6 us)
Async XLA Ops:
  2.4 13.6 %collective-permute-start.1 = (f32[128,512]{1,0:T(8,128)S(1)}, f32[128,512]{1,0:T(8,128)S(1)}, u32[]{:S(2)}, u32[]{:S(2)}) collective-permute-start(f32[128,512]{1,0:T(8,128)S(1)} %bitcast_subtract_fusion), channel_id=1, source_target_pairs={{0,64},{64,0},{1,65},{65,1},{2,66},{66,2},{3,67},{67,3},{4,68},{68... | collective-permute-start | bytes 786440 | tf_op jit(solution)/shard_map/ppermute | solution.py:264
  3.6 12.3 %collective-permute-start = (bf16[4,128,128]{2,1,0:T(8,128)(2,1)S(1)}, bf16[4,128,128]{2,1,0:T(8,128)(2,1)S(1)}, u32[]{:S(2)}, u32[]{:S(2)}) collective-permute-start(bf16[4,128,128]{2,1,0:T(8,128)(2,1)S(1)} %bitcast.67), channel_id=1, source_target_pairs={{0,32},{32,0},{1,33},{33,1},{2,34},{34,2},{3,35},{35,3},{4,36},{36... | collective-permute-start | bytes 393224 | tf_op jit(solution)/shard_map/ppermute | solution.py:22
  20.5 26.3 %collective-permute-start.2 = (bf16[12,256,128]{2,1,0:T(8,128)(2,1)}, bf16[12,256,128]{2,1,0:T(8,128)(2,1)}, u32[]{:S(2)}, u32[]{:S(2)}) collective-permute-start(bf16[12,256,128]{2,1,0:T(8,128)(2,1)} %get-tuple-element.111), channel_id=1, source_target_pairs={{0,7},{1,0},{2,1},{3,2},{4,3},{5,4},{6,5},{7,6},{8,15},{9,8},{10,9... | collective-permute-start | bytes 2359304 | tf_op jit(solution)/shard_map/ppermute | solution.py:22
  26.4 20.9 %collective-permute-start.3 = (bf16[12,256,128]{2,1,0:T(8,128)(2,1)}, bf16[12,256,128]{2,1,0:T(8,128)(2,1)}, u32[]{:S(2)}, u32[]{:S(2)}) collective-permute-start(bf16[12,256,128]{2,1,0:T(8,128)(2,1)} %get-tuple-element.110), channel_id=1, source_target_pairs={{0,1},{1,2},{2,3},{3,4},{4,5},{5,6},{6,7},{7,0},{8,9},{9,10},{10,1... | collective-permute-start | bytes 2359304 | tf_op jit(solution)/shard_map/ppermute | solution.py:22
  28.7 14.6 %collective-permute-start.4 = (bf16[2,1,8,128,128]{4,3,2,1,0:T(8,128)(2,1)}, bf16[2,1,8,128,128]{4,3,2,1,0:T(8,128)(2,1)}, u32[]{:S(2)}, u32[]{:S(2)}) collective-permute-start(bf16[2,1,8,128,128]{4,3,2,1,0:T(8,128)(2,1)} %get-tuple-element.101), channel_id=1, source_target_pairs={{0,24},{8,0},{16,8},{24,16},{1,25},{9,1},{17,9},{25,17},{2,26},{10... | collective-permute-start | bytes 1572872 | tf_op jit(solution)/shard_map/ppermute | solution.py:22
  31.8 15.0 %collective-permute-start.5 = (bf16[2,1,8,128,128]{4,3,2,1,0:T(8,128)(2,1)}, bf16[2,1,8,128,128]{4,3,2,1,0:T(8,128)(2,1)}, u32[]{:S(2)}, u32[]{:S(2)}) collective-permute-start(bf16[2,1,8,128,128]{4,3,2,1,0:T(8,128)(2,1)} %get-tuple-element.100), channel_id=1, source_target_pairs={{0,8},{8,16},{16,24},{24,0},{1,9},{9,17},{17,25},{25,1},{2,10},{10... | collective-permute-start | bytes 1572872 | tf_op jit(solution)/shard_map/ppermute | solution.py:22
  49.5 26.6 %collective-permute-start.8 = (bf16[2,1,8,256,128]{4,3,2,1,0:T(8,128)(2,1)S(1)}, bf16[2,1,8,256,128]{4,3,2,1,0:T(8,128)(2,1)S(1)}, u32[]{:S(2)}, u32[]{:S(2)}) collective-permute-start(bf16[2,1,8,256,128]{4,3,2,1,0:T(8,128)(2,1)S(1)} %get-tuple-element.99), channel_id=1, source_target_pairs={{0,24},{8,0},{16,8},{24,16},{1,25},{9,1},{17,9},{25,17},{2,26},{10... | collective-permute-start | bytes 3145736 | tf_op jit(solution)/shard_map/ppermute | solution.py:22
  52.6 25.1 %collective-permute-start.9 = (bf16[2,1,8,256,128]{4,3,2,1,0:T(8,128)(2,1)S(1)}, bf16[2,1,8,256,128]{4,3,2,1,0:T(8,128)(2,1)S(1)}, u32[]{:S(2)}, u32[]{:S(2)}) collective-permute-start(bf16[2,1,8,256,128]{4,3,2,1,0:T(8,128)(2,1)S(1)} %get-tuple-element.98), channel_id=1, source_target_pairs={{0,8},{8,16},{16,24},{24,0},{1,9},{9,17},{17,25},{25,1},{2,10},{10... | collective-permute-start | bytes 3145736 | tf_op jit(solution)/shard_map/ppermute | solution.py:22
  54.9 19.5 %collective-permute-start.7 = (bf16[12,256,128]{2,1,0:T(8,128)(2,1)S(1)}, bf16[12,256,128]{2,1,0:T(8,128)(2,1)S(1)}, u32[]{:S(2)}, u32[]{:S(2)}) collective-permute-start(bf16[12,256,128]{2,1,0:T(8,128)(2,1)S(1)} %pad_maximum_fusion.4), channel_id=1, source_target_pairs={{0,1},{1,2},{2,3},{3,4},{4,5},{5,6},{6,7},{7,0},{8,9},{9,10},{10,1... | collective-permute-start | bytes 2359304 | tf_op jit(solution)/shard_map/ppermute | solution.py:22
  57.3 18.8 %collective-permute-start.6 = (bf16[12,256,128]{2,1,0:T(8,128)(2,1)S(1)}, bf16[12,256,128]{2,1,0:T(8,128)(2,1)S(1)}, u32[]{:S(2)}, u32[]{:S(2)}) collective-permute-start(bf16[12,256,128]{2,1,0:T(8,128)(2,1)S(1)} %pad_maximum_fusion.3), channel_id=1, source_target_pairs={{0,7},{1,0},{2,1},{3,2},{4,3},{5,4},{6,5},{7,6},{8,15},{9,8},{10,9... | collective-permute-start | bytes 2359304 | tf_op jit(solution)/shard_map/ppermute | solution.py:22
  78.6 18.5 %collective-permute-start.11 = (bf16[12,256,128]{2,1,0:T(8,128)(2,1)S(1)}, bf16[12,256,128]{2,1,0:T(8,128)(2,1)S(1)}, u32[]{:S(2)}, u32[]{:S(2)}) collective-permute-start(bf16[12,256,128]{2,1,0:T(8,128)(2,1)S(1)} %pad_maximum_fusion.6), channel_id=1, source_target_pairs={{0,1},{1,2},{2,3},{3,4},{4,5},{5,6},{6,7},{7,0},{8,9},{9,10},{10,1... | collective-permute-start | bytes 2359304 | tf_op jit(solution)/shard_map/ppermute | solution.py:22
  79.0 18.2 %collective-permute-start.10 = (bf16[12,256,128]{2,1,0:T(8,128)(2,1)S(1)}, bf16[12,256,128]{2,1,0:T(8,128)(2,1)S(1)}, u32[]{:S(2)}, u32[]{:S(2)}) collective-permute-start(bf16[12,256,128]{2,1,0:T(8,128)(2,1)S(1)} %pad_maximum_fusion.5), channel_id=1, source_target_pairs={{0,7},{1,0},{2,1},{3,2},{4,3},{5,4},{6,5},{7,6},{8,15},{9,8},{10,9... | collective-permute-start | bytes 2359304 | tf_op jit(solution)/shard_map/ppermute | solution.py:22
  82.5 29.2 %collective-permute-start.14 = (bf16[4,1280,128]{2,1,0:T(8,128)(2,1)S(1)}, bf16[4,1280,128]{2,1,0:T(8,128)(2,1)S(1)}, u32[]{:S(2)}, u32[]{:S(2)}) collective-permute-start(bf16[4,1280,128]{2,1,0:T(8,128)(2,1)S(1)} %get-tuple-element.105.refs_0_), channel_id=1, source_target_pairs={{0,8},{8,16},{16,24},{24,0},{1,9},{9,17},{17,25},{25,1},{2,10},{10... | collective-permute-start | bytes 3932168 | tf_op jit(solution)/shard_map/ppermute | solution.py:22
  82.5 29.2 %collective-permute-start.15 = (bf16[4,1280,128]{2,1,0:T(8,128)(2,1)S(1)}, bf16[4,1280,128]{2,1,0:T(8,128)(2,1)S(1)}, u32[]{:S(2)}, u32[]{:S(2)}) collective-permute-start(bf16[4,1280,128]{2,1,0:T(8,128)(2,1)S(1)} %get-tuple-element.105.refs_0_), channel_id=1, source_target_pairs={{0,24},{8,0},{16,8},{24,16},{1,25},{9,1},{17,9},{25,17},{2,26},{10... | collective-permute-start | bytes 3932168 | tf_op jit(solution)/shard_map/ppermute | solution.py:22
  97.4 11.7 %collective-permute-start.12 = (bf16[8,256,128]{2,1,0:T(8,128)(2,1)S(1)}, bf16[8,256,128]{2,1,0:T(8,128)(2,1)S(1)}, u32[]{:S(2)}, u32[]{:S(2)}) collective-permute-start(bf16[8,256,128]{2,1,0:T(8,128)(2,1)S(1)} %fusion.2), channel_id=1, source_target_pairs={{0,7},{1,0},{2,1},{3,2},{4,3},{5,4},{6,5},{7,6},{8,15},{9,8},{10,9... | collective-permute-start | bytes 1572872 | tf_op jit(solution)/shard_map/ppermute | solution.py:22
  101.0 7.7 %collective-permute-start.13 = (bf16[4,256,128]{2,1,0:T(8,128)(2,1)S(1)}, bf16[4,256,128]{2,1,0:T(8,128)(2,1)S(1)}, u32[]{:S(2)}, u32[]{:S(2)}) collective-permute-start(bf16[4,256,128]{2,1,0:T(8,128)(2,1)S(1)} %slice.52), channel_id=1, source_target_pairs={{0,1},{1,2},{2,3},{3,4},{4,5},{5,6},{6,7},{7,0},{8,9},{9,10},{10,1... | collective-permute-start | bytes 786440 | tf_op jit(solution)/shard_map/ppermute | solution.py:22
  112.7 23.2 %collective-permute-start.16 = (bf16[4,768,128]{2,1,0:T(8,128)(2,1)}, bf16[4,768,128]{2,1,0:T(8,128)(2,1)}, u32[]{:S(2)}, u32[]{:S(2)}) collective-permute-start(bf16[4,768,128]{2,1,0:T(8,128)(2,1)} %pad_maximum_fusion.7.refs_1_), channel_id=1, source_target_pairs={{0,8},{8,16},{16,24},{24,0},{1,9},{9,17},{17,25},{25,1},{2,10},{10... | collective-permute-start | bytes 2359304 | tf_op jit(solution)/shard_map/ppermute | solution.py:22
  112.9 23.0 %collective-permute-start.17 = (bf16[4,768,128]{2,1,0:T(8,128)(2,1)}, bf16[4,768,128]{2,1,0:T(8,128)(2,1)}, u32[]{:S(2)}, u32[]{:S(2)}) collective-permute-start(bf16[4,768,128]{2,1,0:T(8,128)(2,1)} %pad_maximum_fusion.7.refs_1_), channel_id=1, source_target_pairs={{0,24},{8,0},{16,8},{24,16},{1,25},{9,1},{17,9},{25,17},{2,26},{10... | collective-permute-start | bytes 2359304 | tf_op jit(solution)/shard_map/ppermute | solution.py:22
  117.0 18.8 %all-to-all-start = ((bf16[8,256,128]{2,1,0:T(8,128)(2,1)}), bf16[8,256,128]{2,1,0:T(8,128)(2,1)S(1)}, u32[]{:S(2)}, u32[]{:S(2)}) async-start(bf16[8,256,128]{2,1,0:T(8,128)(2,1)} %fusion.1), calls=%async_computation | async-start | bytes 1048576 | tf_op jit(solution)/shard_map/all_to_all | solution.py:40
  135.9 27.7 %all-to-all-start.1 = ((bf16[16,256,128]{2,1,0:T(8,128)(2,1)}), bf16[16,256,128]{2,1,0:T(8,128)(2,1)S(1)}, u32[]{:S(2)}, u32[]{:S(2)}) async-start(bf16[16,256,128]{2,1,0:T(8,128)(2,1)} %bitcast.20), calls=%async_computation.1 | async-start | bytes 2097152 | tf_op jit(solution)/shard_map/all_to_all | solution.py:40
  140.3 35.3 %collective-permute-start.19 = (bf16[4,1280,128]{2,1,0:T(8,128)(2,1)}, bf16[4,1280,128]{2,1,0:T(8,128)(2,1)S(1)}, u32[]{:S(2)}, u32[]{:S(2)}) collective-permute-start(bf16[4,1280,128]{2,1,0:T(8,128)(2,1)} %copy-done.11), channel_id=1, source_target_pairs={{0,8},{8,16},{16,24},{24,0},{1,9},{9,17},{17,25},{25,1},{2,10},{10... | collective-permute-start | bytes 3932168 | tf_op jit(solution)/shard_map/ppermute | solution.py:22
  142.9 15.1 %collective-permute-start.18 = (f32[128,512]{1,0:T(8,128)S(1)}, f32[128,512]{1,0:T(8,128)S(1)}, u32[]{:S(2)}, u32[]{:S(2)}) collective-permute-start(f32[128,512]{1,0:T(8,128)S(1)} %add.164), channel_id=1, source_target_pairs={{0,128},{128,0},{1,129},{129,1},{2,130},{130,2},{3,131},{131,3},{4... | collective-permute-start | bytes 786440 | tf_op jit(solution)/shard_map/ppermute | solution.py:318
  143.7 32.0 %collective-permute-start.20 = (bf16[4,768,128]{2,1,0:T(8,128)(2,1)}, bf16[4,768,128]{2,1,0:T(8,128)(2,1)}, u32[]{:S(2)}, u32[]{:S(2)}) collective-permute-start(bf16[4,768,128]{2,1,0:T(8,128)(2,1)} %collective-permute-done.17.refs_5_), channel_id=1, source_target_pairs={{0,24},{8,0},{16,8},{24,16},{1,25},{9,1},{17,9},{25,17},{2,26},{10... | collective-permute-start | bytes 2359304 | tf_op jit(solution)/shard_map/ppermute | solution.py:22
  166.0 25.0 %all-to-all-start.2 = ((f32[64,1,128]{2,1,0:T(1,128)}), f32[64,1,128]{2,1,0:T(1,128)S(1)}, u32[]{:S(2)}, u32[]{:S(2)}) async-start(f32[64,1,128]{2,1,0:T(1,128)} %broadcast_in_dim.8), calls=%async_computation.2 | async-start | bytes 65536 | tf_op jit(solution)/shard_map/all_to_all | solution.py:329
  (13 other events, 104.0 us)

commit v6 on v5

--- a/solution.py
+++ b/solution.py
@@ -160,11 +160,14 @@
     )
 
 
-def late_kernel(steps, place, hidden, gain, cotangent, inverse, grad, keys_in, dots_in, after, *refs):
-    count = 2 * len(steps)
+def late_kernel(steps, place, hidden, gain, cotangent, inverse, keys_in, dots_in, after, *refs):
     del after
-    key_out, grad_hidden, held, sems, keys, dots, fresh = refs[count:]
+    grad_hbm, weights = refs[0], refs[1 : 1 + 2 * len(steps)]
+    outs = refs[1 + 2 * len(steps) :]
+    key_out, grad_hidden, held, sems, keys, dots, fresh, grad, done, load_sem, store_sems = outs
     width = hidden.shape[1]
+    load = pltpu.make_async_copy(grad_hbm, grad, load_sem)
+    load.start()
     keys[...] = keys_in[...]
     dots[...] = dots_in[...]
 
@@ -173,33 +176,37 @@
         fresh[:, pl.ds(pl.multiple_of(at, LANES), LANES)] = weighted
 
     use_blocks(
-        steps, place, hidden, gain, cotangent, inverse, refs[:count], held, sems, keys, dots, keep
+        steps, place, hidden, gain, cotangent, inverse, weights, held, sems, keys, dots, keep
     )
     key_out[...] = keys[...].astype(BF16)
     mean = jnp.sum(dots[...], axis=-1, keepdims=True) / width
     inv = inverse[:, :1]
-
-    def result(at, weighted):
-        normed = hidden[:, at].astype(F32) * inv
-        grad_hidden[:, at] = (inv * (weighted - normed * mean)).astype(BF16)
-
-    def early(i, carry):
-        at = pl.ds(pl.multiple_of(i * 512, 512), 512)
-        result(at, grad[:, at])
-        return carry
-
-    lax.fori_loop(0, width // 512, early, 0)
-
-    def late(i, carry):
-        y = (place[1] - steps[0]) & 3
-        at = pl.ds(pl.multiple_of((i // 2) * 4096 + y * 1024 + (i % 2) * 512, 512), 512)
-        result(at, fresh[:, pl.ds(pl.multiple_of(i * 512, 512), 512)])
-        return carry
-
-    lax.fori_loop(0, 4, late, 0)
-
-
-def rows_call(kernel, steps, outs, scratch, operands, weights, name):
+    y = (place[1] - steps[0]) & 3
+    load.wait()
+
+    stores = []
+    for quarter in range(4):
+
+        def finish(i, carry, quarter=quarter):
+            part = quarter * 4 + i
+            at = pl.ds(pl.multiple_of(part * 512, 512), 512)
+            here = (part // 8) * 1024 + (part % 2) * 512
+            new = fresh[:, pl.ds(pl.multiple_of(here, 512), 512)]
+            weighted = jnp.where((part // 2) % 4 == y, new, grad[:, at])
+            normed = hidden[:, at].astype(F32) * inv
+            lanes = pl.ds(pl.multiple_of(i * 512, 512), 512)
+            done[quarter, :, lanes] = (inv * (weighted - normed * mean)).astype(BF16)
+            return carry
+
+        lax.fori_loop(0, 4, finish, 0)
+        there = grad_hidden.at[:, pl.ds(quarter * 2048, 2048)]
+        stores.append(pltpu.make_async_copy(done.at[quarter], there, store_sems.at[quarter]))
+        stores[-1].start()
+    for store in stores:
+        store.wait()
+
+
+def rows_call(kernel, steps, outs, out_specs, scratch, operands, weights, name):
     hidden, cotangent = operands[1], operands[3]
     tokens, width = hidden.shape
     keys = cotangent.shape[1]
@@ -210,7 +217,7 @@
         in_specs=[pl.BlockSpec(memory_space=pltpu.SMEM)]
         + [vmem] * (len(operands) - 1)
         + [pl.BlockSpec(memory_space=pl.ANY)] * len(weights),
-        out_specs=(vmem,) * len(outs),
+        out_specs=out_specs,
         scratch_shapes=[
             pltpu.VMEM((len(steps), width // 4, keys), BF16),
             pltpu.SemaphoreType.DMA((len(steps),)),
@@ -299,25 +306,27 @@
     z5, z3 = left[sums:], right[sums:]
     left = shift(added(part_a, "z", 2, -1, left[:sums]), "z", -1)
     z4 = shift(z3, "z", 1)
-    left, right, z4, first1, first3, b_left, b_right, core = together(
-        left, right, z4, first1, first3, b_left, b_right, core
-    )
+    sum_b = term(part_b, "y", 1, 0).astype(F32) + b_left.astype(F32) + b_right.astype(F32)
+    sum_b = exchange_sum(sum_b.reshape(-1, cut, rows), ("xh", "z"))
+    left, right, z4, first1, first3, core = together(left, right, z4, first1, first3, core)
 
     second = jnp.concatenate([z3, z5, z4], axis=1)
     second1, second3 = shift(second, "y", 1), shift(second, "y", -1)
+    both = mine + core
+    summed = both + lax.ppermute(both, "xl", [(0, 1), (1, 0)])
+    moment = lax.dynamic_index_in_dim(outer_momentum, chosen, 0, keepdims=False)
+    new_params, new_momentum = outer_step(current, moment, summed / 4.0)
     sum_a = term(part_a, "z", 2, 0).reshape(left.shape).astype(F32)
     sum_a = sum_a + left.astype(F32) + right[:sums].astype(F32)
-    sum_a = exchange_sum(sum_a.reshape(-1, cut, rows), ("xh", "y"))
-    sum_b = term(part_b, "y", 1, 0).astype(F32) + b_left.astype(F32) + b_right.astype(F32)
-    sum_b = sum_b.reshape(-1, cut, rows).astype(BF16)
+    sum_a = sum_a.reshape(-1, cut, rows).astype(BF16)
     first2 = shift(first1, "y", 1)
-    sum_a, sum_b, second1, second3, core = together(sum_a, sum_b, second1, second3, core)
+    sum_a, sum_b, second1, second3, new_params, new_momentum = together(
+        sum_a, sum_b, second1, second3, new_params, new_momentum
+    )
 
     second2 = shift(second3, "y", -1)
-    both = mine + core
-    summed = both + lax.ppermute(both, "xl", [(0, 1), (1, 0)])
-    sum_b = exchange_sum(sum_b, ("xh", "z"))
-    sum_b, summed = together(sum_b, summed)
+    sum_a = exchange_sum(sum_a, ("xh", "y"))
+    sum_a, first2, second2 = together(sum_a, first2, second2)
 
     grad_weight = jnp.concatenate([sum_a.T, sum_b.T], axis=-1) * factor
 
@@ -329,6 +338,7 @@
     grad_gain = lax.all_to_all(
         jnp.broadcast_to(own_sum[None], (devices, rows)), GROUP, 0, 0, tiled=True
     ).reshape(-1)
+    vmem = pl.BlockSpec(memory_space=pltpu.VMEM)
     keys = cotangent.shape[1]
     tokens, features = hidden.shape
     operands = (place, hidden, norm_gain, cotangent, inverse)
@@ -340,6 +350,7 @@
             jax.ShapeDtypeStruct((tokens, keys), F32),
             jax.ShapeDtypeStruct((tokens, LANES), F32),
         ),
+        (vmem,) * 3,
         (),
         operands,
         (first, second, first1, second1, first3, second3),
@@ -353,18 +364,21 @@
             jax.ShapeDtypeStruct((tokens, keys), BF16),
             jax.ShapeDtypeStruct((tokens, features), BF16),
         ),
+        (vmem, pl.BlockSpec(memory_space=pl.ANY)),
         (
             pltpu.VMEM((tokens, keys), F32),
             pltpu.VMEM((tokens, LANES), F32),
             pltpu.VMEM((tokens, features // 4), F32),
-        ),
-        (*operands, *partial, own_sum[None]),
-        (first2, second2),
+            pltpu.VMEM((tokens, features), F32),
+            pltpu.VMEM((4, tokens, features // 4), BF16),
+            pltpu.SemaphoreType.DMA,
+            pltpu.SemaphoreType.DMA((4,)),
+        ),
+        (*operands, *partial[1:], own_sum[None]),
+        (partial[0], first2, second2),
         "late_rows",
     )
 
-    moment = lax.dynamic_index_in_dim(outer_momentum, chosen, 0, keepdims=False)
-    new_params, new_momentum = outer_step(current, moment, summed / 4.0)
     return (
         key_out[None],
         grad_weight[None],

time: 193 us -> 212 us (1.098)
  waiting for transfers between devices: 72.2 us -> 95.2 us
  starting transfers between devices: 51.4 us -> 43.6 us
  other arithmetic: 16.2 us -> 19.3 us
    ppermute x19, waiting for transfers between devices: 54.5 us -> 80.4 us  [shift(): return lax.ppermute(value, axis, [(i, (i + step) % n) for i in range(n)])]
    ppermute x19, starting transfers between devices: 34.6 us -> 27 us  [shift(): return lax.ppermute(value, axis, [(i, (i + step) % n) for i in range(n)])]
    all_to_all x2, waiting for transfers between devices: 17.7 us -> 11.9 us  [exchange_sum(): blocks = lax.all_to_all(part.astype(BF16), axes, 0, 0, tiled=True)]
    ppermute x1, waiting for transfers between devices: 0.01 us -> 2.85 us  [per_device(): summed = both + lax.ppermute(both, 'xl', [(0, 1), (1, 0)])]
  transfers between devices with their start and end apart: 24 -> 24, of which waited for: 12 -> 14; matrix products, arithmetic and copies ran while one was open for 9% -> 9% of each run, Pallas kernels for 19% -> 17%
where the time goes in v6:
time: 212 us; the launch traced here: 210 us
  waiting for transfers between devices  95.2 us (45%)
  starting transfers between devices  43.6 us (21%)
  Pallas kernels  36.4 us (17%)
  other arithmetic  19.3 us (9%)
  local copies, waits for them, and re-layouts  14.2 us (7%)
    ppermute x19, waiting for transfers between devices, shift(): return lax.ppermute(value, axis, [(i, (i + step) % n) for i in range(n)])  80.4 us
    ppermute x19, starting transfers between devices, shift(): return lax.ppermute(value, axis, [(i, (i + step) % n) for i in range(n)])  27 us
    pallas_call x2, Pallas kernels, rows_call(): pl.pallas_call(functools.partial(kernel, steps), out_shape=outs, in_specs...  26.3 us
    all_to_all x2, waiting for transfers between devices, exchange_sum(): blocks = lax.all_to_all(part.astype(BF16), axes, 0, 0, tiled=True)  11.9 us
    pallas_call x1, Pallas kernels, weight_grad(): pl.pallas_call(weight_grad_kernel, grid=(blocks // per_step,), out_shape=...  10.1 us
    all_to_all x2, starting transfers between devices, exchange_sum(): blocks = lax.all_to_all(part.astype(BF16), axes, 0, 0, tiled=True)  8.17 us
    all_to_all x1, starting transfers between devices, per_device(): lax.all_to_all(jnp.broadcast_to(own_sum[None], (devices, rows)), GROUP, 0...  6.85 us
    convert_element_type x6, other arithmetic, added(): return (mine.astype(F32) + received.astype(F32)).astype(BF16)  5.58 us
  transfers between devices with their start and end apart: 24, of which 14 were waited for; matrix products, arithmetic and copies ran while one was open for 9% of the time, Pallas kernels for 17%

profile of v6, /device:TPU:2, one launch (start us, length us, event | category | flops | bytes accessed | tf_op | source)
XLA Modules:
  0.0 210.4 jit_solution(16334586932509608365)
XLA Ops:
  5.8 10.1 %weight_grad.1 = (bf16[64,256,128]{2,1,0:T(8,128)(2,1)}, bf16[64,256,128]{2,1,0:T(8,128)(2,1)}, f32[256,128]{1,0:T(8,128)}) custom-call(bf16[256,8192]{1,0:T(8,128)(2,1)} %bitcast.63, f32[1,8192]{1,0:T(1,128)} %gain.5, bf16[256,512]{1,0:T(8,128)(2,1)} %bitcast.75), custom_call_target="tpu_custom_call" | custom-call | flops 2147483648 | bytes 23068672 | tf_op jit(solution)/shard_map/weight_grad/pallas_call | solution.py:81
  20.5 5.9 %collective-permute-start.2 = (bf16[12,256,128]{2,1,0:T(8,128)(2,1)}, bf16[12,256,128]{2,1,0:T(8,128)(2,1)}, u32[]{:S(2)}, u32[]{:S(2)}) collective-permute-start(bf16[12,256,128]{2,1,0:T(8,128)(2,1)} %get-tuple-element.111), channel_id=1, source_target_pairs={{0,7},{1,0},{2,1},{3,2},{4,3},{5,4},{6,5},{7,6},{8,15},{9,8},{10,9... | collective-permute-start | bytes 2359304 | tf_op jit(solution)/shard_map/ppermute | solution.py:22
  28.7 3.0 %collective-permute-start.4 = (bf16[2,1,8,128,128]{4,3,2,1,0:T(8,128)(2,1)}, bf16[2,1,8,128,128]{4,3,2,1,0:T(8,128)(2,1)}, u32[]{:S(2)}, u32[]{:S(2)}) collective-permute-start(bf16[2,1,8,128,128]{4,3,2,1,0:T(8,128)(2,1)} %get-tuple-element.99), channel_id=1, source_target_pairs={{0,24},{8,0},{16,8},{24,16},{1,25},{9,1},{17,9},{25,17},{2,26},{10... | collective-permute-start | bytes 1572872 | tf_op jit(solution)/shard_map/ppermute | solution.py:22
  31.8 11.6 %collective-permute-done.4 = bf16[2,1,8,128,128]{4,3,2,1,0:T(8,128)(2,1)} collective-permute-done((bf16[2,1,8,128,128]{4,3,2,1,0:T(8,128)(2,1)}, bf16[2,1,8,128,128]{4,3,2,1,0:T(8,128)(2,1)}, u32[]{:S(2)}, u32[]{:S(2)}) %collective-permute-start.4) | collective-permute-done | bytes 524320 | tf_op jit(solution)/shard_map/ppermute | solution.py:22
  43.3 3.4 %collective-permute-done.5 = bf16[2,1,8,128,128]{4,3,2,1,0:T(8,128)(2,1)} collective-permute-done((bf16[2,1,8,128,128]{4,3,2,1,0:T(8,128)(2,1)}, bf16[2,1,8,128,128]{4,3,2,1,0:T(8,128)(2,1)}, u32[]{:S(2)}, u32[]{:S(2)}) %collective-permute-start.5) | collective-permute-done | bytes 524320 | tf_op jit(solution)/shard_map/ppermute | solution.py:22
  50.9 2.5 %collective-permute-start.6 = (bf16[12,256,128]{2,1,0:T(8,128)(2,1)S(1)}, bf16[12,256,128]{2,1,0:T(8,128)(2,1)S(1)}, u32[]{:S(2)}, u32[]{:S(2)}) collective-permute-start(bf16[12,256,128]{2,1,0:T(8,128)(2,1)S(1)} %pad_maximum_fusion.3), channel_id=1, source_target_pairs={{0,7},{1,0},{2,1},{3,2},{4,3},{5,4},{6,5},{7,6},{8,15},{9,8},{10,9... | collective-permute-start | bytes 2359304 | tf_op jit(solution)/shard_map/ppermute | solution.py:22
  59.1 10.4 %collective-permute-done.6 = bf16[12,256,128]{2,1,0:T(8,128)(2,1)S(1)} collective-permute-done((bf16[12,256,128]{2,1,0:T(8,128)(2,1)S(1)}, bf16[12,256,128]{2,1,0:T(8,128)(2,1)S(1)}, u32[]{:S(2)}, u32[]{:S(2)}) %collective-permute-start.6) | collective-permute-done | bytes 786464 | tf_op jit(solution)/shard_map/ppermute | solution.py:22
  69.5 7.3 %collective-permute-done.7 = bf16[12,256,128]{2,1,0:T(8,128)(2,1)S(1)} collective-permute-done((bf16[12,256,128]{2,1,0:T(8,128)(2,1)S(1)}, bf16[12,256,128]{2,1,0:T(8,128)(2,1)S(1)}, u32[]{:S(2)}, u32[]{:S(2)}) %collective-permute-start.7) | collective-permute-done | bytes 786464 | tf_op jit(solution)/shard_map/ppermute | solution.py:22
  78.4 2.7 %collective-permute-done.9 = bf16[2,1,8,256,128]{4,3,2,1,0:T(8,128)(2,1)S(1)} collective-permute-done((bf16[2,1,8,256,128]{4,3,2,1,0:T(8,128)(2,1)S(1)}, bf16[2,1,8,256,128]{4,3,2,1,0:T(8,128)(2,1)S(1)}, u32[]{:S(2)}, u32[]{:S(2)}) %collective-permute-start.9) | collective-permute-done | bytes 1048608 | tf_op jit(solution)/shard_map/ppermute | solution.py:22
  86.3 3.2 %collective-permute-start.15 = (bf16[4,1280,128]{2,1,0:T(8,128)(2,1)}, bf16[4,1280,128]{2,1,0:T(8,128)(2,1)}, u32[]{:S(2)}, u32[]{:S(2)}) collective-permute-start(bf16[4,1280,128]{2,1,0:T(8,128)(2,1)} %copy-done.11), channel_id=1, source_target_pairs={{0,24},{8,0},{16,8},{24,16},{1,25},{9,1},{17,9},{25,17},{2,26},{10... | collective-permute-start | bytes 3932168 | tf_op jit(solution)/shard_map/ppermute | solution.py:22
  89.5 2.6 %add_convert_fusion = bf16[2,1,8,256,128]{4,3,2,1,0:T(8,128)(2,1)} fusion(bf16[2,1,8,256,128]{4,3,2,1,0:T(8,128)(2,1)S(1)} %copy-done.5, bf16[2,1,8,256,128]{4,3,2,1,0:T(8,128)(2,1)S(1)} %copy-done.3, bf16[2,4,8,256,128]{4,3,2,1,0:T(8,128)(2,1)} %bitcast.60, s32[]{:T(128)S(6)} %select_n.57), kind=kLoop, calls=%fused_computation.1 | loop fusion | flops 3145728 | bytes 4194308 | tf_op jit(solution)/shard_map/convert_element_type | solution.py:40
  92.1 4.0 %all-to-all-start = ((bf16[16,256,128]{2,1,0:T(8,128)(2,1)}), bf16[16,256,128]{2,1,0:T(8,128)(2,1)S(1)}, u32[]{:S(2)}, u32[]{:S(2)}) async-start(bf16[16,256,128]{2,1,0:T(8,128)(2,1)} %bitcast.20), calls=%async_computation | async-start | bytes 2097152 | tf_op jit(solution)/shard_map/all_to_all | solution.py:40
  96.2 12.6 %collective-permute-done.10 = bf16[12,256,128]{2,1,0:T(8,128)(2,1)} collective-permute-done((bf16[12,256,128]{2,1,0:T(8,128)(2,1)}, bf16[12,256,128]{2,1,0:T(8,128)(2,1)}, u32[]{:S(2)}, u32[]{:S(2)}) %collective-permute-start.10) | collective-permute-done | bytes 786464 | tf_op jit(solution)/shard_map/ppermute | solution.py:22
  108.8 8.3 %collective-permute-done.11 = bf16[12,256,128]{2,1,0:T(8,128)(2,1)} collective-permute-done((bf16[12,256,128]{2,1,0:T(8,128)(2,1)}, bf16[12,256,128]{2,1,0:T(8,128)(2,1)}, u32[]{:S(2)}, u32[]{:S(2)}) %collective-permute-start.11) | collective-permute-done | bytes 786464 | tf_op jit(solution)/shard_map/ppermute | solution.py:22
  122.4 8.7 %collective-permute-done.13 = bf16[4,256,128]{2,1,0:T(8,128)(2,1)S(1)} collective-permute-done((bf16[4,256,128]{2,1,0:T(8,128)(2,1)S(1)}, bf16[4,256,128]{2,1,0:T(8,128)(2,1)S(1)}, u32[]{:S(2)}, u32[]{:S(2)}) %collective-permute-start.13) | collective-permute-done | bytes 262176 | tf_op jit(solution)/shard_map/ppermute | solution.py:22
  131.1 3.2 %collective-permute-done.12 = bf16[8,256,128]{2,1,0:T(8,128)(2,1)S(1)} collective-permute-done((bf16[8,256,128]{2,1,0:T(8,128)(2,1)S(1)}, bf16[8,256,128]{2,1,0:T(8,128)(2,1)S(1)}, u32[]{:S(2)}, u32[]{:S(2)}) %collective-permute-start.12) | collective-permute-done | bytes 524320 | tf_op jit(solution)/shard_map/ppermute | solution.py:22
  135.3 3.2 %collective-permute-start.17 = (bf16[4,768,128]{2,1,0:T(8,128)(2,1)}, bf16[4,768,128]{2,1,0:T(8,128)(2,1)}, u32[]{:S(2)}, u32[]{:S(2)}) collective-permute-start(bf16[4,768,128]{2,1,0:T(8,128)(2,1)} %pad_maximum_fusion.7.refs_1_), channel_id=1, source_target_pairs={{0,24},{8,0},{16,8},{24,16},{1,25},{9,1},{17,9},{25,17},{2,26},{10... | collective-permute-start | bytes 2359304 | tf_op jit(solution)/shard_map/ppermute | solution.py:22
  142.2 2.8 %collective-permute-done.18 = f32[128,512]{1,0:T(8,128)S(1)} collective-permute-done((f32[128,512]{1,0:T(8,128)S(1)}, f32[128,512]{1,0:T(8,128)S(1)}, u32[]{:S(2)}, u32[]{:S(2)}) %collective-permute-start.18) | collective-permute-done | bytes 262176 | tf_op jit(solution)/shard_map/ppermute | solution.py:316
  147.1 10.2 %collective-permute-done.16.refs_3_ = bf16[4,768,128]{2,1,0:T(8,128)(2,1)} collective-permute-done((bf16[4,768,128]{2,1,0:T(8,128)(2,1)}, bf16[4,768,128]{2,1,0:T(8,128)(2,1)}, u32[]{:S(2)}, u32[]{:S(2)}) %collective-permute-start.16) | collective-permute-done | bytes 786464 | tf_op jit(solution)/shard_map/ppermute | solution.py:22
  157.3 4.1 %all-to-all-start.1 = ((bf16[8,256,128]{2,1,0:T(8,128)(2,1)}), bf16[8,256,128]{2,1,0:T(8,128)(2,1)S(1)}, u32[]{:S(2)}, u32[]{:S(2)}) async-start(bf16[8,256,128]{2,1,0:T(8,128)(2,1)} %fusion.1), calls=%async_computation.1 | async-start | bytes 1048576 | tf_op jit(solution)/shard_map/all_to_all | solution.py:40
  162.1 12.9 %early_rows.1 = (f32[256,8192]{1,0:T(8,128)}, f32[256,512]{1,0:T(8,128)}, f32[256,128]{1,0:T(8,128)}) custom-call(s32[3]{0:T(128)} %pad_add_fusion.place, bf16[256,8192]{1,0:T(8,128)(2,1)} %bitcast.64, f32[1,8192]{1,0:T(1,128)} %gain.5, bf16[256,512]{1,0:T(8,128)(2,1)} %bitcast.76, f32[256,128]{1,0:T(8,128)} %get-tuple-element.47.inverse, ...), custom_call_target="tpu_custom_call" | custom-call | flops 3221225472 | bytes 18874368 | tf_op jit(solution)/shard_map/early_rows/pallas_call | solution.py:214
  175.0 11.8 %all-to-all-done.1 = bf16[8,256,128]{2,1,0:T(8,128)(2,1)S(1)} async-done(((bf16[8,256,128]{2,1,0:T(8,128)(2,1)}), bf16[8,256,128]{2,1,0:T(8,128)(2,1)S(1)}, u32[]{:S(2)}, u32[]{:S(2)}) %all-to-all-start.1) | async-done | bytes 524320 | tf_op jit(solution)/shard_map/all_to_all | solution.py:40
  189.4 6.8 %all-to-all-start.2 = ((f32[64,1,128]{2,1,0:T(1,128)}), f32[64,1,128]{2,1,0:T(1,128)S(1)}, u32[]{:S(2)}, u32[]{:S(2)}) async-start(f32[64,1,128]{2,1,0:T(1,128)} %broadcast_in_dim.8), calls=%async_computation.2 | async-start | bytes 65536 | tf_op jit(solution)/shard_map/all_to_all | solution.py:338
  196.3 13.4 %late_rows.1 = (bf16[256,512]{1,0:T(8,128)(2,1)}, bf16[256,8192]{1,0:T(8,128)(2,1)}) custom-call(s32[3]{0:T(128)} %pad_add_fusion.place, bf16[256,8192]{1,0:T(8,128)(2,1)} %bitcast.65, f32[1,8192]{1,0:T(1,128)} %gain.5, bf16[256,512]{1,0:T(8,128)(2,1)} %bitcast.77, f32[256,128]{1,0:T(8,128)} %get-tuple-element.47.inverse, ...), custom_call_target="tpu_custom_call" | custom-call | flops 1073741824 | bytes 14680064 | tf_op jit(solution)/shard_map/late_rows/pallas_call | solution.py:214
  (91 shorter events, 43.7 us)
Async XLA Ops:
  2.4 13.6 %collective-permute-start.1 = (f32[128,512]{1,0:T(8,128)S(1)}, f32[128,512]{1,0:T(8,128)S(1)}, u32[]{:S(2)}, u32[]{:S(2)}) collective-permute-start(f32[128,512]{1,0:T(8,128)S(1)} %bitcast_subtract_fusion), channel_id=1, source_target_pairs={{0,64},{64,0},{1,65},{65,1},{2,66},{66,2},{3,67},{67,3},{4,68},{68... | collective-permute-start | bytes 786440 | tf_op jit(solution)/shard_map/ppermute | solution.py:271
  3.6 12.3 %collective-permute-start = (bf16[4,128,128]{2,1,0:T(8,128)(2,1)S(1)}, bf16[4,128,128]{2,1,0:T(8,128)(2,1)S(1)}, u32[]{:S(2)}, u32[]{:S(2)}) collective-permute-start(bf16[4,128,128]{2,1,0:T(8,128)(2,1)S(1)} %bitcast.68), channel_id=1, source_target_pairs={{0,32},{32,0},{1,33},{33,1},{2,34},{34,2},{3,35},{35,3},{4,36},{36... | collective-permute-start | bytes 393224 | tf_op jit(solution)/shard_map/ppermute | solution.py:22
  20.5 26.3 %collective-permute-start.2 = (bf16[12,256,128]{2,1,0:T(8,128)(2,1)}, bf16[12,256,128]{2,1,0:T(8,128)(2,1)}, u32[]{:S(2)}, u32[]{:S(2)}) collective-permute-start(bf16[12,256,128]{2,1,0:T(8,128)(2,1)} %get-tuple-element.111), channel_id=1, source_target_pairs={{0,7},{1,0},{2,1},{3,2},{4,3},{5,4},{6,5},{7,6},{8,15},{9,8},{10,9... | collective-permute-start | bytes 2359304 | tf_op jit(solution)/shard_map/ppermute | solution.py:22
  26.4 20.9 %collective-permute-start.3 = (bf16[12,256,128]{2,1,0:T(8,128)(2,1)}, bf16[12,256,128]{2,1,0:T(8,128)(2,1)}, u32[]{:S(2)}, u32[]{:S(2)}) collective-permute-start(bf16[12,256,128]{2,1,0:T(8,128)(2,1)} %get-tuple-element.110), channel_id=1, source_target_pairs={{0,1},{1,2},{2,3},{3,4},{4,5},{5,6},{6,7},{7,0},{8,9},{9,10},{10,1... | collective-permute-start | bytes 2359304 | tf_op jit(solution)/shard_map/ppermute | solution.py:22
  28.7 14.6 %collective-permute-start.4 = (bf16[2,1,8,128,128]{4,3,2,1,0:T(8,128)(2,1)}, bf16[2,1,8,128,128]{4,3,2,1,0:T(8,128)(2,1)}, u32[]{:S(2)}, u32[]{:S(2)}) collective-permute-start(bf16[2,1,8,128,128]{4,3,2,1,0:T(8,128)(2,1)} %get-tuple-element.99), channel_id=1, source_target_pairs={{0,24},{8,0},{16,8},{24,16},{1,25},{9,1},{17,9},{25,17},{2,26},{10... | collective-permute-start | bytes 1572872 | tf_op jit(solution)/shard_map/ppermute | solution.py:22
  31.7 15.0 %collective-permute-start.5 = (bf16[2,1,8,128,128]{4,3,2,1,0:T(8,128)(2,1)}, bf16[2,1,8,128,128]{4,3,2,1,0:T(8,128)(2,1)}, u32[]{:S(2)}, u32[]{:S(2)}) collective-permute-start(bf16[2,1,8,128,128]{4,3,2,1,0:T(8,128)(2,1)} %get-tuple-element.98), channel_id=1, source_target_pairs={{0,8},{8,16},{16,24},{24,0},{1,9},{9,17},{17,25},{25,1},{2,10},{10... | collective-permute-start | bytes 1572872 | tf_op jit(solution)/shard_map/ppermute | solution.py:22
  50.9 18.6 %collective-permute-start.6 = (bf16[12,256,128]{2,1,0:T(8,128)(2,1)S(1)}, bf16[12,256,128]{2,1,0:T(8,128)(2,1)S(1)}, u32[]{:S(2)}, u32[]{:S(2)}) collective-permute-start(bf16[12,256,128]{2,1,0:T(8,128)(2,1)S(1)} %pad_maximum_fusion.3), channel_id=1, source_target_pairs={{0,7},{1,0},{2,1},{3,2},{4,3},{5,4},{6,5},{7,6},{8,15},{9,8},{10,9... | collective-permute-start | bytes 2359304 | tf_op jit(solution)/shard_map/ppermute | solution.py:22
  55.1 23.3 %collective-permute-start.8 = (bf16[2,1,8,256,128]{4,3,2,1,0:T(8,128)(2,1)S(1)}, bf16[2,1,8,256,128]{4,3,2,1,0:T(8,128)(2,1)S(1)}, u32[]{:S(2)}, u32[]{:S(2)}) collective-permute-start(bf16[2,1,8,256,128]{4,3,2,1,0:T(8,128)(2,1)S(1)} %get-tuple-element.97), channel_id=1, source_target_pairs={{0,24},{8,0},{16,8},{24,16},{1,25},{9,1},{17,9},{25,17},{2,26},{10... | collective-permute-start | bytes 3145736 | tf_op jit(solution)/shard_map/ppermute | solution.py:22
  56.0 25.1 %collective-permute-start.9 = (bf16[2,1,8,256,128]{4,3,2,1,0:T(8,128)(2,1)S(1)}, bf16[2,1,8,256,128]{4,3,2,1,0:T(8,128)(2,1)S(1)}, u32[]{:S(2)}, u32[]{:S(2)}) collective-permute-start(bf16[2,1,8,256,128]{4,3,2,1,0:T(8,128)(2,1)S(1)} %get-tuple-element.96), channel_id=1, source_target_pairs={{0,8},{8,16},{16,24},{24,0},{1,9},{9,17},{17,25},{25,1},{2,10},{10... | collective-permute-start | bytes 3145736 | tf_op jit(solution)/shard_map/ppermute | solution.py:22
  58.5 18.4 %collective-permute-start.7 = (bf16[12,256,128]{2,1,0:T(8,128)(2,1)S(1)}, bf16[12,256,128]{2,1,0:T(8,128)(2,1)S(1)}, u32[]{:S(2)}, u32[]{:S(2)}) collective-permute-start(bf16[12,256,128]{2,1,0:T(8,128)(2,1)S(1)} %pad_maximum_fusion.4), channel_id=1, source_target_pairs={{0,1},{1,2},{2,3},{3,4},{4,5},{5,6},{6,7},{7,0},{8,9},{9,10},{10,1... | collective-permute-start | bytes 2359304 | tf_op jit(solution)/shard_map/ppermute | solution.py:22
  83.0 25.7 %collective-permute-start.10 = (bf16[12,256,128]{2,1,0:T(8,128)(2,1)}, bf16[12,256,128]{2,1,0:T(8,128)(2,1)}, u32[]{:S(2)}, u32[]{:S(2)}) collective-permute-start(bf16[12,256,128]{2,1,0:T(8,128)(2,1)} %pad_maximum_fusion.5), channel_id=1, source_target_pairs={{0,7},{1,0},{2,1},{3,2},{4,3},{5,4},{6,5},{7,6},{8,15},{9,8},{10,9... | collective-permute-start | bytes 2359304 | tf_op jit(solution)/shard_map/ppermute | solution.py:22
  84.5 32.5 %collective-permute-start.11 = (bf16[12,256,128]{2,1,0:T(8,128)(2,1)}, bf16[12,256,128]{2,1,0:T(8,128)(2,1)}, u32[]{:S(2)}, u32[]{:S(2)}) collective-permute-start(bf16[12,256,128]{2,1,0:T(8,128)(2,1)} %pad_maximum_fusion.6), channel_id=1, source_target_pairs={{0,1},{1,2},{2,3},{3,4},{4,5},{5,6},{6,7},{7,0},{8,9},{9,10},{10,1... | collective-permute-start | bytes 2359304 | tf_op jit(solution)/shard_map/ppermute | solution.py:22
  86.3 48.1 %collective-permute-start.14 = (bf16[4,1280,128]{2,1,0:T(8,128)(2,1)}, bf16[4,1280,128]{2,1,0:T(8,128)(2,1)}, u32[]{:S(2)}, u32[]{:S(2)}) collective-permute-start(bf16[4,1280,128]{2,1,0:T(8,128)(2,1)} %copy-done.11), channel_id=1, source_target_pairs={{0,8},{8,16},{16,24},{24,0},{1,9},{9,17},{17,25},{25,1},{2,10},{10... | collective-permute-start | bytes 3932168 | tf_op jit(solution)/shard_map/ppermute | solution.py:22
  86.3 48.1 %collective-permute-start.15 = (bf16[4,1280,128]{2,1,0:T(8,128)(2,1)}, bf16[4,1280,128]{2,1,0:T(8,128)(2,1)}, u32[]{:S(2)}, u32[]{:S(2)}) collective-permute-start(bf16[4,1280,128]{2,1,0:T(8,128)(2,1)} %copy-done.11), channel_id=1, source_target_pairs={{0,24},{8,0},{16,8},{24,16},{1,25},{9,1},{17,9},{25,17},{2,26},{10... | collective-permute-start | bytes 3932168 | tf_op jit(solution)/shard_map/ppermute | solution.py:22
  92.1 54.8 %all-to-all-start = ((bf16[16,256,128]{2,1,0:T(8,128)(2,1)}), bf16[16,256,128]{2,1,0:T(8,128)(2,1)S(1)}, u32[]{:S(2)}, u32[]{:S(2)}) async-start(bf16[16,256,128]{2,1,0:T(8,128)(2,1)} %bitcast.20), calls=%async_computation | async-start | bytes 2097152 | tf_op jit(solution)/shard_map/all_to_all | solution.py:40
  118.3 16.0 %collective-permute-start.12 = (bf16[8,256,128]{2,1,0:T(8,128)(2,1)S(1)}, bf16[8,256,128]{2,1,0:T(8,128)(2,1)S(1)}, u32[]{:S(2)}, u32[]{:S(2)}) collective-permute-start(bf16[8,256,128]{2,1,0:T(8,128)(2,1)S(1)} %fusion.2), channel_id=1, source_target_pairs={{0,7},{1,0},{2,1},{3,2},{4,3},{5,4},{6,5},{7,6},{8,15},{9,8},{10,9... | collective-permute-start | bytes 1572872 | tf_op jit(solution)/shard_map/ppermute | solution.py:22
  119.4 11.7 %collective-permute-start.13 = (bf16[4,256,128]{2,1,0:T(8,128)(2,1)S(1)}, bf16[4,256,128]{2,1,0:T(8,128)(2,1)S(1)}, u32[]{:S(2)}, u32[]{:S(2)}) collective-permute-start(bf16[4,256,128]{2,1,0:T(8,128)(2,1)S(1)} %slice.52), channel_id=1, source_target_pairs={{0,1},{1,2},{2,3},{3,4},{4,5},{5,6},{6,7},{7,0},{8,9},{9,10},{10,1... | collective-permute-start | bytes 786440 | tf_op jit(solution)/shard_map/ppermute | solution.py:22
  135.3 22.0 %collective-permute-start.16 = (bf16[4,768,128]{2,1,0:T(8,128)(2,1)}, bf16[4,768,128]{2,1,0:T(8,128)(2,1)}, u32[]{:S(2)}, u32[]{:S(2)}) collective-permute-start(bf16[4,768,128]{2,1,0:T(8,128)(2,1)} %pad_maximum_fusion.7.refs_1_), channel_id=1, source_target_pairs={{0,8},{8,16},{16,24},{24,0},{1,9},{9,17},{17,25},{25,1},{2,10},{10... | collective-permute-start | bytes 2359304 | tf_op jit(solution)/shard_map/ppermute | solution.py:22
  135.3 22.0 %collective-permute-start.17 = (bf16[4,768,128]{2,1,0:T(8,128)(2,1)}, bf16[4,768,128]{2,1,0:T(8,128)(2,1)}, u32[]{:S(2)}, u32[]{:S(2)}) collective-permute-start(bf16[4,768,128]{2,1,0:T(8,128)(2,1)} %pad_maximum_fusion.7.refs_1_), channel_id=1, source_target_pairs={{0,24},{8,0},{16,8},{24,16},{1,25},{9,1},{17,9},{25,17},{2,26},{10... | collective-permute-start | bytes 2359304 | tf_op jit(solution)/shard_map/ppermute | solution.py:22
  138.6 6.5 %collective-permute-start.18 = (f32[128,512]{1,0:T(8,128)S(1)}, f32[128,512]{1,0:T(8,128)S(1)}, u32[]{:S(2)}, u32[]{:S(2)}) collective-permute-start(f32[128,512]{1,0:T(8,128)S(1)} %add.164), channel_id=1, source_target_pairs={{0,128},{128,0},{1,129},{129,1},{2,130},{130,2},{3,131},{131,3},{4... | collective-permute-start | bytes 786440 | tf_op jit(solution)/shard_map/ppermute | solution.py:316
  140.1 46.8 %collective-permute-start.19 = (bf16[4,1280,128]{2,1,0:T(8,128)(2,1)}, bf16[4,1280,128]{2,1,0:T(8,128)(2,1)S(1)}, u32[]{:S(2)}, u32[]{:S(2)}) collective-permute-start(bf16[4,1280,128]{2,1,0:T(8,128)(2,1)} %collective-permute-done.14.refs_2_), channel_id=1, source_target_pairs={{0,8},{8,16},{16,24},{24,0},{1,9},{9,17},{17,25},{25,1},{2,10},{10... | collective-permute-start | bytes 3932168 | tf_op jit(solution)/shard_map/ppermute | solution.py:22
  157.3 29.7 %collective-permute-start.20 = (bf16[4,768,128]{2,1,0:T(8,128)(2,1)}, bf16[4,768,128]{2,1,0:T(8,128)(2,1)S(1)}, u32[]{:S(2)}, u32[]{:S(2)}) collective-permute-start(bf16[4,768,128]{2,1,0:T(8,128)(2,1)} %collective-permute-done.17.refs_5_), channel_id=1, source_target_pairs={{0,24},{8,0},{16,8},{24,16},{1,25},{9,1},{17,9},{25,17},{2,26},{10... | collective-permute-start | bytes 2359304 | tf_op jit(solution)/shard_map/ppermute | solution.py:22
  157.3 29.6 %all-to-all-start.1 = ((bf16[8,256,128]{2,1,0:T(8,128)(2,1)}), bf16[8,256,128]{2,1,0:T(8,128)(2,1)S(1)}, u32[]{:S(2)}, u32[]{:S(2)}) async-start(bf16[8,256,128]{2,1,0:T(8,128)(2,1)} %fusion.1), calls=%async_computation.1 | async-start | bytes 1048576 | tf_op jit(solution)/shard_map/all_to_all | solution.py:40
  189.4 20.3 %all-to-all-start.2 = ((f32[64,1,128]{2,1,0:T(1,128)}), f32[64,1,128]{2,1,0:T(1,128)S(1)}, u32[]{:S(2)}, u32[]{:S(2)}) async-start(f32[64,1,128]{2,1,0:T(1,128)} %broadcast_in_dim.8), calls=%async_computation.2 | async-start | bytes 65536 | tf_op jit(solution)/shard_map/all_to_all | solution.py:338
  (13 other events, 106.6 us)

commit v7 on v6

--- a/solution.py
+++ b/solution.py
@@ -306,27 +306,31 @@
     z5, z3 = left[sums:], right[sums:]
     left = shift(added(part_a, "z", 2, -1, left[:sums]), "z", -1)
     z4 = shift(z3, "z", 1)
-    sum_b = term(part_b, "y", 1, 0).astype(F32) + b_left.astype(F32) + b_right.astype(F32)
-    sum_b = exchange_sum(sum_b.reshape(-1, cut, rows), ("xh", "z"))
-    left, right, z4, first1, first3, core = together(left, right, z4, first1, first3, core)
+    left, right, z4, first1, first3, b_left, b_right, core = together(
+        left, right, z4, first1, first3, b_left, b_right, core
+    )
 
     second = jnp.concatenate([z3, z5, z4], axis=1)
     second1, second3 = shift(second, "y", 1), shift(second, "y", -1)
+    sum_a = term(part_a, "z", 2, 0).reshape(left.shape).astype(F32)
+    sum_a = sum_a + left.astype(F32) + right[:sums].astype(F32)
+    sum_a = exchange_sum(sum_a.reshape(-1, cut, rows), ("xh", "y"))
+    sum_b = term(part_b, "y", 1, 0).astype(F32) + b_left.astype(F32) + b_right.astype(F32)
+    at_x = lax.axis_index("xh")
+    away = lax.dynamic_slice_in_dim(sum_b, 1 - at_x, 1, 0).astype(BF16)
+    sum_b = lax.dynamic_slice_in_dim(sum_b, at_x, 1, 0) + shift(away, "xh", 1).astype(F32)
+    sum_b = sum_b.reshape(-1, cut, rows).astype(BF16)
     both = mine + core
     summed = both + lax.ppermute(both, "xl", [(0, 1), (1, 0)])
     moment = lax.dynamic_index_in_dim(outer_momentum, chosen, 0, keepdims=False)
     new_params, new_momentum = outer_step(current, moment, summed / 4.0)
-    sum_a = term(part_a, "z", 2, 0).reshape(left.shape).astype(F32)
-    sum_a = sum_a + left.astype(F32) + right[:sums].astype(F32)
-    sum_a = sum_a.reshape(-1, cut, rows).astype(BF16)
     first2 = shift(first1, "y", 1)
     sum_a, sum_b, second1, second3, new_params, new_momentum = together(
         sum_a, sum_b, second1, second3, new_params, new_momentum
     )
 
     second2 = shift(second3, "y", -1)
-    sum_a = exchange_sum(sum_a, ("xh", "y"))
-    sum_a, first2, second2 = together(sum_a, first2, second2)
+    sum_b = exchange_sum(sum_b, "z")
 
     grad_weight = jnp.concatenate([sum_a.T, sum_b.T], axis=-1) * factor
 

time: 212 us -> 196 us (0.925)
  waiting for transfers between devices: 95.2 us -> 59.6 us
  starting transfers between devices: 43.6 us -> 58.3 us
  local copies, waits for them, and re-layouts: 14.2 us -> 17.6 us
    ppermute x19 -> x20, waiting for transfers between devices: 80.4 us -> 56.2 us  [shift(): return lax.ppermute(value, axis, [(i, (i + step) % n) for i in range(n)])]
    ppermute x19 -> x20, starting transfers between devices: 27 us -> 38.4 us  [shift(): return lax.ppermute(value, axis, [(i, (i + step) % n) for i in range(n)])]
    all_to_all x2, waiting for transfers between devices: 11.9 us -> 3.39 us  [exchange_sum(): blocks = lax.all_to_all(part.astype(BF16), axes, 0, 0, tiled=True)]
    all_to_all x1, starting transfers between devices: 6.85 us -> 11.3 us  [per_device(): lax.all_to_all(jnp.broadcast_to(own_sum[None], (devices, rows)), GROUP, 0...]
    ppermute x1, waiting for transfers between devices: 2.85 us -> 0.01 us  [per_device(): summed = both + lax.ppermute(both, 'xl', [(0, 1), (1, 0)])]
    add x0 -> x1, other arithmetic: none -> 2.3 us  [per_device(): term(part_b, 'y', 1, 0).astype(F32) + b_left.astype(F32)]
    unnamed x31 -> x27, local copies, waits for them, and re-layouts: 4.07 us -> 5.88 us
  transfers between devices with their start and end apart: 24 -> 25, of which waited for: 14 -> 13; matrix products, arithmetic and copies ran while one was open for 9% -> 13% of each run, Pallas kernels for 17% -> 19%
where the time goes in v7:
time: 196 us; the launch traced here: 194 us
  waiting for transfers between devices  59.6 us (30%)
  starting transfers between devices  58.3 us (30%)
  Pallas kernels  36.5 us (19%)
  other arithmetic  20.3 us (10%)
  local copies, waits for them, and re-layouts  17.6 us (9%)
    ppermute x20, waiting for transfers between devices, shift(): return lax.ppermute(value, axis, [(i, (i + step) % n) for i in range(n)])  56.2 us
    ppermute x20, starting transfers between devices, shift(): return lax.ppermute(value, axis, [(i, (i + step) % n) for i in range(n)])  38.4 us
    pallas_call x2, Pallas kernels, rows_call(): pl.pallas_call(functools.partial(kernel, steps), out_shape=outs, in_specs...  26.4 us
    all_to_all x1, starting transfers between devices, per_device(): lax.all_to_all(jnp.broadcast_to(own_sum[None], (devices, rows)), GROUP, 0...  11.3 us
    pallas_call x1, Pallas kernels, weight_grad(): pl.pallas_call(weight_grad_kernel, grid=(blocks // per_step,), out_shape=...  10.1 us
    all_to_all x2, starting transfers between devices, exchange_sum(): blocks = lax.all_to_all(part.astype(BF16), axes, 0, 0, tiled=True)  6.99 us
    convert_element_type x6, other arithmetic, added(): return (mine.astype(F32) + received.astype(F32)).astype(BF16)  6.01 us
    unnamed x27, local copies, waits for them, and re-layouts  5.88 us
  transfers between devices with their start and end apart: 25, of which 13 were waited for; matrix products, arithmetic and copies ran while one was open for 13% of the time, Pallas kernels for 19%

profile of v7, /device:TPU:2, one launch (start us, length us, event | category | flops | bytes accessed | tf_op | source)
XLA Modules:
  0.0 193.9 jit_solution(11808875403314923396)
XLA Ops:
  5.9 10.1 %weight_grad.1 = (bf16[64,256,128]{2,1,0:T(8,128)(2,1)}, bf16[64,256,128]{2,1,0:T(8,128)(2,1)}, f32[256,128]{1,0:T(8,128)}) custom-call(bf16[256,8192]{1,0:T(8,128)(2,1)} %bitcast.64, f32[1,8192]{1,0:T(1,128)} %gain.5, bf16[256,512]{1,0:T(8,128)(2,1)} %bitcast.76), custom_call_target="tpu_custom_call" | custom-call | flops 2147483648 | bytes 23068672 | tf_op jit(solution)/shard_map/weight_grad/pallas_call | solution.py:81
  16.7 2.5 %constant_dynamic-slice_fusion.2 = (bf16[2,4,1,256,128]{4,3,1,0,2:T(8,128)(2,1)S(1)}, bf16[2,4,1,256,128]{4,3,1,0,2:T(8,128)(2,1)S(1)}, bf16[2,4,1,256,128]{4,3,...) fusion(s32[]{:T(128)S(6)} %select_n.62, ...), kind=kLoop, calls=%fused_computation.45 | loop fusion | bytes 8388640 | tf_op jit(solution)/shard_map/dynamic_slice | solution.py:31
  20.5 5.9 %collective-permute-start.2 = (bf16[12,256,128]{2,1,0:T(8,128)(2,1)}, bf16[12,256,128]{2,1,0:T(8,128)(2,1)}, u32[]{:S(2)}, u32[]{:S(2)}) collective-permute-start(bf16[12,256,128]{2,1,0:T(8,128)(2,1)} %get-tuple-element.109), channel_id=1, source_target_pairs={{0,7},{1,0},{2,1},{3,2},{4,3},{5,4},{6,5},{7,6},{8,15},{9,8},{10,9... | collective-permute-start | bytes 2359304 | tf_op jit(solution)/shard_map/ppermute | solution.py:22
  28.7 3.0 %collective-permute-start.4 = (bf16[2,1,8,128,128]{4,3,2,1,0:T(8,128)(2,1)}, bf16[2,1,8,128,128]{4,3,2,1,0:T(8,128)(2,1)}, u32[]{:S(2)}, u32[]{:S(2)}) collective-permute-start(bf16[2,1,8,128,128]{4,3,2,1,0:T(8,128)(2,1)} %get-tuple-element.97), channel_id=1, source_target_pairs={{0,24},{8,0},{16,8},{24,16},{1,25},{9,1},{17,9},{25,17},{2,26},{10... | collective-permute-start | bytes 1572872 | tf_op jit(solution)/shard_map/ppermute | solution.py:22
  33.1 10.2 %collective-permute-done.4 = bf16[2,1,8,128,128]{4,3,2,1,0:T(8,128)(2,1)} collective-permute-done((bf16[2,1,8,128,128]{4,3,2,1,0:T(8,128)(2,1)}, bf16[2,1,8,128,128]{4,3,2,1,0:T(8,128)(2,1)}, u32[]{:S(2)}, u32[]{:S(2)}) %collective-permute-start.4) | collective-permute-done | bytes 524320 | tf_op jit(solution)/shard_map/ppermute | solution.py:22
  43.3 3.4 %collective-permute-done.5 = bf16[2,1,8,128,128]{4,3,2,1,0:T(8,128)(2,1)} collective-permute-done((bf16[2,1,8,128,128]{4,3,2,1,0:T(8,128)(2,1)}, bf16[2,1,8,128,128]{4,3,2,1,0:T(8,128)(2,1)}, u32[]{:S(2)}, u32[]{:S(2)}) %collective-permute-start.5) | collective-permute-done | bytes 524320 | tf_op jit(solution)/shard_map/ppermute | solution.py:22
  49.5 3.1 %collective-permute-start.8 = (bf16[2,1,8,256,128]{4,3,2,1,0:T(8,128)(2,1)S(1)}, bf16[2,1,8,256,128]{4,3,2,1,0:T(8,128)(2,1)S(1)}, u32[]{:S(2)}, u32[]{:S(2)}) collective-permute-start(bf16[2,1,8,256,128]{4,3,2,1,0:T(8,128)(2,1)S(1)} %get-tuple-element.95), channel_id=1, source_target_pairs={{0,24},{8,0},{16,8},{24,16},{1,25},{9,1},{17,9},{25,17},{2,26},{10... | collective-permute-start | bytes 3145736 | tf_op jit(solution)/shard_map/ppermute | solution.py:22
  58.7 3.3 %collective-permute-start.6 = (bf16[12,256,128]{2,1,0:T(8,128)(2,1)S(1)}, bf16[12,256,128]{2,1,0:T(8,128)(2,1)S(1)}, u32[]{:S(2)}, u32[]{:S(2)}) collective-permute-start(bf16[12,256,128]{2,1,0:T(8,128)(2,1)S(1)} %pad_maximum_fusion.3), channel_id=1, source_target_pairs={{0,7},{1,0},{2,1},{3,2},{4,3},{5,4},{6,5},{7,6},{8,15},{9,8},{10,9... | collective-permute-start | bytes 2359304 | tf_op jit(solution)/shard_map/ppermute | solution.py:22
  62.0 13.1 %collective-permute-done.7 = bf16[12,256,128]{2,1,0:T(8,128)(2,1)S(1)} collective-permute-done((bf16[12,256,128]{2,1,0:T(8,128)(2,1)S(1)}, bf16[12,256,128]{2,1,0:T(8,128)(2,1)S(1)}, u32[]{:S(2)}, u32[]{:S(2)}) %collective-permute-start.7) | collective-permute-done | bytes 786464 | tf_op jit(solution)/shard_map/ppermute | solution.py:22
  75.2 2.4 %collective-permute-done.6 = bf16[12,256,128]{2,1,0:T(8,128)(2,1)S(1)} collective-permute-done((bf16[12,256,128]{2,1,0:T(8,128)(2,1)S(1)}, bf16[12,256,128]{2,1,0:T(8,128)(2,1)S(1)}, u32[]{:S(2)}, u32[]{:S(2)}) %collective-permute-start.6) | collective-permute-done | bytes 786464 | tf_op jit(solution)/shard_map/ppermute | solution.py:22
  80.1 3.8 %collective-permute-start.10 = (bf16[12,256,128]{2,1,0:T(8,128)(2,1)S(1)}, bf16[12,256,128]{2,1,0:T(8,128)(2,1)S(1)}, u32[]{:S(2)}, u32[]{:S(2)}) collective-permute-start(bf16[12,256,128]{2,1,0:T(8,128)(2,1)S(1)} %pad_maximum_fusion.5), channel_id=1, source_target_pairs={{0,7},{1,0},{2,1},{3,2},{4,3},{5,4},{6,5},{7,6},{8,15},{9,8},{10,9... | collective-permute-start | bytes 2359304 | tf_op jit(solution)/shard_map/ppermute | solution.py:22
  84.2 2.9 %collective-permute-start.15 = (bf16[4,1280,128]{2,1,0:T(8,128)(2,1)}, bf16[4,1280,128]{2,1,0:T(8,128)(2,1)}, u32[]{:S(2)}, u32[]{:S(2)}) collective-permute-start(bf16[4,1280,128]{2,1,0:T(8,128)(2,1)} %get-tuple-element.103.refs_0_), channel_id=1, source_target_pairs={{0,24},{8,0},{16,8},{24,16},{1,25},{9,1},{17,9},{25,17},{2,26},{10... | collective-permute-start | bytes 3932168 | tf_op jit(solution)/shard_map/ppermute | solution.py:22
  87.1 10.8 %collective-permute-done.11 = bf16[12,256,128]{2,1,0:T(8,128)(2,1)S(1)} collective-permute-done((bf16[12,256,128]{2,1,0:T(8,128)(2,1)S(1)}, bf16[12,256,128]{2,1,0:T(8,128)(2,1)S(1)}, u32[]{:S(2)}, u32[]{:S(2)}) %collective-permute-start.11) | collective-permute-done | bytes 786464 | tf_op jit(solution)/shard_map/ppermute | solution.py:22
  99.5 3.7 %collective-permute-start.12 = (bf16[8,256,128]{2,1,0:T(8,128)(2,1)}, bf16[8,256,128]{2,1,0:T(8,128)(2,1)}, u32[]{:S(2)}, u32[]{:S(2)}) collective-permute-start(bf16[8,256,128]{2,1,0:T(8,128)(2,1)} %fusion.2), channel_id=1, source_target_pairs={{0,7},{1,0},{2,1},{3,2},{4,3},{5,4},{6,5},{7,6},{8,15},{9,8},{10,9... | collective-permute-start | bytes 1572872 | tf_op jit(solution)/shard_map/ppermute | solution.py:22
  103.3 7.6 %collective-permute-done.13 = bf16[4,256,128]{2,1,0:T(8,128)(2,1)} collective-permute-done((bf16[4,256,128]{2,1,0:T(8,128)(2,1)S(1)}, bf16[4,256,128]{2,1,0:T(8,128)(2,1)}, u32[]{:S(2)}, u32[]{:S(2)}) %collective-permute-start.13) | collective-permute-done | bytes 262176 | tf_op jit(solution)/shard_map/ppermute | solution.py:22
  116.2 2.3 %collective-permute-start.18 = (bf16[4,768,128]{2,1,0:T(8,128)(2,1)}, bf16[4,768,128]{2,1,0:T(8,128)(2,1)}, u32[]{:S(2)}, u32[]{:S(2)}) collective-permute-start(bf16[4,768,128]{2,1,0:T(8,128)(2,1)} %pad_maximum_fusion.7.refs_1_), channel_id=1, source_target_pairs={{0,24},{8,0},{16,8},{24,16},{1,25},{9,1},{17,9},{25,17},{2,26},{10... | collective-permute-start | bytes 2359304 | tf_op jit(solution)/shard_map/ppermute | solution.py:22
  122.8 3.5 %all-to-all-start = ((bf16[8,256,128]{2,1,0:T(8,128)(2,1)}), bf16[8,256,128]{2,1,0:T(8,128)(2,1)S(1)}, u32[]{:S(2)}, u32[]{:S(2)}) async-start(bf16[8,256,128]{2,1,0:T(8,128)(2,1)} %fusion.1), calls=%async_computation | async-start | bytes 1048576 | tf_op jit(solution)/shard_map/all_to_all | solution.py:40
  129.5 3.4 %collective-permute-start.16 = (bf16[1,1,8,256,128]{4,3,2,1,0:T(8,128)(2,1)}, bf16[1,1,8,256,128]{4,3,2,1,0:T(8,128)(2,1)S(1)}, u32[]{:S(2)}, u32[]{:S(2)}) collective-permute-start(bf16[1,1,8,256,128]{4,3,2,1,0:T(8,128)(2,1)} %dynamic-slice_convert_fusion), channel_id=1, source_target_pairs={{0,32},{32,0},{1,33},{33,1},{2,34},{34,2},{3,35},{35,3},{4,36},{36... | collective-permute-start | bytes 1572872 | tf_op jit(solution)/shard_map/ppermute | solution.py:22
  135.0 3.4 %all-to-all-done = bf16[8,256,128]{2,1,0:T(8,128)(2,1)S(1)} async-done(((bf16[8,256,128]{2,1,0:T(8,128)(2,1)}), bf16[8,256,128]{2,1,0:T(8,128)(2,1)S(1)}, u32[]{:S(2)}, u32[]{:S(2)}) %all-to-all-start) | async-done | bytes 524320 | tf_op jit(solution)/shard_map/all_to_all | solution.py:40
  138.5 4.9 %collective-permute-done.16 = bf16[1,1,8,256,128]{4,3,2,1,0:T(8,128)(2,1)S(1)} collective-permute-done((bf16[1,1,8,256,128]{4,3,2,1,0:T(8,128)(2,1)}, bf16[1,1,8,256,128]{4,3,2,1,0:T(8,128)(2,1)S(1)}, u32[]{:S(2)}, u32[]{:S(2)}) %collective-permute-start.16) | collective-permute-done | bytes 524320 | tf_op jit(solution)/shard_map/ppermute | solution.py:22
  144.3 3.5 %all-to-all-start.1 = ((bf16[8,256,128]{2,1,0:T(8,128)(2,1)}), bf16[8,256,128]{2,1,0:T(8,128)(2,1)S(1)}, u32[]{:S(2)}, u32[]{:S(2)}) async-start(bf16[8,256,128]{2,1,0:T(8,128)(2,1)} %fusion.7), calls=%async_computation.1 | async-start | bytes 1048576 | tf_op jit(solution)/shard_map/all_to_all | solution.py:40
  151.8 13.0 %early_rows.1 = (f32[256,8192]{1,0:T(8,128)}, f32[256,512]{1,0:T(8,128)}, f32[256,128]{1,0:T(8,128)}) custom-call(s32[3]{0:T(128)} %pad_add_fusion.place, bf16[256,8192]{1,0:T(8,128)(2,1)} %bitcast.65, f32[1,8192]{1,0:T(1,128)} %gain.5, bf16[256,512]{1,0:T(8,128)(2,1)} %bitcast.77, f32[256,128]{1,0:T(8,128)} %get-tuple-element.46.inverse, ...), custom_call_target="tpu_custom_call" | custom-call | flops 3221225472 | bytes 18874368 | tf_op jit(solution)/shard_map/early_rows/pallas_call | solution.py:214
  167.1 11.3 %all-to-all-start.2 = ((f32[64,1,128]{2,1,0:T(1,128)}), f32[64,1,128]{2,1,0:T(1,128)S(1)}, u32[]{:S(2)}, u32[]{:S(2)}) async-start(f32[64,1,128]{2,1,0:T(1,128)} %broadcast_in_dim.8), calls=%async_computation.2 | async-start | bytes 65536 | tf_op jit(solution)/shard_map/all_to_all | solution.py:342
  179.9 13.4 %late_rows.1 = (bf16[256,512]{1,0:T(8,128)(2,1)}, bf16[256,8192]{1,0:T(8,128)(2,1)}) custom-call(s32[3]{0:T(128)} %pad_add_fusion.place, bf16[256,8192]{1,0:T(8,128)(2,1)} %bitcast.66, f32[1,8192]{1,0:T(1,128)} %gain.5, bf16[256,512]{1,0:T(8,128)(2,1)} %bitcast.78, f32[256,128]{1,0:T(8,128)} %get-tuple-element.46.inverse, ...), custom_call_target="tpu_custom_call" | custom-call | flops 1073741824 | bytes 14680064 | tf_op jit(solution)/shard_map/late_rows/pallas_call | solution.py:214
  (91 shorter events, 47.7 us)
Async XLA Ops:
  2.4 13.6 %collective-permute-start.1 = (f32[128,512]{1,0:T(8,128)S(1)}, f32[128,512]{1,0:T(8,128)S(1)}, u32[]{:S(2)}, u32[]{:S(2)}) collective-permute-start(f32[128,512]{1,0:T(8,128)S(1)} %bitcast_subtract_fusion), channel_id=1, source_target_pairs={{0,64},{64,0},{1,65},{65,1},{2,66},{66,2},{3,67},{67,3},{4,68},{68... | collective-permute-start | bytes 786440 | tf_op jit(solution)/shard_map/ppermute | solution.py:271
  3.6 12.3 %collective-permute-start = (bf16[4,128,128]{2,1,0:T(8,128)(2,1)S(1)}, bf16[4,128,128]{2,1,0:T(8,128)(2,1)S(1)}, u32[]{:S(2)}, u32[]{:S(2)}) collective-permute-start(bf16[4,128,128]{2,1,0:T(8,128)(2,1)S(1)} %bitcast.69), channel_id=1, source_target_pairs={{0,32},{32,0},{1,33},{33,1},{2,34},{34,2},{3,35},{35,3},{4,36},{36... | collective-permute-start | bytes 393224 | tf_op jit(solution)/shard_map/ppermute | solution.py:22
  20.5 26.2 %collective-permute-start.2 = (bf16[12,256,128]{2,1,0:T(8,128)(2,1)}, bf16[12,256,128]{2,1,0:T(8,128)(2,1)}, u32[]{:S(2)}, u32[]{:S(2)}) collective-permute-start(bf16[12,256,128]{2,1,0:T(8,128)(2,1)} %get-tuple-element.109), channel_id=1, source_target_pairs={{0,7},{1,0},{2,1},{3,2},{4,3},{5,4},{6,5},{7,6},{8,15},{9,8},{10,9... | collective-permute-start | bytes 2359304 | tf_op jit(solution)/shard_map/ppermute | solution.py:22
  26.4 20.9 %collective-permute-start.3 = (bf16[12,256,128]{2,1,0:T(8,128)(2,1)}, bf16[12,256,128]{2,1,0:T(8,128)(2,1)}, u32[]{:S(2)}, u32[]{:S(2)}) collective-permute-start(bf16[12,256,128]{2,1,0:T(8,128)(2,1)} %get-tuple-element.108), channel_id=1, source_target_pairs={{0,1},{1,2},{2,3},{3,4},{4,5},{5,6},{6,7},{7,0},{8,9},{9,10},{10,1... | collective-permute-start | bytes 2359304 | tf_op jit(solution)/shard_map/ppermute | solution.py:22
  28.7 14.6 %collective-permute-start.4 = (bf16[2,1,8,128,128]{4,3,2,1,0:T(8,128)(2,1)}, bf16[2,1,8,128,128]{4,3,2,1,0:T(8,128)(2,1)}, u32[]{:S(2)}, u32[]{:S(2)}) collective-permute-start(bf16[2,1,8,128,128]{4,3,2,1,0:T(8,128)(2,1)} %get-tuple-element.97), channel_id=1, source_target_pairs={{0,24},{8,0},{16,8},{24,16},{1,25},{9,1},{17,9},{25,17},{2,26},{10... | collective-permute-start | bytes 1572872 | tf_op jit(solution)/shard_map/ppermute | solution.py:22
  31.7 15.0 %collective-permute-start.5 = (bf16[2,1,8,128,128]{4,3,2,1,0:T(8,128)(2,1)}, bf16[2,1,8,128,128]{4,3,2,1,0:T(8,128)(2,1)}, u32[]{:S(2)}, u32[]{:S(2)}) collective-permute-start(bf16[2,1,8,128,128]{4,3,2,1,0:T(8,128)(2,1)} %get-tuple-element.96), channel_id=1, source_target_pairs={{0,8},{8,16},{16,24},{24,0},{1,9},{9,17},{17,25},{25,1},{2,10},{10... | collective-permute-start | bytes 1572872 | tf_op jit(solution)/shard_map/ppermute | solution.py:22
  49.5 28.0 %collective-permute-start.8 = (bf16[2,1,8,256,128]{4,3,2,1,0:T(8,128)(2,1)S(1)}, bf16[2,1,8,256,128]{4,3,2,1,0:T(8,128)(2,1)S(1)}, u32[]{:S(2)}, u32[]{:S(2)}) collective-permute-start(bf16[2,1,8,256,128]{4,3,2,1,0:T(8,128)(2,1)S(1)} %get-tuple-element.95), channel_id=1, source_target_pairs={{0,24},{8,0},{16,8},{24,16},{1,25},{9,1},{17,9},{25,17},{2,26},{10... | collective-permute-start | bytes 3145736 | tf_op jit(solution)/shard_map/ppermute | solution.py:22
  52.6 25.1 %collective-permute-start.9 = (bf16[2,1,8,256,128]{4,3,2,1,0:T(8,128)(2,1)S(1)}, bf16[2,1,8,256,128]{4,3,2,1,0:T(8,128)(2,1)S(1)}, u32[]{:S(2)}, u32[]{:S(2)}) collective-permute-start(bf16[2,1,8,256,128]{4,3,2,1,0:T(8,128)(2,1)S(1)} %get-tuple-element.94), channel_id=1, source_target_pairs={{0,8},{8,16},{16,24},{24,0},{1,9},{9,17},{17,25},{25,1},{2,10},{10... | collective-permute-start | bytes 3145736 | tf_op jit(solution)/shard_map/ppermute | solution.py:22
  55.6 19.5 %collective-permute-start.7 = (bf16[12,256,128]{2,1,0:T(8,128)(2,1)S(1)}, bf16[12,256,128]{2,1,0:T(8,128)(2,1)S(1)}, u32[]{:S(2)}, u32[]{:S(2)}) collective-permute-start(bf16[12,256,128]{2,1,0:T(8,128)(2,1)S(1)} %pad_maximum_fusion.4), channel_id=1, source_target_pairs={{0,1},{1,2},{2,3},{3,4},{4,5},{5,6},{6,7},{7,0},{8,9},{9,10},{10,1... | collective-permute-start | bytes 2359304 | tf_op jit(solution)/shard_map/ppermute | solution.py:22
  58.7 18.8 %collective-permute-start.6 = (bf16[12,256,128]{2,1,0:T(8,128)(2,1)S(1)}, bf16[12,256,128]{2,1,0:T(8,128)(2,1)S(1)}, u32[]{:S(2)}, u32[]{:S(2)}) collective-permute-start(bf16[12,256,128]{2,1,0:T(8,128)(2,1)S(1)} %pad_maximum_fusion.3), channel_id=1, source_target_pairs={{0,7},{1,0},{2,1},{3,2},{4,3},{5,4},{6,5},{7,6},{8,15},{9,8},{10,9... | collective-permute-start | bytes 2359304 | tf_op jit(solution)/shard_map/ppermute | solution.py:22
  79.0 18.9 %collective-permute-start.11 = (bf16[12,256,128]{2,1,0:T(8,128)(2,1)S(1)}, bf16[12,256,128]{2,1,0:T(8,128)(2,1)S(1)}, u32[]{:S(2)}, u32[]{:S(2)}) collective-permute-start(bf16[12,256,128]{2,1,0:T(8,128)(2,1)S(1)} %pad_maximum_fusion.6), channel_id=1, source_target_pairs={{0,1},{1,2},{2,3},{3,4},{4,5},{5,6},{6,7},{7,0},{8,9},{9,10},{10,1... | collective-permute-start | bytes 2359304 | tf_op jit(solution)/shard_map/ppermute | solution.py:22
  80.1 18.3 %collective-permute-start.10 = (bf16[12,256,128]{2,1,0:T(8,128)(2,1)S(1)}, bf16[12,256,128]{2,1,0:T(8,128)(2,1)S(1)}, u32[]{:S(2)}, u32[]{:S(2)}) collective-permute-start(bf16[12,256,128]{2,1,0:T(8,128)(2,1)S(1)} %pad_maximum_fusion.5), channel_id=1, source_target_pairs={{0,7},{1,0},{2,1},{3,2},{4,3},{5,4},{6,5},{7,6},{8,15},{9,8},{10,9... | collective-permute-start | bytes 2359304 | tf_op jit(solution)/shard_map/ppermute | solution.py:22
  83.9 29.5 %collective-permute-start.14 = (bf16[4,1280,128]{2,1,0:T(8,128)(2,1)}, bf16[4,1280,128]{2,1,0:T(8,128)(2,1)}, u32[]{:S(2)}, u32[]{:S(2)}) collective-permute-start(bf16[4,1280,128]{2,1,0:T(8,128)(2,1)} %get-tuple-element.103.refs_0_), channel_id=1, source_target_pairs={{0,8},{8,16},{16,24},{24,0},{1,9},{9,17},{17,25},{25,1},{2,10},{10... | collective-permute-start | bytes 3932168 | tf_op jit(solution)/shard_map/ppermute | solution.py:22
  84.2 29.2 %collective-permute-start.15 = (bf16[4,1280,128]{2,1,0:T(8,128)(2,1)}, bf16[4,1280,128]{2,1,0:T(8,128)(2,1)}, u32[]{:S(2)}, u32[]{:S(2)}) collective-permute-start(bf16[4,1280,128]{2,1,0:T(8,128)(2,1)} %get-tuple-element.103.refs_0_), channel_id=1, source_target_pairs={{0,24},{8,0},{16,8},{24,16},{1,25},{9,1},{17,9},{25,17},{2,26},{10... | collective-permute-start | bytes 3932168 | tf_op jit(solution)/shard_map/ppermute | solution.py:22
  99.5 12.1 %collective-permute-start.12 = (bf16[8,256,128]{2,1,0:T(8,128)(2,1)}, bf16[8,256,128]{2,1,0:T(8,128)(2,1)}, u32[]{:S(2)}, u32[]{:S(2)}) collective-permute-start(bf16[8,256,128]{2,1,0:T(8,128)(2,1)} %fusion.2), channel_id=1, source_target_pairs={{0,7},{1,0},{2,1},{3,2},{4,3},{5,4},{6,5},{7,6},{8,15},{9,8},{10,9... | collective-permute-start | bytes 1572872 | tf_op jit(solution)/shard_map/ppermute | solution.py:22
  115.3 29.0 %collective-permute-start.17 = (bf16[4,768,128]{2,1,0:T(8,128)(2,1)}, bf16[4,768,128]{2,1,0:T(8,128)(2,1)}, u32[]{:S(2)}, u32[]{:S(2)}) collective-permute-start(bf16[4,768,128]{2,1,0:T(8,128)(2,1)} %pad_maximum_fusion.7.refs_1_), channel_id=1, source_target_pairs={{0,8},{8,16},{16,24},{24,0},{1,9},{9,17},{17,25},{25,1},{2,10},{10... | collective-permute-start | bytes 2359304 | tf_op jit(solution)/shard_map/ppermute | solution.py:22
  116.2 28.1 %collective-permute-start.18 = (bf16[4,768,128]{2,1,0:T(8,128)(2,1)}, bf16[4,768,128]{2,1,0:T(8,128)(2,1)}, u32[]{:S(2)}, u32[]{:S(2)}) collective-permute-start(bf16[4,768,128]{2,1,0:T(8,128)(2,1)} %pad_maximum_fusion.7.refs_1_), channel_id=1, source_target_pairs={{0,24},{8,0},{16,8},{24,16},{1,25},{9,1},{17,9},{25,17},{2,26},{10... | collective-permute-start | bytes 2359304 | tf_op jit(solution)/shard_map/ppermute | solution.py:22
  119.3 13.6 %collective-permute-start.19 = (f32[128,512]{1,0:T(8,128)}, f32[128,512]{1,0:T(8,128)}, u32[]{:S(2)}, u32[]{:S(2)}) collective-permute-start(f32[128,512]{1,0:T(8,128)} %add.177), channel_id=1, source_target_pairs={{0,128},{128,0},{1,129},{129,1},{2,130},{130,2},{3,131},{131,3},{4... | collective-permute-start | bytes 786440 | tf_op jit(solution)/shard_map/ppermute | solution.py:324
  122.8 15.6 %all-to-all-start = ((bf16[8,256,128]{2,1,0:T(8,128)(2,1)}), bf16[8,256,128]{2,1,0:T(8,128)(2,1)S(1)}, u32[]{:S(2)}, u32[]{:S(2)}) async-start(bf16[8,256,128]{2,1,0:T(8,128)(2,1)} %fusion.1), calls=%async_computation | async-start | bytes 1048576 | tf_op jit(solution)/shard_map/all_to_all | solution.py:40
  129.5 13.9 %collective-permute-start.16 = (bf16[1,1,8,256,128]{4,3,2,1,0:T(8,128)(2,1)}, bf16[1,1,8,256,128]{4,3,2,1,0:T(8,128)(2,1)S(1)}, u32[]{:S(2)}, u32[]{:S(2)}) collective-permute-start(bf16[1,1,8,256,128]{4,3,2,1,0:T(8,128)(2,1)} %dynamic-slice_convert_fusion), channel_id=1, source_target_pairs={{0,32},{32,0},{1,33},{33,1},{2,34},{34,2},{3,35},{35,3},{4,36},{36... | collective-permute-start | bytes 1572872 | tf_op jit(solution)/shard_map/ppermute | solution.py:22
  144.3 20.5 %all-to-all-start.1 = ((bf16[8,256,128]{2,1,0:T(8,128)(2,1)}), bf16[8,256,128]{2,1,0:T(8,128)(2,1)S(1)}, u32[]{:S(2)}, u32[]{:S(2)}) async-start(bf16[8,256,128]{2,1,0:T(8,128)(2,1)} %fusion.7), calls=%async_computation.1 | async-start | bytes 1048576 | tf_op jit(solution)/shard_map/all_to_all | solution.py:40
  147.8 30.6 %collective-permute-start.20 = (bf16[4,1280,128]{2,1,0:T(8,128)(2,1)}, bf16[4,1280,128]{2,1,0:T(8,128)(2,1)S(1)}, u32[]{:S(2)}, u32[]{:S(2)}) collective-permute-start(bf16[4,1280,128]{2,1,0:T(8,128)(2,1)} %collective-permute-done.14.refs_2_), channel_id=1, source_target_pairs={{0,8},{8,16},{16,24},{24,0},{1,9},{9,17},{17,25},{25,1},{2,10},{10... | collective-permute-start | bytes 3932168 | tf_op jit(solution)/shard_map/ppermute | solution.py:22
  150.2 28.3 %collective-permute-start.21 = (bf16[4,768,128]{2,1,0:T(8,128)(2,1)}, bf16[4,768,128]{2,1,0:T(8,128)(2,1)S(1)}, u32[]{:S(2)}, u32[]{:S(2)}) collective-permute-start(bf16[4,768,128]{2,1,0:T(8,128)(2,1)} %collective-permute-done.18.refs_5_), channel_id=1, source_target_pairs={{0,24},{8,0},{16,8},{24,16},{1,25},{9,1},{17,9},{25,17},{2,26},{10... | collective-permute-start | bytes 2359304 | tf_op jit(solution)/shard_map/ppermute | solution.py:22
  167.1 26.1 %all-to-all-start.2 = ((f32[64,1,128]{2,1,0:T(1,128)}), f32[64,1,128]{2,1,0:T(1,128)S(1)}, u32[]{:S(2)}, u32[]{:S(2)}) async-start(f32[64,1,128]{2,1,0:T(1,128)} %broadcast_in_dim.8), calls=%async_computation.2 | async-start | bytes 65536 | tf_op jit(solution)/shard_map/all_to_all | solution.py:342
  (12 other events, 150.8 us)

commit v8 on v7

--- a/solution.py
+++ b/solution.py
@@ -306,8 +306,13 @@
     z5, z3 = left[sums:], right[sums:]
     left = shift(added(part_a, "z", 2, -1, left[:sums]), "z", -1)
     z4 = shift(z3, "z", 1)
-    left, right, z4, first1, first3, b_left, b_right, core = together(
-        left, right, z4, first1, first3, b_left, b_right, core
+    sum_b = term(part_b, "y", 1, 0).astype(F32) + b_left.astype(F32) + b_right.astype(F32)
+    at_x = lax.axis_index("xh")
+    over_x = shift(lax.dynamic_slice_in_dim(sum_b, 1 - at_x, 1, 0).astype(BF16), "xh", 1)
+    sum_b = lax.dynamic_slice_in_dim(sum_b, at_x, 1, 0) + over_x.astype(F32)
+    sum_b = sum_b.reshape(-1, cut, rows).astype(BF16)
+    left, right, z4, first1, first3, sum_b, core = together(
+        left, right, z4, first1, first3, sum_b, core
     )
 
     second = jnp.concatenate([z3, z5, z4], axis=1)
@@ -315,11 +320,6 @@
     sum_a = term(part_a, "z", 2, 0).reshape(left.shape).astype(F32)
     sum_a = sum_a + left.astype(F32) + right[:sums].astype(F32)
     sum_a = exchange_sum(sum_a.reshape(-1, cut, rows), ("xh", "y"))
-    sum_b = term(part_b, "y", 1, 0).astype(F32) + b_left.astype(F32) + b_right.astype(F32)
-    at_x = lax.axis_index("xh")
-    away = lax.dynamic_slice_in_dim(sum_b, 1 - at_x, 1, 0).astype(BF16)
-    sum_b = lax.dynamic_slice_in_dim(sum_b, at_x, 1, 0) + shift(away, "xh", 1).astype(F32)
-    sum_b = sum_b.reshape(-1, cut, rows).astype(BF16)
     both = mine + core
     summed = both + lax.ppermute(both, "xl", [(0, 1), (1, 0)])
     moment = lax.dynamic_index_in_dim(outer_momentum, chosen, 0, keepdims=False)

time: 196 us -> 188 us (0.959)
  waiting for transfers between devices: 59.6 us -> 52.3 us
  starting transfers between devices: 58.3 us -> 54.9 us
    ppermute x20, waiting for transfers between devices: 56.2 us -> 41.8 us  [shift(): return lax.ppermute(value, axis, [(i, (i + step) % n) for i in range(n)])]
    all_to_all x2, waiting for transfers between devices: 3.39 us -> 9.62 us  [exchange_sum(): blocks = lax.all_to_all(part.astype(BF16), axes, 0, 0, tiled=True)]
    ppermute x20, starting transfers between devices: 38.4 us -> 36.1 us  [shift(): return lax.ppermute(value, axis, [(i, (i + step) % n) for i in range(n)])]
  transfers between devices with their start and end apart: 25 -> 25, of which waited for: 13 -> 12; matrix products, arithmetic and copies ran while one was open for 13% -> 16% of each run, Pallas kernels for 19% -> 20%
where the time goes in v8:
time: 188 us; the launch traced here: 186 us
  starting transfers between devices  54.9 us (29%)
  waiting for transfers between devices  52.3 us (28%)
  Pallas kernels  36.6 us (19%)
  other arithmetic  21.6 us (11%)
  local copies, waits for them, and re-layouts  19.5 us (10%)
    ppermute x20, waiting for transfers between devices, shift(): return lax.ppermute(value, axis, [(i, (i + step) % n) for i in range(n)])  41.8 us
    ppermute x20, starting transfers between devices, shift(): return lax.ppermute(value, axis, [(i, (i + step) % n) for i in range(n)])  36.1 us
    pallas_call x2, Pallas kernels, rows_call(): pl.pallas_call(functools.partial(kernel, steps), out_shape=outs, in_specs...  26.4 us
    all_to_all x1, starting transfers between devices, per_device(): lax.all_to_all(jnp.broadcast_to(own_sum[None], (devices, rows)), GROUP, 0...  10.1 us
    pallas_call x1, Pallas kernels, weight_grad(): pl.pallas_call(weight_grad_kernel, grid=(blocks // per_step,), out_shape=...  10.1 us
    all_to_all x2, waiting for transfers between devices, exchange_sum(): blocks = lax.all_to_all(part.astype(BF16), axes, 0, 0, tiled=True)  9.62 us
    all_to_all x2, starting transfers between devices, exchange_sum(): blocks = lax.all_to_all(part.astype(BF16), axes, 0, 0, tiled=True)  7.02 us
    convert_element_type x6, other arithmetic, added(): return (mine.astype(F32) + received.astype(F32)).astype(BF16)  6.97 us
  transfers between devices with their start and end apart: 25, of which 12 were waited for; matrix products, arithmetic and copies ran while one was open for 16% of the time, Pallas kernels for 20%

profile of v8, /device:TPU:2, one launch (start us, length us, event | category | flops | bytes accessed | tf_op | source)
XLA Modules:
  0.0 186.4 jit_solution(18304835790508545615)
XLA Ops:
  5.8 10.1 %weight_grad.1 = (bf16[64,256,128]{2,1,0:T(8,128)(2,1)}, bf16[64,256,128]{2,1,0:T(8,128)(2,1)}, f32[256,128]{1,0:T(8,128)}) custom-call(bf16[256,8192]{1,0:T(8,128)(2,1)} %bitcast.64, f32[1,8192]{1,0:T(1,128)} %gain.5, bf16[256,512]{1,0:T(8,128)(2,1)} %bitcast.76), custom_call_target="tpu_custom_call" | custom-call | flops 2147483648 | bytes 23068672 | tf_op jit(solution)/shard_map/weight_grad/pallas_call | solution.py:81
  16.7 2.5 %constant_dynamic-slice_fusion.2 = (bf16[2,4,1,256,128]{4,3,1,0,2:T(8,128)(2,1)S(1)}, bf16[2,4,1,256,128]{4,3,1,0,2:T(8,128)(2,1)S(1)}, bf16[2,4,1,256,128]{4,3,...) fusion(s32[]{:T(128)S(6)} %select_n.65, ...), kind=kLoop, calls=%fused_computation.45 | loop fusion | bytes 8388640 | tf_op jit(solution)/shard_map/dynamic_slice | solution.py:31
  20.5 5.9 %collective-permute-start.2 = (bf16[12,256,128]{2,1,0:T(8,128)(2,1)}, bf16[12,256,128]{2,1,0:T(8,128)(2,1)}, u32[]{:S(2)}, u32[]{:S(2)}) collective-permute-start(bf16[12,256,128]{2,1,0:T(8,128)(2,1)} %get-tuple-element.107), channel_id=1, source_target_pairs={{0,7},{1,0},{2,1},{3,2},{4,3},{5,4},{6,5},{7,6},{8,15},{9,8},{10,9... | collective-permute-start | bytes 2359304 | tf_op jit(solution)/shard_map/ppermute | solution.py:22
  26.4 2.3 %constant_dynamic-slice_fusion.8 = (bf16[2,1,8,128,128]{4,3,2,1,0:T(8,128)(2,1)}, bf16[2,1,8,128,128]{4,3,2,1,0:T(8,128)(2,1)}) fusion(bf16[2,4,8,256,128]{4,3,2,1,0:T(8,128)(2,1)} %bitcast.60, s32[]{:T(128)S(6)} %select_n.54, s32[]{:T(128)S(6)} %add.186), kind=kLoop, calls=%fused_computation.51 | loop fusion | bytes 2097160 | tf_op jit(solution)/shard_map/slice | solution.py:284
  28.7 3.0 %collective-permute-start.4 = (bf16[2,1,8,128,128]{4,3,2,1,0:T(8,128)(2,1)}, bf16[2,1,8,128,128]{4,3,2,1,0:T(8,128)(2,1)}, u32[]{:S(2)}, u32[]{:S(2)}) collective-permute-start(bf16[2,1,8,128,128]{4,3,2,1,0:T(8,128)(2,1)} %get-tuple-element.95), channel_id=1, source_target_pairs={{0,24},{8,0},{16,8},{24,16},{1,25},{9,1},{17,9},{25,17},{2,26},{10... | collective-permute-start | bytes 1572872 | tf_op jit(solution)/shard_map/ppermute | solution.py:22
  33.1 10.2 %collective-permute-done.4 = bf16[2,1,8,128,128]{4,3,2,1,0:T(8,128)(2,1)} collective-permute-done((bf16[2,1,8,128,128]{4,3,2,1,0:T(8,128)(2,1)}, bf16[2,1,8,128,128]{4,3,2,1,0:T(8,128)(2,1)}, u32[]{:S(2)}, u32[]{:S(2)}) %collective-permute-start.4) | collective-permute-done | bytes 524320 | tf_op jit(solution)/shard_map/ppermute | solution.py:22
  43.3 3.4 %collective-permute-done.5 = bf16[2,1,8,128,128]{4,3,2,1,0:T(8,128)(2,1)} collective-permute-done((bf16[2,1,8,128,128]{4,3,2,1,0:T(8,128)(2,1)}, bf16[2,1,8,128,128]{4,3,2,1,0:T(8,128)(2,1)}, u32[]{:S(2)}, u32[]{:S(2)}) %collective-permute-start.5) | collective-permute-done | bytes 524320 | tf_op jit(solution)/shard_map/ppermute | solution.py:22
  49.5 3.1 %collective-permute-start.8 = (bf16[2,1,8,256,128]{4,3,2,1,0:T(8,128)(2,1)S(1)}, bf16[2,1,8,256,128]{4,3,2,1,0:T(8,128)(2,1)S(1)}, u32[]{:S(2)}, u32[]{:S(2)}) collective-permute-start(bf16[2,1,8,256,128]{4,3,2,1,0:T(8,128)(2,1)S(1)} %get-tuple-element.93), channel_id=1, source_target_pairs={{0,24},{8,0},{16,8},{24,16},{1,25},{9,1},{17,9},{25,17},{2,26},{10... | collective-permute-start | bytes 3145736 | tf_op jit(solution)/shard_map/ppermute | solution.py:22
  58.7 3.3 %collective-permute-start.6 = (bf16[12,256,128]{2,1,0:T(8,128)(2,1)S(1)}, bf16[12,256,128]{2,1,0:T(8,128)(2,1)S(1)}, u32[]{:S(2)}, u32[]{:S(2)}) collective-permute-start(bf16[12,256,128]{2,1,0:T(8,128)(2,1)S(1)} %pad_maximum_fusion.3), channel_id=1, source_target_pairs={{0,7},{1,0},{2,1},{3,2},{4,3},{5,4},{6,5},{7,6},{8,15},{9,8},{10,9... | collective-permute-start | bytes 2359304 | tf_op jit(solution)/shard_map/ppermute | solution.py:22
  62.0 13.1 %collective-permute-done.7 = bf16[12,256,128]{2,1,0:T(8,128)(2,1)S(1)} collective-permute-done((bf16[12,256,128]{2,1,0:T(8,128)(2,1)S(1)}, bf16[12,256,128]{2,1,0:T(8,128)(2,1)S(1)}, u32[]{:S(2)}, u32[]{:S(2)}) %collective-permute-start.7) | collective-permute-done | bytes 786464 | tf_op jit(solution)/shard_map/ppermute | solution.py:22
  75.2 2.4 %collective-permute-done.6 = bf16[12,256,128]{2,1,0:T(8,128)(2,1)S(1)} collective-permute-done((bf16[12,256,128]{2,1,0:T(8,128)(2,1)S(1)}, bf16[12,256,128]{2,1,0:T(8,128)(2,1)S(1)}, u32[]{:S(2)}, u32[]{:S(2)}) %collective-permute-start.6) | collective-permute-done | bytes 786464 | tf_op jit(solution)/shard_map/ppermute | solution.py:22
  81.8 3.5 %collective-permute-start.10 = (bf16[12,256,128]{2,1,0:T(8,128)(2,1)}, bf16[12,256,128]{2,1,0:T(8,128)(2,1)}, u32[]{:S(2)}, u32[]{:S(2)}) collective-permute-start(bf16[12,256,128]{2,1,0:T(8,128)(2,1)} %pad_maximum_fusion.5), channel_id=1, source_target_pairs={{0,7},{1,0},{2,1},{3,2},{4,3},{5,4},{6,5},{7,6},{8,15},{9,8},{10,9... | collective-permute-start | bytes 2359304 | tf_op jit(solution)/shard_map/ppermute | solution.py:22
  85.6 2.9 %collective-permute-start.15 = (bf16[4,1280,128]{2,1,0:T(8,128)(2,1)}, bf16[4,1280,128]{2,1,0:T(8,128)(2,1)}, u32[]{:S(2)}, u32[]{:S(2)}) collective-permute-start(bf16[4,1280,128]{2,1,0:T(8,128)(2,1)} %get-tuple-element.101.refs_0_), channel_id=1, source_target_pairs={{0,24},{8,0},{16,8},{24,16},{1,25},{9,1},{17,9},{25,17},{2,26},{10... | collective-permute-start | bytes 3932168 | tf_op jit(solution)/shard_map/ppermute | solution.py:22
  88.6 2.3 %convert_add_fusion = f32[2,1,8,256,128]{4,3,2,1,0:T(8,128)S(1)} fusion(bf16[2,1,8,256,128]{4,3,2,1,0:T(8,128)(2,1)} %copy-done.4, bf16[2,1,8,256,128]{4,3,2,1,0:T(8,128)(2,1)} %copy-done.3, bf16[2,4,8,256,128]{4,3,2,1,0:T(8,128)(2,1)} %bitcast.62, s32[]{:T(128)S(6)} %select_n.62), kind=kLoop, calls=%fused_computation | loop fusion | flops 2621440 | bytes 5242884 | tf_op jit(solution)/shard_map/add | solution.py:309
  93.1 5.8 %collective-permute-done.11 = bf16[12,256,128]{2,1,0:T(8,128)(2,1)} collective-permute-done((bf16[12,256,128]{2,1,0:T(8,128)(2,1)}, bf16[12,256,128]{2,1,0:T(8,128)(2,1)}, u32[]{:S(2)}, u32[]{:S(2)}) %collective-permute-start.11) | collective-permute-done | bytes 786464 | tf_op jit(solution)/shard_map/ppermute | solution.py:22
  102.2 3.7 %collective-permute-start.12 = (bf16[8,256,128]{2,1,0:T(8,128)(2,1)}, bf16[8,256,128]{2,1,0:T(8,128)(2,1)}, u32[]{:S(2)}, u32[]{:S(2)}) collective-permute-start(bf16[8,256,128]{2,1,0:T(8,128)(2,1)} %fusion.2), channel_id=1, source_target_pairs={{0,7},{1,0},{2,1},{3,2},{4,3},{5,4},{6,5},{7,6},{8,15},{9,8},{10,9... | collective-permute-start | bytes 1572872 | tf_op jit(solution)/shard_map/ppermute | solution.py:22
  110.0 4.6 %collective-permute-done.13 = bf16[4,256,128]{2,1,0:T(8,128)(2,1)S(1)} collective-permute-done((bf16[4,256,128]{2,1,0:T(8,128)(2,1)S(1)}, bf16[4,256,128]{2,1,0:T(8,128)(2,1)S(1)}, u32[]{:S(2)}, u32[]{:S(2)}) %collective-permute-start.13) | collective-permute-done | bytes 262176 | tf_op jit(solution)/shard_map/ppermute | solution.py:22
  115.9 2.3 %collective-permute-start.18 = (bf16[4,768,128]{2,1,0:T(8,128)(2,1)S(1)}, bf16[4,768,128]{2,1,0:T(8,128)(2,1)S(1)}, u32[]{:S(2)}, u32[]{:S(2)}) collective-permute-start(bf16[4,768,128]{2,1,0:T(8,128)(2,1)S(1)} %pad_maximum_fusion.7.refs_1_), channel_id=1, source_target_pairs={{0,24},{8,0},{16,8},{24,16},{1,25},{9,1},{17,9},{25,17},{2,26},{10... | collective-permute-start | bytes 2359304 | tf_op jit(solution)/shard_map/ppermute | solution.py:22
  122.0 3.5 %all-to-all-start = ((bf16[8,256,128]{2,1,0:T(8,128)(2,1)}), bf16[8,256,128]{2,1,0:T(8,128)(2,1)S(1)}, u32[]{:S(2)}, u32[]{:S(2)}) async-start(bf16[8,256,128]{2,1,0:T(8,128)(2,1)} %fusion.1), calls=%async_computation | async-start | bytes 1048576 | tf_op jit(solution)/shard_map/all_to_all | solution.py:40
  128.2 9.6 %all-to-all-done = bf16[8,256,128]{2,1,0:T(8,128)(2,1)S(1)} async-done(((bf16[8,256,128]{2,1,0:T(8,128)(2,1)}), bf16[8,256,128]{2,1,0:T(8,128)(2,1)S(1)}, u32[]{:S(2)}, u32[]{:S(2)}) %all-to-all-start) | async-done | bytes 524320 | tf_op jit(solution)/shard_map/all_to_all | solution.py:40
  138.0 3.5 %all-to-all-start.1 = ((bf16[8,256,128]{2,1,0:T(8,128)(2,1)}), bf16[8,256,128]{2,1,0:T(8,128)(2,1)S(1)}, u32[]{:S(2)}, u32[]{:S(2)}) async-start(bf16[8,256,128]{2,1,0:T(8,128)(2,1)} %fusion.7), calls=%async_computation.1 | async-start | bytes 1048576 | tf_op jit(solution)/shard_map/all_to_all | solution.py:40
  145.5 13.0 %early_rows.1 = (f32[256,8192]{1,0:T(8,128)}, f32[256,512]{1,0:T(8,128)}, f32[256,128]{1,0:T(8,128)}) custom-call(s32[3]{0:T(128)} %pad_add_fusion.place, bf16[256,8192]{1,0:T(8,128)(2,1)} %bitcast.65, f32[1,8192]{1,0:T(1,128)} %gain.5, bf16[256,512]{1,0:T(8,128)(2,1)} %bitcast.77, f32[256,128]{1,0:T(8,128)} %get-tuple-element.45.inverse, ...), custom_call_target="tpu_custom_call" | custom-call | flops 3221225472 | bytes 18874368 | tf_op jit(solution)/shard_map/early_rows/pallas_call | solution.py:214
  160.8 10.1 %all-to-all-start.2 = ((f32[64,1,128]{2,1,0:T(1,128)}), f32[64,1,128]{2,1,0:T(1,128)S(1)}, u32[]{:S(2)}, u32[]{:S(2)}) async-start(f32[64,1,128]{2,1,0:T(1,128)} %broadcast_in_dim.8), calls=%async_computation.2 | async-start | bytes 65536 | tf_op jit(solution)/shard_map/all_to_all | solution.py:342
  172.4 13.4 %late_rows.1 = (bf16[256,512]{1,0:T(8,128)(2,1)}, bf16[256,8192]{1,0:T(8,128)(2,1)}) custom-call(s32[3]{0:T(128)} %pad_add_fusion.place, bf16[256,8192]{1,0:T(8,128)(2,1)} %bitcast.66, f32[1,8192]{1,0:T(1,128)} %gain.5, bf16[256,512]{1,0:T(8,128)(2,1)} %bitcast.78, f32[256,128]{1,0:T(8,128)} %get-tuple-element.45.inverse, ...), custom_call_target="tpu_custom_call" | custom-call | flops 1073741824 | bytes 14680064 | tf_op jit(solution)/shard_map/late_rows/pallas_call | solution.py:214
  (91 shorter events, 47.1 us)
Async XLA Ops:
  2.4 13.6 %collective-permute-start.1 = (f32[128,512]{1,0:T(8,128)S(1)}, f32[128,512]{1,0:T(8,128)S(1)}, u32[]{:S(2)}, u32[]{:S(2)}) collective-permute-start(f32[128,512]{1,0:T(8,128)S(1)} %bitcast_subtract_fusion), channel_id=1, source_target_pairs={{0,64},{64,0},{1,65},{65,1},{2,66},{66,2},{3,67},{67,3},{4,68},{68... | collective-permute-start | bytes 786440 | tf_op jit(solution)/shard_map/ppermute | solution.py:271
  3.6 12.3 %collective-permute-start = (bf16[4,128,128]{2,1,0:T(8,128)(2,1)S(1)}, bf16[4,128,128]{2,1,0:T(8,128)(2,1)S(1)}, u32[]{:S(2)}, u32[]{:S(2)}) collective-permute-start(bf16[4,128,128]{2,1,0:T(8,128)(2,1)S(1)} %bitcast.69), channel_id=1, source_target_pairs={{0,32},{32,0},{1,33},{33,1},{2,34},{34,2},{3,35},{35,3},{4,36},{36... | collective-permute-start | bytes 393224 | tf_op jit(solution)/shard_map/ppermute | solution.py:22
  20.5 26.2 %collective-permute-start.2 = (bf16[12,256,128]{2,1,0:T(8,128)(2,1)}, bf16[12,256,128]{2,1,0:T(8,128)(2,1)}, u32[]{:S(2)}, u32[]{:S(2)}) collective-permute-start(bf16[12,256,128]{2,1,0:T(8,128)(2,1)} %get-tuple-element.107), channel_id=1, source_target_pairs={{0,7},{1,0},{2,1},{3,2},{4,3},{5,4},{6,5},{7,6},{8,15},{9,8},{10,9... | collective-permute-start | bytes 2359304 | tf_op jit(solution)/shard_map/ppermute | solution.py:22
  26.4 20.9 %collective-permute-start.3 = (bf16[12,256,128]{2,1,0:T(8,128)(2,1)}, bf16[12,256,128]{2,1,0:T(8,128)(2,1)}, u32[]{:S(2)}, u32[]{:S(2)}) collective-permute-start(bf16[12,256,128]{2,1,0:T(8,128)(2,1)} %get-tuple-element.106), channel_id=1, source_target_pairs={{0,1},{1,2},{2,3},{3,4},{4,5},{5,6},{6,7},{7,0},{8,9},{9,10},{10,1... | collective-permute-start | bytes 2359304 | tf_op jit(solution)/shard_map/ppermute | solution.py:22
  28.7 14.6 %collective-permute-start.4 = (bf16[2,1,8,128,128]{4,3,2,1,0:T(8,128)(2,1)}, bf16[2,1,8,128,128]{4,3,2,1,0:T(8,128)(2,1)}, u32[]{:S(2)}, u32[]{:S(2)}) collective-permute-start(bf16[2,1,8,128,128]{4,3,2,1,0:T(8,128)(2,1)} %get-tuple-element.95), channel_id=1, source_target_pairs={{0,24},{8,0},{16,8},{24,16},{1,25},{9,1},{17,9},{25,17},{2,26},{10... | collective-permute-start | bytes 1572872 | tf_op jit(solution)/shard_map/ppermute | solution.py:22
  31.7 15.0 %collective-permute-start.5 = (bf16[2,1,8,128,128]{4,3,2,1,0:T(8,128)(2,1)}, bf16[2,1,8,128,128]{4,3,2,1,0:T(8,128)(2,1)}, u32[]{:S(2)}, u32[]{:S(2)}) collective-permute-start(bf16[2,1,8,128,128]{4,3,2,1,0:T(8,128)(2,1)} %get-tuple-element.94), channel_id=1, source_target_pairs={{0,8},{8,16},{16,24},{24,0},{1,9},{9,17},{17,25},{25,1},{2,10},{10... | collective-permute-start | bytes 1572872 | tf_op jit(solution)/shard_map/ppermute | solution.py:22
  49.5 28.0 %collective-permute-start.8 = (bf16[2,1,8,256,128]{4,3,2,1,0:T(8,128)(2,1)S(1)}, bf16[2,1,8,256,128]{4,3,2,1,0:T(8,128)(2,1)S(1)}, u32[]{:S(2)}, u32[]{:S(2)}) collective-permute-start(bf16[2,1,8,256,128]{4,3,2,1,0:T(8,128)(2,1)S(1)} %get-tuple-element.93), channel_id=1, source_target_pairs={{0,24},{8,0},{16,8},{24,16},{1,25},{9,1},{17,9},{25,17},{2,26},{10... | collective-permute-start | bytes 3145736 | tf_op jit(solution)/shard_map/ppermute | solution.py:22
  52.6 25.1 %collective-permute-start.9 = (bf16[2,1,8,256,128]{4,3,2,1,0:T(8,128)(2,1)S(1)}, bf16[2,1,8,256,128]{4,3,2,1,0:T(8,128)(2,1)S(1)}, u32[]{:S(2)}, u32[]{:S(2)}) collective-permute-start(bf16[2,1,8,256,128]{4,3,2,1,0:T(8,128)(2,1)S(1)} %get-tuple-element.92), channel_id=1, source_target_pairs={{0,8},{8,16},{16,24},{24,0},{1,9},{9,17},{17,25},{25,1},{2,10},{10... | collective-permute-start | bytes 3145736 | tf_op jit(solution)/shard_map/ppermute | solution.py:22
  55.6 19.5 %collective-permute-start.7 = (bf16[12,256,128]{2,1,0:T(8,128)(2,1)S(1)}, bf16[12,256,128]{2,1,0:T(8,128)(2,1)S(1)}, u32[]{:S(2)}, u32[]{:S(2)}) collective-permute-start(bf16[12,256,128]{2,1,0:T(8,128)(2,1)S(1)} %pad_maximum_fusion.4), channel_id=1, source_target_pairs={{0,1},{1,2},{2,3},{3,4},{4,5},{5,6},{6,7},{7,0},{8,9},{9,10},{10,1... | collective-permute-start | bytes 2359304 | tf_op jit(solution)/shard_map/ppermute | solution.py:22
  58.7 18.8 %collective-permute-start.6 = (bf16[12,256,128]{2,1,0:T(8,128)(2,1)S(1)}, bf16[12,256,128]{2,1,0:T(8,128)(2,1)S(1)}, u32[]{:S(2)}, u32[]{:S(2)}) collective-permute-start(bf16[12,256,128]{2,1,0:T(8,128)(2,1)S(1)} %pad_maximum_fusion.3), channel_id=1, source_target_pairs={{0,7},{1,0},{2,1},{3,2},{4,3},{5,4},{6,5},{7,6},{8,15},{9,8},{10,9... | collective-permute-start | bytes 2359304 | tf_op jit(solution)/shard_map/ppermute | solution.py:22
  79.9 19.1 %collective-permute-start.11 = (bf16[12,256,128]{2,1,0:T(8,128)(2,1)}, bf16[12,256,128]{2,1,0:T(8,128)(2,1)}, u32[]{:S(2)}, u32[]{:S(2)}) collective-permute-start(bf16[12,256,128]{2,1,0:T(8,128)(2,1)} %pad_maximum_fusion.6), channel_id=1, source_target_pairs={{0,1},{1,2},{2,3},{3,4},{4,5},{5,6},{6,7},{7,0},{8,9},{9,10},{10,1... | collective-permute-start | bytes 2359304 | tf_op jit(solution)/shard_map/ppermute | solution.py:22
  81.8 18.4 %collective-permute-start.10 = (bf16[12,256,128]{2,1,0:T(8,128)(2,1)}, bf16[12,256,128]{2,1,0:T(8,128)(2,1)}, u32[]{:S(2)}, u32[]{:S(2)}) collective-permute-start(bf16[12,256,128]{2,1,0:T(8,128)(2,1)} %pad_maximum_fusion.5), channel_id=1, source_target_pairs={{0,7},{1,0},{2,1},{3,2},{4,3},{5,4},{6,5},{7,6},{8,15},{9,8},{10,9... | collective-permute-start | bytes 2359304 | tf_op jit(solution)/shard_map/ppermute | solution.py:22
  85.3 29.5 %collective-permute-start.14 = (bf16[4,1280,128]{2,1,0:T(8,128)(2,1)}, bf16[4,1280,128]{2,1,0:T(8,128)(2,1)}, u32[]{:S(2)}, u32[]{:S(2)}) collective-permute-start(bf16[4,1280,128]{2,1,0:T(8,128)(2,1)} %get-tuple-element.101.refs_0_), channel_id=1, source_target_pairs={{0,8},{8,16},{16,24},{24,0},{1,9},{9,17},{17,25},{25,1},{2,10},{10... | collective-permute-start | bytes 3932168 | tf_op jit(solution)/shard_map/ppermute | solution.py:22
  85.6 29.2 %collective-permute-start.15 = (bf16[4,1280,128]{2,1,0:T(8,128)(2,1)}, bf16[4,1280,128]{2,1,0:T(8,128)(2,1)}, u32[]{:S(2)}, u32[]{:S(2)}) collective-permute-start(bf16[4,1280,128]{2,1,0:T(8,128)(2,1)} %get-tuple-element.101.refs_0_), channel_id=1, source_target_pairs={{0,24},{8,0},{16,8},{24,16},{1,25},{9,1},{17,9},{25,17},{2,26},{10... | collective-permute-start | bytes 3932168 | tf_op jit(solution)/shard_map/ppermute | solution.py:22
  91.7 15.3 %collective-permute-start.16 = (bf16[1,1,8,256,128]{4,3,2,1,0:T(8,128)(2,1)}, bf16[1,1,8,256,128]{4,3,2,1,0:T(8,128)(2,1)}, u32[]{:S(2)}, u32[]{:S(2)}) collective-permute-start(bf16[1,1,8,256,128]{4,3,2,1,0:T(8,128)(2,1)} %dynamic-slice_convert_fusion), channel_id=1, source_target_pairs={{0,32},{32,0},{1,33},{33,1},{2,34},{34,2},{3,35},{35,3},{4,36},{36... | collective-permute-start | bytes 1572872 | tf_op jit(solution)/shard_map/ppermute | solution.py:22
  102.2 12.3 %collective-permute-start.12 = (bf16[8,256,128]{2,1,0:T(8,128)(2,1)}, bf16[8,256,128]{2,1,0:T(8,128)(2,1)}, u32[]{:S(2)}, u32[]{:S(2)}) collective-permute-start(bf16[8,256,128]{2,1,0:T(8,128)(2,1)} %fusion.2), channel_id=1, source_target_pairs={{0,7},{1,0},{2,1},{3,2},{4,3},{5,4},{6,5},{7,6},{8,15},{9,8},{10,9... | collective-permute-start | bytes 1572872 | tf_op jit(solution)/shard_map/ppermute | solution.py:22
  114.9 23.0 %collective-permute-start.17 = (bf16[4,768,128]{2,1,0:T(8,128)(2,1)S(1)}, bf16[4,768,128]{2,1,0:T(8,128)(2,1)}, u32[]{:S(2)}, u32[]{:S(2)}) collective-permute-start(bf16[4,768,128]{2,1,0:T(8,128)(2,1)S(1)} %pad_maximum_fusion.7.refs_1_), channel_id=1, source_target_pairs={{0,8},{8,16},{16,24},{24,0},{1,9},{9,17},{17,25},{25,1},{2,10},{10... | collective-permute-start | bytes 2359304 | tf_op jit(solution)/shard_map/ppermute | solution.py:22
  115.9 22.1 %collective-permute-start.18 = (bf16[4,768,128]{2,1,0:T(8,128)(2,1)S(1)}, bf16[4,768,128]{2,1,0:T(8,128)(2,1)S(1)}, u32[]{:S(2)}, u32[]{:S(2)}) collective-permute-start(bf16[4,768,128]{2,1,0:T(8,128)(2,1)S(1)} %pad_maximum_fusion.7.refs_1_), channel_id=1, source_target_pairs={{0,24},{8,0},{16,8},{24,16},{1,25},{9,1},{17,9},{25,17},{2,26},{10... | collective-permute-start | bytes 2359304 | tf_op jit(solution)/shard_map/ppermute | solution.py:22
  118.3 8.0 %collective-permute-start.19 = (f32[128,512]{1,0:T(8,128)S(1)}, f32[128,512]{1,0:T(8,128)S(1)}, u32[]{:S(2)}, u32[]{:S(2)}) collective-permute-start(f32[128,512]{1,0:T(8,128)S(1)} %add.177), channel_id=1, source_target_pairs={{0,128},{128,0},{1,129},{129,1},{2,130},{130,2},{3,131},{131,3},{4... | collective-permute-start | bytes 786440 | tf_op jit(solution)/shard_map/ppermute | solution.py:324
  122.0 15.9 %all-to-all-start = ((bf16[8,256,128]{2,1,0:T(8,128)(2,1)}), bf16[8,256,128]{2,1,0:T(8,128)(2,1)S(1)}, u32[]{:S(2)}, u32[]{:S(2)}) async-start(bf16[8,256,128]{2,1,0:T(8,128)(2,1)} %fusion.1), calls=%async_computation | async-start | bytes 1048576 | tf_op jit(solution)/shard_map/all_to_all | solution.py:40
  138.0 20.5 %all-to-all-start.1 = ((bf16[8,256,128]{2,1,0:T(8,128)(2,1)}), bf16[8,256,128]{2,1,0:T(8,128)(2,1)S(1)}, u32[]{:S(2)}, u32[]{:S(2)}) async-start(bf16[8,256,128]{2,1,0:T(8,128)(2,1)} %fusion.7), calls=%async_computation.1 | async-start | bytes 1048576 | tf_op jit(solution)/shard_map/all_to_all | solution.py:40
  141.5 29.5 %collective-permute-start.20 = (bf16[4,1280,128]{2,1,0:T(8,128)(2,1)}, bf16[4,1280,128]{2,1,0:T(8,128)(2,1)S(1)}, u32[]{:S(2)}, u32[]{:S(2)}) collective-permute-start(bf16[4,1280,128]{2,1,0:T(8,128)(2,1)} %collective-permute-done.14.refs_2_), channel_id=1, source_target_pairs={{0,8},{8,16},{16,24},{24,0},{1,9},{9,17},{17,25},{25,1},{2,10},{10... | collective-permute-start | bytes 3932168 | tf_op jit(solution)/shard_map/ppermute | solution.py:22
  144.1 26.9 %collective-permute-start.21 = (bf16[4,768,128]{2,1,0:T(8,128)(2,1)}, bf16[4,768,128]{2,1,0:T(8,128)(2,1)S(1)}, u32[]{:S(2)}, u32[]{:S(2)}) collective-permute-start(bf16[4,768,128]{2,1,0:T(8,128)(2,1)} %copy-done.10), channel_id=1, source_target_pairs={{0,24},{8,0},{16,8},{24,16},{1,25},{9,1},{17,9},{25,17},{2,26},{10... | collective-permute-start | bytes 2359304 | tf_op jit(solution)/shard_map/ppermute | solution.py:22
  160.8 24.9 %all-to-all-start.2 = ((f32[64,1,128]{2,1,0:T(1,128)}), f32[64,1,128]{2,1,0:T(1,128)S(1)}, u32[]{:S(2)}, u32[]{:S(2)}) async-start(f32[64,1,128]{2,1,0:T(1,128)} %broadcast_in_dim.8), calls=%async_computation.2 | async-start | bytes 65536 | tf_op jit(solution)/shard_map/all_to_all | solution.py:342
  (12 other events, 81.4 us)
